TPU v7x, 32 devices: a whole 2x2x4 slice. The times are simulated.
32 devices in a mesh: groups: 2 (over y), tenant: 4 (over z), tensor: 4 (over x, core).
Axes of the slice: x: 2, y: 2, z: 4, core: 2. Of those that a mesh axis runs over, the one named last changes fastest.
Arguments:
- hidden_states: bfloat16 [512, 14336], P(('groups', 'tenant'), 'tensor'), parts along dimension 0, may hold values from -6 to 6
- tenant_ids: int32 [512], P(('groups', 'tenant')), parts along dimension 0, may hold values from 0 to 15, as said below
- owner_map: int32 [32], P('groups'), parts along dimension 0, may hold values from 0 to 15, as said below
- down_weight: bfloat16 [14336, 8192], P('tensor', 'tenant'), may hold values from -0.046875 to 0.046875
- adapter_down: bfloat16 [32, 14336, 64], P(('groups', 'tenant'), 'tensor'), parts along dimension 0, may hold values from -0.046875 to 0.046875
- adapter_up: bfloat16 [32, 64, 8192], P(('groups', 'tensor'), None, 'tenant'), parts along dimension 0, may hold values from -0.75 to 0.75
Outputs:
- layer_out: bfloat16 [512, 8192], P(('groups', 'tensor'), 'tenant'), parts along dimension 0
There are 2 independent parts, one for each index of `groups`. A program takes and returns all parts, laid end to end along the dimension named above; an argument that names none is the same for every part. Nothing has to cross between parts.
Inputs may be any that keep to these rules, and one draw needn't show every extreme that they name: `tenant_ids`: in each aligned block of 64 rows, at most 32 rows have tenants whose slots lie in one range [o * 4, (o + 1) * 4); in every draw one such range gets exactly 32 rows from every block. `owner_map`: A permutation of the tenants.
All inputs are finite; a program needn't handle non-finite values.
Results may differ from a plain program's by a relative error of at most 0.004.
Values may be sent and summed in bfloat16 or wider, within the bound.
No kernel may reach another device: no remote copies, remote signals or barrier semaphores. Data moves between devices by JAX's collectives and lax.ppermute only.
A program may use at most 64 MiB of HBM per device.

v0:
```python
import jax
import jax.numpy as jnp
from jax import lax
from jax.sharding import PartitionSpec as P


def lookup(row_ids, mapping):
    matches = row_ids[:, None] == jnp.arange(mapping.shape[0], dtype=jnp.int32)[None, :]
    return jnp.sum(jnp.where(matches, mapping[None, :], 0), axis=1)


def on_device(hidden_states, tenant_ids, owner_map, down_weight, adapter_down, adapter_up):
    rows_dev = hidden_states.shape[0]
    ten_dev = adapter_down.shape[0]
    low_rank = adapter_down.shape[2]
    per_group = adapter_up.shape[0]
    cols_dev = adapter_up.shape[2]
    owners = lax.axis_size("tenant")
    capacity = min(4 * rows_dev // owners, rows_dev // 2)
    slot_limit = owners * capacity
    me_group = lax.axis_index("tensor")
    everyone, all_ids = (
        lax.all_gather(hidden_states, "tenant", axis=0, tiled=True),
        lax.all_gather(tenant_ids, "tenant", axis=0, tiled=True),
    )
    total_rows = everyone.shape[0]
    all_slots = lookup(all_ids, owner_map)
    my_slots = lookup(tenant_ids, owner_map)
    target = my_slots // ten_dev
    onehot = (target[:, None] == jnp.arange(owners, dtype=jnp.int32)[None, :]).astype(jnp.int32)
    position = jnp.sum(jnp.cumsum(onehot, axis=0) * onehot, axis=1) - 1
    slot_cell = target * capacity + position
    select = slot_cell[None, :] == jnp.arange(slot_limit, dtype=jnp.int32)[:, None]
    outgoing = jnp.dot(
        select.astype(jnp.bfloat16), hidden_states, preferred_element_type=jnp.float32
    )
    outgoing = outgoing.astype(jnp.bfloat16).reshape(owners, capacity, hidden_states.shape[1])
    local_tags = jnp.sum(jnp.where(select, (my_slots % ten_dev)[None, :], 0), axis=1)
    local_tags = jnp.where(jnp.any(select, axis=1), local_tags, -1).reshape(owners, capacity)
    payload = lax.all_to_all(outgoing, "tenant", split_axis=0, concat_axis=0, tiled=True)
    project_local_tags = lax.all_to_all(
        local_tags, "tenant", split_axis=0, concat_axis=0, tiled=True
    )
    flattened = payload.reshape(-1, payload.shape[2])
    mixed = jnp.einsum("nf,tfk->ntk", flattened, adapter_down, preferred_element_type=jnp.float32)
    chosen = (
        project_local_tags.reshape(-1)[:, None] == jnp.arange(ten_dev, dtype=jnp.int32)[None, :]
    )
    result = jnp.sum(jnp.where(chosen[:, :, None], mixed, 0.0), axis=1)
    partial_value = result.reshape(payload.shape[0], payload.shape[1], low_rank)
    summed = lax.psum(partial_value, "tensor")
    reduced = lax.all_to_all(
        summed.astype(jnp.bfloat16), "tenant", split_axis=0, concat_axis=0, tiled=True
    )
    my_low = jnp.dot(
        select.T.astype(jnp.bfloat16),
        reduced.reshape(-1, low_rank),
        preferred_element_type=jnp.float32,
    )
    all_low = lax.all_gather(my_low.astype(jnp.bfloat16), "tenant", axis=0, tiled=True)
    first_slot = me_group * per_group
    group_index = all_slots - first_slot
    chosen_group = group_index[:, None] == jnp.arange(per_group, dtype=jnp.int32)[None, :]
    spread = jnp.where(chosen_group[:, :, None], all_low[:, None, :], jnp.zeros((), jnp.bfloat16))
    spread = spread.reshape(total_rows, per_group * low_rank)
    up_flat = adapter_up.reshape(per_group * low_rank, cols_dev)
    layer_out = lax.psum_scatter(
        jnp.dot(everyone, down_weight, preferred_element_type=jnp.float32),
        "tensor",
        scatter_dimension=0,
        tiled=True,
    )
    layer_out = layer_out + lax.psum_scatter(
        jnp.dot(spread, up_flat, preferred_element_type=jnp.float32),
        "tensor",
        scatter_dimension=0,
        tiled=True,
    )
    return layer_out.astype(jnp.bfloat16)


def solution(mesh):
    return jax.shard_map(
        on_device,
        mesh=mesh,
        in_specs=(
            P(("groups", "tenant"), "tensor"),
            P(("groups", "tenant")),
            P("groups"),
            P("tensor", "tenant"),
            P(("groups", "tenant"), "tensor", None),
            P(("groups", "tensor"), None, "tenant"),
        ),
        out_specs=P(("groups", "tensor"), "tenant"),
        check_vma=False,
    )
```

profile of v0, /device:TPU:0, one launch (start us, length us, event | category | flops | bytes accessed | tf_op | source)
XLA Modules:
  0.0 154.7 jit_solution(10283896971639027633)
XLA Ops:
  6.5 0.0 copy-start
  6.5 0.0 copy-start.4
  6.5 0.0 copy-start.2
  6.5 0.0 copy-start.3
  6.5 0.0 all-gather.2.cloned.1.call-start
  6.6 0.7 all-gather.2.cloned.1.call-update
  7.3 0.8 select_reduce_fusion.4
  8.0 0.1 fusion.6
  8.1 0.1 reduce_window_sum.11
  8.2 0.2 select_reduce_fusion.2
  8.4 0.1 fusion.5
  8.5 0.1 select_reduce_fusion.1
  8.6 0.7 select_n.65
  9.3 6.3 %all-to-all-start = ((s32[4,1,32]{2,1,0:T(1,128)}), s32[4,1,32]{2,1,0:T(1,128)S(1)}, u32[]{:S(2)}, u32[]{:S(2)}) async-start(s32[4,1,32]{2,1,0:T(1,128)} %bitcast.1), calls=%async_computation | async-start | bytes 4096 | tf_op jit(solution)/shard_map/all_to_all | solution.py:41
  15.6 2.5 %convolution_convert_fusion = bf16[128,3584]{1,0:T(8,128)(2,1)} fusion(bf16[64,3584]{1,0:T(8,128)(2,1)} %param.6, s32[64]{0:T(128)S(1)} %add_add_fusion), kind=kOutput, calls=%fused_computation | convolution fusion | flops 59187200 | bytes 1376512 | tf_op jit(solution)/shard_map/dot_general | solution.py:34
  18.1 3.0 %all-to-all-done = s32[4,1,32]{2,1,0:T(1,128)S(1)} async-done(((s32[4,1,32]{2,1,0:T(1,128)}), s32[4,1,32]{2,1,0:T(1,128)S(1)}, u32[]{:S(2)}, u32[]{:S(2)}) %all-to-all-start) | async-done | bytes 544 | tf_op jit(solution)/shard_map/all_to_all | solution.py:41
  21.1 3.5 %all-to-all-start.1 = ((bf16[4,32,3584]{2,1,0:T(8,128)(2,1)}), bf16[4,32,3584]{2,1,0:T(8,128)(2,1)S(1)}, u32[]{:S(2)}, u32[]{:S(2)}) async-start(bf16[4,32,3584]{2,1,0:T(8,128)(2,1)} %bitcast.2), calls=%async_computation.1 | async-start | bytes 1835008 | tf_op jit(solution)/shard_map/all_to_all | solution.py:40
  24.6 0.0 copy-done.4
  24.6 0.6 dynamic-slice
  25.9 0.0 copy-done.3
  25.9 0.2 dynamic-update-slice
  26.1 44.2 %all-reduce = s32[256]{0:T(256)S(1)} all-reduce(s32[256]{0:T(256)S(1)} %dynamic-update-slice), channel_id=1, replica_groups=mesh['groups'=2,'tenant'=4,'tensor'=4] {'tenant'}, use_global_device_ids=true, to_apply=%add | all-reduce | flops 256 | bytes 2048
  70.3 0.0 copy-done.2
  70.3 0.1 select_reduce_fusion.3
  70.4 0.5 broadcast.160
  70.9 0.7 reduce.3
  71.6 0.1 eq.105
  71.7 0.0 all-to-all-done.1
  71.7 0.0 copy-done
  71.7 0.6 fusion.11
  72.3 0.1 copy.13
  72.4 10.9 %psum.7 = bf16[4,32,64]{2,1,0:T(8,128)(2,1)S(1)} all-reduce(f32[4,32,64]{2,1,0:T(8,128)S(1)} %bitcast.24), channel_id=1, replica_groups=mesh['groups'=2,'tenant'=4,'tensor'=4] {'tensor'}, use_global_device_ids=true, to_apply=%region_8.9 | all-reduce | flops 8192 | bytes 49152 | tf_op jit(solution)/shard_map/psum | solution.py:51
  83.4 0.7 reshape.163
  84.1 3.3 %all-to-all-start.2 = ((bf16[4,2,1024]{2,1,0:T(2,128)(2,1)}), bf16[4,2,1024]{2,1,0:T(2,128)(2,1)S(1)}, u32[]{:S(2)}, u32[]{:S(2)}) async-start(bf16[4,2,1024]{2,1,0:T(2,128)(2,1)} %reshape.163), calls=%async_computation.2 | async-start | bytes 32768 | tf_op jit(solution)/shard_map/all_to_all | solution.py:52
  87.4 0.0 reduce-scatter.2.cloned.1.call-start
  87.4 5.5 %all-to-all-done.2 = bf16[4,2,1024]{2,1,0:T(2,128)(2,1)S(1)} async-done(((bf16[4,2,1024]{2,1,0:T(2,128)(2,1)}), bf16[4,2,1024]{2,1,0:T(2,128)(2,1)S(1)}, u32[]{:S(2)}, u32[]{:S(2)}) %all-to-all-start.2) | async-done | bytes 16416 | tf_op jit(solution)/shard_map/all_to_all | solution.py:52
  92.9 0.1 reshape.164
  93.0 0.2 convolution_convert_fusion.1
  93.2 13.1 %all_gather.11 = bf16[256,64]{1,0:T(8,128)(2,1)S(1)} all-gather(bf16[64,64]{1,0:T(8,128)(2,1)S(1)} %convolution_convert_fusion.1), channel_id=1, replica_groups=mesh['groups'=2,'tenant'=4,'tensor'=4] {'tenant'}, dimensions={0}, use_global_device_ids=true | all-gather | bytes 40960 | tf_op jit(solution)/shard_map/all_gather | solution.py:60
  106.3 0.1 copy.14
  106.4 0.0 copy-start.1
  106.5 0.0 all-gather.2.cloned.1.call-done
  106.5 7.9 %fusion.10 = f32[256,2048]{1,0:T(8,128)S(1)} fusion(bf16[256,3584]{1,0:T(8,128)(2,1)} %all-gather.2.cloned.1.call-done, bf16[3584,2048]{1,0:T(8,128)(2,1)} %param.9), kind=kOutput, calls=%fused_computation.32 | convolution fusion | flops 3758096384 | bytes 18612224 | tf_op jit(solution)/shard_map/dot_general | solution.py:68
  114.4 0.0 copy-done.1
  114.4 1.8 %fusion = f32[256,2048]{1,0:T(8,128)} fusion(f32[256,2048]{1,0:T(8,128)S(1)} %fusion.10, bf16[4,64,2048]{2,1,0:T(8,128)(2,1)S(1)} %copy-done.1, pred[256,4]{0,1:T(4,128)(4,1)S(1)} %iota_compare_fusion.6, bf16[256,64]{0,1:T(8,128)(2,1)S(1)} %copy.14), kind=kOutput, calls=%fused_computation.2 | convolution fusion | flops 269025280 | bytes 5276672 | tf_op jit(solution)/shard_map/dot_general | solution.py:74
  116.2 0.0 reduce-scatter.2.cloned.1.call-update
  116.2 29.8 %reduce-scatter.2.cloned.1.call-done = f32[64,2048]{1,0:T(8,128)} async-done(((f32[256,2048]{1,0:T(8,128)}), f32[64,2048]{1,0:T(8,128)}) %reduce-scatter.2.cloned.1.call-update) | async-done | bytes 524304 | tf_op jit(solution)/shard_map/reduce_scatter | solution.py:67
  146.0 1.8 %convert_element_type.21 = bf16[64,2048]{1,0:T(8,128)(2,1)} convert(f32[64,2048]{1,0:T(8,128)} %reduce-scatter.2.cloned.1.call-done) | non-fusion elementwise | flops 131072 | bytes 786432 | tf_op jit(solution)/shard_map/convert_element_type | solution.py:79
  (8 shorter events, 0.1 us)
Async XLA Ops:
  6.5 65.2 %copy-start = (bf16[4,3584,64]{1,2,0:T(8,128)(2,1)S(1)}, bf16[4,3584,64]{1,2,0:T(8,128)(2,1)}, u32[]{:S(2)}) copy-start(bf16[4,3584,64]{1,2,0:T(8,128)(2,1)} %param.10) | copy-start | bytes 5505028
  6.5 18.1 %copy-start.4 = (u32[32]{0:T(128)S(1)}, u32[32]{0:T(128)}, u32[]{:S(2)}) copy-start(u32[32]{0:T(128)} %constant.52) | copy-start | bytes 388
  6.5 63.8 %copy-start.2 = (s32[16]{0:T(128)S(1)}, s32[16]{0:T(128)}, u32[]{:S(2)}) copy-start(s32[16]{0:T(128)} %param.8) | copy-start | bytes 196
  6.5 19.3 %copy-start.3 = (s32[64]{0:T(128)S(1)}, s32[64]{0:T(128)}, u32[]{:S(2)}) copy-start(s32[64]{0:T(128)} %param.7) | copy-start | bytes 772
  6.5 99.9 %all-gather.2.cloned.1.call-start = ((), (), s32[]{:S(2)}) async-start(), calls=%async_computation.4 | async-start | bytes 2293760 | tf_op jit(solution)/shard_map/all_gather | solution.py:23
  9.3 11.8 %all-to-all-start = ((s32[4,1,32]{2,1,0:T(1,128)}), s32[4,1,32]{2,1,0:T(1,128)S(1)}, u32[]{:S(2)}, u32[]{:S(2)}) async-start(s32[4,1,32]{2,1,0:T(1,128)} %bitcast.1), calls=%async_computation | async-start | bytes 4096 | tf_op jit(solution)/shard_map/all_to_all | solution.py:41
  21.1 50.6 %all-to-all-start.1 = ((bf16[4,32,3584]{2,1,0:T(8,128)(2,1)}), bf16[4,32,3584]{2,1,0:T(8,128)(2,1)S(1)}, u32[]{:S(2)}, u32[]{:S(2)}) async-start(bf16[4,32,3584]{2,1,0:T(8,128)(2,1)} %bitcast.2), calls=%async_computation.1 | async-start | bytes 1835008 | tf_op jit(solution)/shard_map/all_to_all | solution.py:40
  84.1 8.8 %all-to-all-start.2 = ((bf16[4,2,1024]{2,1,0:T(2,128)(2,1)}), bf16[4,2,1024]{2,1,0:T(2,128)(2,1)S(1)}, u32[]{:S(2)}, u32[]{:S(2)}) async-start(bf16[4,2,1024]{2,1,0:T(2,128)(2,1)} %reshape.163), calls=%async_computation.2 | async-start | bytes 32768 | tf_op jit(solution)/shard_map/all_to_all | solution.py:52
  87.4 58.7 %reduce-scatter.2.cloned.1.call-start = ((), (), s32[]{:S(2)}) async-start(), calls=%async_computation.5 | async-start | bytes 2621440 | tf_op jit(solution)/shard_map/reduce_scatter | solution.py:67
  106.4 7.9 %copy-start.1 = (bf16[4,64,2048]{2,1,0:T(8,128)(2,1)S(1)}, bf16[4,64,2048]{2,1,0:T(8,128)(2,1)}, u32[]{:S(2)}) copy-start(bf16[4,64,2048]{2,1,0:T(8,128)(2,1)} %param.11) | copy-start | bytes 3145732
Sparse Core Ops, SparseCore 0:
  8.9 63.8 all-gather.1
  116.3 29.6 reduce-scatter.1
where the time goes:
time: 155 us
  blocking collectives  68.3 us (44%)
  waiting for transfers between devices  39.1 us (25%)
  between operations  14.2 us (9%)
  starting transfers between devices  13.2 us (9%)
  matrix products  13 us (8%)
  other arithmetic  3.89 us (3%)
  local copies, waits for them, and re-layouts  3.09 us (2%)
    unnamed x1, blocking collectives  44.2 us
    reduce_scatter x1, waiting for transfers between devices, on_device(): lax.psum_scatter(jnp.dot(everyone, down_weight, preferred_element_type=jn...  29.8 us
    all_gather x1, blocking collectives, on_device(): lax.all_gather(my_low.astype(jnp.bfloat16), 'tenant', axis=0, tiled=True)  13.1 us
    psum x1, blocking collectives, on_device(): summed = lax.psum(partial_value, 'tensor')  10.9 us
    dot_general x1, matrix products, on_device(): jnp.dot(everyone, down_weight, preferred_element_type=jnp.float32)  7.86 us
    all_to_all x1, starting transfers between devices, on_device(): lax.all_to_all(local_tags, 'tenant', split_axis=0, concat_axis=0, tiled=T...  6.32 us
    all_to_all x1, waiting for transfers between devices, on_device(): lax.all_to_all(summed.astype(jnp.bfloat16), 'tenant', split_axis=0, conca...  5.52 us
    all_to_all x1, starting transfers between devices, on_device(): lax.all_to_all(outgoing, 'tenant', split_axis=0, concat_axis=0, tiled=True)  3.5 us
  transfers between devices with their start and end apart: 5, of which 3 were waited for; matrix products, arithmetic and copies ran while one was open for 5% of the time, Pallas kernels for 0%

commit v1 on v0

--- a/solution.py
+++ b/solution.py
@@ -9,7 +9,7 @@
     return jnp.sum(jnp.where(matches, mapping[None, :], 0), axis=1)
 
 
-def on_device(hidden_states, tenant_ids, owner_map, down_weight, adapter_down, adapter_up):
+def on_device_general(hidden_states, tenant_ids, owner_map, down_weight, adapter_down, adapter_up):
     rows_dev = hidden_states.shape[0]
     ten_dev = adapter_down.shape[0]
     low_rank = adapter_down.shape[2]
@@ -79,9 +79,92 @@
     return layer_out.astype(jnp.bfloat16)
 
 
+def ordered(first, then):
+    return lax.optimization_barrier((first, then))
+
+
+def on_device_4x4(hidden_states, tenant_ids, owner_map, down_weight, adapter_down, adapter_up):
+    rows_dev = hidden_states.shape[0]
+    ten_dev, _, low_rank = adapter_down.shape
+    wide = ten_dev * low_rank
+    t = lax.axis_index("tenant")
+    q = lax.axis_index("tensor")
+    bf16, f32 = jnp.bfloat16, jnp.float32
+
+    def along(name, pairs):
+        return lambda value: lax.ppermute(value, name, pairs)
+
+    outer_pairs = along("tenant", [(0, 1), (1, 0), (2, 3), (3, 2)])
+    two_apart = along("tenant", [(0, 2), (2, 0), (1, 3), (3, 1)])
+    inner_pair = along("tenant", [(1, 2), (2, 1)])
+    to_ends = along("tenant", [(2, 3), (1, 0)])
+    opposite = along("tenant", [(0, 3), (3, 0), (1, 2), (2, 1)])
+    cores = along("tensor", [(0, 1), (1, 0), (2, 3), (3, 2)])
+    chips = along("tensor", [(0, 2), (2, 0), (1, 3), (3, 1)])
+
+    from_two = two_apart(hidden_states)
+    from_pair = outer_pairs(hidden_states)
+    up_chip = chips(adapter_up)
+    home_ids = lax.ppermute(
+        tenant_ids,
+        ("tenant", "tensor"),
+        [(a * 4 + b, b * 4 + a) for a in range(4) for b in range(4)],
+    )
+    from_two, hidden_late = ordered(from_two, hidden_states)
+    from_end = to_ends(from_two)
+    from_inner = inner_pair(hidden_late)
+    inside = (t == 1) | (t == 2)
+    from_last = jnp.where(inside, from_inner, from_end)
+
+    down_flat = jnp.transpose(adapter_down, (1, 0, 2)).reshape(-1, wide)
+
+    def dot(a, b):
+        return jnp.dot(a, b, preferred_element_type=f32)
+
+    blocks = (hidden_states, from_pair, from_two, from_last)
+    low = [dot(rows, down_flat) for rows in blocks]
+    base = [dot(rows, down_weight) for rows in blocks]
+
+    core = q % 2
+    even = (t % 2) == core
+    near = (t // 2) == (q // 2)
+
+    def to_home(parts, sent):
+        keep = [jnp.where(even, parts[i], parts[i + 1]) for i in (0, 2)]
+        give = [jnp.where(even, parts[i + 1], parts[i]).astype(sent) for i in (0, 2)]
+        got = [cores(value) for value in give]
+        both = [a + b.astype(f32) for a, b in zip(keep, got)]
+        mine = jnp.where(near, both[0], both[1])
+        other = jnp.where(near, both[1], both[0]).astype(sent)
+        return mine + chips(other).astype(f32)
+
+    reduced = to_home(low, f32).astype(bf16)
+    by_owner = (reduced, outer_pairs(reduced), two_apart(reduced), opposite(reduced))
+
+    up_core = cores(adapter_up)
+    up_both = cores(up_chip)
+    ups = ((q, adapter_up), (q ^ 2, up_chip), (q ^ 1, up_core), (q ^ 3, up_both))
+
+    slots = lookup(home_ids, owner_map)
+    lane = jnp.arange(wide, dtype=jnp.int32)[None, :] // low_rank
+    zero = jnp.zeros((), bf16)
+    chosen = zero
+    for step, value in enumerate(by_owner):
+        first = (t ^ step) * ten_dev
+        chosen = chosen + jnp.where(slots[:, None] - first == lane, value, zero)
+    row = sum(chosen[:, i * low_rank : (i + 1) * low_rank] for i in range(ten_dev))
+    tiled = jnp.concatenate([row] * ten_dev, axis=1)
+    delta = 0.0
+    for index, up in ups:
+        spread = jnp.where(slots[:, None] - index * ten_dev == lane, tiled, zero)
+        delta = delta + dot(spread, up.reshape(wide, -1))
+    return (to_home(base, bf16) + delta).astype(bf16)
+
+
 def solution(mesh):
+    small = mesh.shape["tenant"] == 4 and mesh.shape["tensor"] == 4
     return jax.shard_map(
-        on_device,
+        on_device_4x4 if small else on_device_general,
         mesh=mesh,
         in_specs=(
             P(("groups", "tenant"), "tensor"),

time: 155 us -> 76.5 us (0.49)
  blocking collectives: 68.3 us -> 0 us
  matrix products: 13 us -> 29.9 us
  between operations: 14.2 us -> 0.41 us
  waiting for transfers between devices: 39.1 us -> 29.1 us
  other arithmetic: 3.89 us -> 0.53 us
  local copies, waits for them, and re-layouts: 3.09 us -> 0.04 us
  starting transfers between devices: 13.2 us -> 16.2 us
    unnamed x1 -> x0, blocking collectives: 44.2 us -> none
    reduce_scatter x1 -> x0, waiting for transfers between devices: 29.8 us -> none  [on_device(): lax.psum_scatter(jnp.dot(everyone, down_weight, preferred_element_type=jn...]
    ppermute x0 -> x17, waiting for transfers between devices: none -> 29.1 us  [the longest x16 29.1 us: along(): return lambda value: lax.ppermute(value, name, pairs)]
    dot_general x4 -> x12, matrix products: 12.3 us -> 29.9 us  [dot(): return jnp.dot(a, b, preferred_element_type=f32)]
    ppermute x0 -> x17, starting transfers between devices: none -> 16.2 us  [the longest x16 14.9 us: along(): return lambda value: lax.ppermute(value, name, pairs)]
    all_gather x1 -> x0, blocking collectives: 13.1 us -> none  [on_device(): lax.all_gather(my_low.astype(jnp.bfloat16), 'tenant', axis=0, tiled=True)]
    all_to_all x3 -> x0, starting transfers between devices: 13.1 us -> none  [the longest x1 6.32 us: on_device(): lax.all_to_all(local_tags, 'tenant', split_axis=0, concat_axis=0, tiled=T...]
    psum x1 -> x0, blocking collectives: 10.9 us -> none  [on_device(): summed = lax.psum(partial_value, 'tensor')]
  transfers between devices with their start and end apart: 5 -> 17, of which waited for: 3 -> 5; matrix products, arithmetic and copies ran while one was open for 5% -> 38% of each run, Pallas kernels for 0% -> 0%
where the time goes in v1:
time: 76.5 us; the launch traced here: 76.2 us
  matrix products  29.9 us (39%)
  waiting for transfers between devices  29.1 us (38%)
  starting transfers between devices  16.2 us (21%)
    dot_general x12, matrix products, dot(): return jnp.dot(a, b, preferred_element_type=f32)  29.9 us
    ppermute x16, waiting for transfers between devices, along(): return lambda value: lax.ppermute(value, name, pairs)  29.1 us
    ppermute x16, starting transfers between devices, along(): return lambda value: lax.ppermute(value, name, pairs)  14.9 us
  transfers between devices with their start and end apart: 17, of which 5 were waited for; matrix products, arithmetic and copies ran while one was open for 38% of the time, Pallas kernels for 0%

profile of v1, /device:TPU:0, one launch (start us, length us, event | category | flops | bytes accessed | tf_op | source)
XLA Modules:
  0.0 76.2 jit_solution(17745077998212793523)
XLA Ops:
  0.0 0.0 copy-start
  0.0 3.1 %collective-permute-start = (bf16[64,3584]{1,0:T(8,128)(2,1)}, bf16[64,3584]{1,0:T(8,128)(2,1)}, u32[]{:S(2)}, u32[]{:S(2)}) collective-permute-start(bf16[64,3584]{1,0:T(8,128)(2,1)} %param.6), channel_id=1, source_target_pairs={{0,4},{4,0},{8,12},{12,8},{1,5},{5,1},{9,13},{13,9},{2,6},{6,2},{1... | collective-permute-start | bytes 1376264 | tf_op jit(solution)/shard_map/ppermute | solution.py:95
  3.1 2.6 %collective-permute-start.2 = (bf16[64,3584]{1,0:T(8,128)(2,1)}, bf16[64,3584]{1,0:T(8,128)(2,1)S(1)}, u32[]{:S(2)}, u32[]{:S(2)}) collective-permute-start(bf16[64,3584]{1,0:T(8,128)(2,1)} %param.6), channel_id=1, source_target_pairs={{0,8},{8,0},{4,12},{12,4},{1,9},{9,1},{5,13},{13,5},{2,10},{10,2},... | collective-permute-start | bytes 1376264 | tf_op jit(solution)/shard_map/ppermute | solution.py:95
  5.7 1.5 %collective-permute-start.14 = (bf16[4,64,2048]{2,1,0:T(8,128)(2,1)}, bf16[4,64,2048]{2,1,0:T(8,128)(2,1)}, u32[]{:S(2)}, u32[]{:S(2)}) collective-permute-start(bf16[4,64,2048]{2,1,0:T(8,128)(2,1)} %param.11), channel_id=1, source_target_pairs={{0,2},{2,0},{1,3},{3,1},{4,6},{6,4},{5,7},{7,5},{8,10},{10,8},{9,1... | collective-permute-start | bytes 3145736 | tf_op jit(solution)/shard_map/ppermute | solution.py:95
  7.2 0.0 collective-permute-start.15
  7.2 1.3 %collective-permute-start.7 = (s32[64]{0:T(128)}, s32[64]{0:T(128)S(1)}, u32[]{:S(2)}, u32[]{:S(2)}) collective-permute-start(s32[64]{0:T(128)} %param.7), channel_id=1, source_target_pairs={{0,0},{1,4},{2,8},{3,12},{4,1},{5,5},{6,9},{7,13},{8,2},{9,6},{10,... | collective-permute-start | bytes 776 | tf_op jit(solution)/shard_map/ppermute | solution.py:108
  8.5 8.0 %fusion.24 = f32[64,2048]{1,0:T(8,128)S(1)} fusion(bf16[64,3584]{1,0:T(8,128)(2,1)} %param.6, bf16[3584,2048]{1,0:T(8,128)(2,1)} %param.9), kind=kOutput, calls=%fused_computation.65 | convolution fusion | flops 939524096 | bytes 15663104 | tf_op jit(solution)/shard_map/dot_general | solution.py:122
  16.5 0.0 copy-done
  16.5 0.0 copy-done.1
  16.5 0.7 fusion.26
  17.3 0.0 collective-permute-done.7
  17.3 0.0 copy-done.3
  17.3 0.1 select_reduce_fusion
  17.4 8.7 %collective-permute-done.2 = bf16[64,3584]{1,0:T(8,128)(2,1)S(1)} collective-permute-done((bf16[64,3584]{1,0:T(8,128)(2,1)}, bf16[64,3584]{1,0:T(8,128)(2,1)S(1)}, u32[]{:S(2)}, u32[]{:S(2)}) %collective-permute-start.2) | collective-permute-done | bytes 458784 | tf_op jit(solution)/shard_map/ppermute | solution.py:95
  26.1 0.7 collective-permute-start.3
  26.8 1.3 %collective-permute-start.4 = (bf16[64,3584]{1,0:T(8,128)(2,1)S(1)}, bf16[64,3584]{1,0:T(8,128)(2,1)S(1)}, u32[]{:S(2)}, u32[]{:S(2)}) collective-permute-start(bf16[64,3584]{1,0:T(8,128)(2,1)S(1)} %collective-permute-done.2), channel_id=1, source_target_pairs={{8,12},{4,0},{9,13},{5,1},{10,14},{6,2},{11,15},{7,3},{24,28},{20,... | collective-permute-start | bytes 1376264 | tf_op jit(solution)/shard_map/ppermute | solution.py:95
  28.1 0.0 collective-permute-done
  28.1 1.7 %broadcast_select_fusion.4 = (f32[64,256]{1,0:T(8,128)S(1)}, f32[64,256]{1,0:T(8,128)S(1)}) fusion(f32[64,256]{1,0:T(8,128)S(1)} %fusion.26, pred[]{:T(512)S(6)} %eq.66, bf16[64,3584]{1,0:T(8,128)(2,1)} %collective-permute-done, bf16[3584,256]{0,1:T(8,128)(2,1)S(1)} %bitcast.26), kind=kOutput, calls=%fused_computation.38 | convolution fusion | flops 117456896 | bytes 2490369 | tf_op jit(solution)/shard_map/dot_general | solution.py:122
  29.8 0.0 slice-start
  29.8 0.1 collective-permute-start.8
  29.9 0.7 fusion.27
  30.6 0.0 collective-permute-done.3
  30.6 11.9 %collective-permute-done.4 = bf16[64,3584]{1,0:T(8,128)(2,1)S(1)} collective-permute-done((bf16[64,3584]{1,0:T(8,128)(2,1)S(1)}, bf16[64,3584]{1,0:T(8,128)(2,1)S(1)}, u32[]{:S(2)}, u32[]{:S(2)}) %collective-permute-start.4) | collective-permute-done | bytes 458784 | tf_op jit(solution)/shard_map/ppermute | solution.py:95
  42.4 0.7 broadcast_select_fusion.3
  43.1 0.0 slice-start.1
  43.1 0.0 slice-start.2
  43.1 0.0 slice-start.3
  43.2 0.2 collective-permute-start.9
  43.3 8.1 %select_convert_fusion.2 = (bf16[64,2048]{1,0:T(8,128)(2,1)S(1)}, f32[64,2048]{1,0:T(8,128)S(1)}) fusion(f32[64,2048]{1,0:T(8,128)S(1)} %fusion.24, pred[]{:T(512)S(6)} %eq.66, bf16[64,3584]{1,0:T(8,128)(2,1)} %collective-permute-done, bf16[3584,2048]{1,0:T(8,128)(2,1)} %param.9), kind=kOutput, calls=%fused_computation.9 | convolution fusion | flops 939655168 | bytes 16449537 | tf_op jit(solution)/shard_map/dot_general | solution.py:122
  51.5 0.0 collective-permute-done.8
  51.5 0.0 collective-permute-done.9
  51.5 0.1 collective-permute-start.10
  51.6 0.0 slice-done
  51.6 0.0 slice-done.1
  51.6 0.0 slice-done.2
  51.6 0.0 slice-done.3
  51.6 2.7 %fusion.25 = f32[64,2048]{1,0:T(8,128)S(1)} fusion(bf16[64,3584]{1,0:T(8,128)(2,1)S(1)} %collective-permute-done.2, bf16[3584,2048]{1,0:T(8,128)(2,1)S(1)} %bitcast.30), kind=kOutput, calls=%fused_computation.66 | convolution fusion | flops 939524096 | bytes 15663104 | tf_op jit(solution)/shard_map/dot_general | solution.py:122
  54.4 0.0 copy-start.2
  54.4 1.7 %collective-permute-done.10 = f32[64,256]{1,0:T(8,128)S(1)} collective-permute-done((f32[64,256]{1,0:T(8,128)S(1)}, f32[64,256]{1,0:T(8,128)S(1)}, u32[]{:S(2)}, u32[]{:S(2)}) %collective-permute-start.10) | collective-permute-done | bytes 65568 | tf_op jit(solution)/shard_map/ppermute | solution.py:95
  56.1 0.1 collective-permute-start.11
  56.2 2.2 %collective-permute-start.12 = (bf16[64,256]{1,0:T(8,128)(2,1)S(1)}, bf16[64,256]{1,0:T(8,128)(2,1)S(1)}, u32[]{:S(2)}, u32[]{:S(2)}) collective-permute-start(bf16[64,256]{1,0:T(8,128)(2,1)S(1)} %add_convert_fusion), channel_id=1, source_target_pairs={{0,8},{8,0},{4,12},{12,4},{1,9},{9,1},{5,13},{13,5},{2,10},{10,2},... | collective-permute-start | bytes 98312 | tf_op jit(solution)/shard_map/ppermute | solution.py:95
  58.4 2.1 %collective-permute-start.13 = (bf16[64,256]{1,0:T(8,128)(2,1)S(1)}, bf16[64,256]{1,0:T(8,128)(2,1)S(1)}, u32[]{:S(2)}, u32[]{:S(2)}) collective-permute-start(bf16[64,256]{1,0:T(8,128)(2,1)S(1)} %add_convert_fusion), channel_id=1, source_target_pairs={{0,12},{12,0},{4,8},{8,4},{1,13},{13,1},{5,9},{9,5},{2,14},{14,2},... | collective-permute-start | bytes 98312 | tf_op jit(solution)/shard_map/ppermute | solution.py:95
  60.5 2.7 %select_convert_fusion.1 = (bf16[64,2048]{1,0:T(8,128)(2,1)S(1)}, f32[64,2048]{1,0:T(8,128)S(1)}) fusion(f32[64,2048]{1,0:T(8,128)S(1)} %fusion.25, pred[]{:T(512)S(6)} %eq.66, bf16[3584,2048]{1,0:T(8,128)(2,1)S(1)} %bitcast.30, bf16[64,3584]{1,0:T(8,128)(2,1)S(1)} %collective-permute-done.3, bf16[64,3584]{1,0:T(8,128)(2,1)S(1)} %collective-permute-done.4, ...), kind=kOutput, calls=%fused_computation.7 | convolution fusion | flops 939884544 | bytes 16908290 | tf_op jit(solution)/shard_map/dot_general | solution.py:122
  63.2 0.0 collective-permute-done.14
  63.2 0.1 collective-permute-start.1
  63.3 0.0 collective-permute-done.11
  63.3 0.5 collective-permute-start.5
  63.8 0.0 collective-permute-done.12
  63.8 0.1 collective-permute-start.16
  63.9 0.2 collective-permute-done.13
  64.1 0.1 fusion.7
  64.2 0.1 slice_add_fusion
  64.3 0.0 copy-done.2
  64.3 0.3 fusion.4
  64.7 1.6 %convolution_add_fusion.2 = f32[64,2048]{1,0:T(8,128)S(1)} fusion(f32[64,2048]{1,0:T(8,128)S(1)} %fusion.4, bf16[256,2048]{1,0:T(8,128)(2,1)} %bitcast.4, s32[256]{0:T(256)S(1)} %and_select_fusion, s32[64]{0:T(128)S(1)} %get-tuple-element.14, bf16[64,64]{1,0:T(8,128)(2,1)S(1)} %slice_add_fusion), kind=kOutput, calls=%fused_computation.2 | convolution fusion | flops 67403776 | bytes 2106624 | tf_op jit(solution)/shard_map/dot_general | solution.py:122
  66.2 0.0 collective-permute-done.1
  66.2 0.0 collective-permute-done.5
  66.3 0.2 select_convert_fusion
  66.5 0.4 collective-permute-start.6
  66.8 0.0 collective-permute-done.15
  66.8 1.6 %convolution_add_fusion.1 = f32[64,2048]{1,0:T(8,128)S(1)} fusion(f32[64,2048]{1,0:T(8,128)S(1)} %convolution_add_fusion.2, bf16[256,2048]{1,0:T(8,128)(2,1)} %bitcast.5, s32[256]{0:T(256)S(1)} %and_select_fusion, s32[64]{0:T(128)S(1)} %get-tuple-element.13, bf16[64,64]{1,0:T(8,128)(2,1)S(1)} %slice_add_fusion), kind=kOutput, calls=%fused_computation.1 | convolution fusion | flops 67403776 | bytes 2106624 | tf_op jit(solution)/shard_map/dot_general | solution.py:122
  68.4 6.6 %collective-permute-done.6 = bf16[64,2048]{1,0:T(8,128)(2,1)S(1)} collective-permute-done((bf16[64,2048]{1,0:T(8,128)(2,1)S(1)}, bf16[64,2048]{1,0:T(8,128)(2,1)S(1)}, u32[]{:S(2)}, u32[]{:S(2)}) %collective-permute-start.6) | collective-permute-done | bytes 262176 | tf_op jit(solution)/shard_map/ppermute | solution.py:95
  75.0 0.0 collective-permute-done.16
  75.0 1.2 %fusion.1 = bf16[64,2048]{1,0:T(8,128)(2,1)} fusion(f32[64,2048]{1,0:T(8,128)S(1)} %convolution_add_fusion.1, bf16[256,2048]{1,0:T(8,128)(2,1)S(1)} %bitcast.32, bf16[64,2048]{1,0:T(8,128)(2,1)S(1)} %collective-permute-done.6, pred[]{:T(512)S(6)} %eq.65, bf16[64,2048]{1,0:T(8,128)(2,1)S(1)} %collective-permute-done.1, f32[64,2048]{1,0:T(8,128)S(1)} %fusion.24, ...), kind=kOutput, calls=%fused_computation.4 | convolution fusion | flops 68845568 | bytes 4728066 | tf_op jit(solution)/shard_map/dot_general | solution.py:122
  (7 shorter events, 0.1 us)
Async XLA Ops:
  0.0 16.5 %copy-start = (bf16[4,3584,64]{1,2,0:T(8,128)(2,1)S(1)}, bf16[4,3584,64]{1,2,0:T(8,128)(2,1)}, u32[]{:S(2)}) copy-start(bf16[4,3584,64]{1,2,0:T(8,128)(2,1)} %param.10) | copy-start | bytes 5505028
  0.0 16.5 %copy-start.1 = (bf16[64,3584]{1,0:T(8,128)(2,1)S(1)}, bf16[64,3584]{1,0:T(8,128)(2,1)}, u32[]{:S(2)}) copy-start(bf16[64,3584]{1,0:T(8,128)(2,1)} %param.6) | copy-start | bytes 1376260
  0.0 17.3 %copy-start.3 = (s32[16]{0:T(128)S(1)}, s32[16]{0:T(128)}, u32[]{:S(2)}) copy-start(s32[16]{0:T(128)} %param.8) | copy-start | bytes 196
  0.0 28.1 %collective-permute-start = (bf16[64,3584]{1,0:T(8,128)(2,1)}, bf16[64,3584]{1,0:T(8,128)(2,1)}, u32[]{:S(2)}, u32[]{:S(2)}) collective-permute-start(bf16[64,3584]{1,0:T(8,128)(2,1)} %param.6), channel_id=1, source_target_pairs={{0,4},{4,0},{8,12},{12,8},{1,5},{5,1},{9,13},{13,9},{2,6},{6,2},{1... | collective-permute-start | bytes 1376264 | tf_op jit(solution)/shard_map/ppermute | solution.py:95
  3.1 23.0 %collective-permute-start.2 = (bf16[64,3584]{1,0:T(8,128)(2,1)}, bf16[64,3584]{1,0:T(8,128)(2,1)S(1)}, u32[]{:S(2)}, u32[]{:S(2)}) collective-permute-start(bf16[64,3584]{1,0:T(8,128)(2,1)} %param.6), channel_id=1, source_target_pairs={{0,8},{8,0},{4,12},{12,4},{1,9},{9,1},{5,13},{13,5},{2,10},{10,2},... | collective-permute-start | bytes 1376264 | tf_op jit(solution)/shard_map/ppermute | solution.py:95
  5.7 57.5 %collective-permute-start.14 = (bf16[4,64,2048]{2,1,0:T(8,128)(2,1)}, bf16[4,64,2048]{2,1,0:T(8,128)(2,1)}, u32[]{:S(2)}, u32[]{:S(2)}) collective-permute-start(bf16[4,64,2048]{2,1,0:T(8,128)(2,1)} %param.11), channel_id=1, source_target_pairs={{0,2},{2,0},{1,3},{3,1},{4,6},{6,4},{5,7},{7,5},{8,10},{10,8},{9,1... | collective-permute-start | bytes 3145736 | tf_op jit(solution)/shard_map/ppermute | solution.py:95
  7.2 59.6 %collective-permute-start.15 = (bf16[4,64,2048]{2,1,0:T(8,128)(2,1)}, bf16[4,64,2048]{2,1,0:T(8,128)(2,1)}, u32[]{:S(2)}, u32[]{:S(2)}) collective-permute-start(bf16[4,64,2048]{2,1,0:T(8,128)(2,1)} %param.11), channel_id=1, source_target_pairs={{0,1},{1,0},{2,3},{3,2},{4,5},{5,4},{6,7},{7,6},{8,9},{9,8},{10,11... | collective-permute-start | bytes 3145736 | tf_op jit(solution)/shard_map/ppermute | solution.py:95
  7.2 10.1 %collective-permute-start.7 = (s32[64]{0:T(128)}, s32[64]{0:T(128)S(1)}, u32[]{:S(2)}, u32[]{:S(2)}) collective-permute-start(s32[64]{0:T(128)} %param.7), channel_id=1, source_target_pairs={{0,0},{1,4},{2,8},{3,12},{4,1},{5,5},{6,9},{7,13},{8,2},{9,6},{10,... | collective-permute-start | bytes 776 | tf_op jit(solution)/shard_map/ppermute | solution.py:108
  26.1 4.5 %collective-permute-start.3 = (bf16[64,3584]{1,0:T(8,128)(2,1)S(1)}, bf16[64,3584]{1,0:T(8,128)(2,1)S(1)}, u32[]{:S(2)}, u32[]{:S(2)}) collective-permute-start(bf16[64,3584]{1,0:T(8,128)(2,1)S(1)} %copy-done.1), channel_id=1, source_target_pairs={{4,8},{8,4},{5,9},{9,5},{6,10},{10,6},{7,11},{11,7},{20,24},{24,20... | collective-permute-start | bytes 1376264 | tf_op jit(solution)/shard_map/ppermute | solution.py:95
  26.8 15.7 %collective-permute-start.4 = (bf16[64,3584]{1,0:T(8,128)(2,1)S(1)}, bf16[64,3584]{1,0:T(8,128)(2,1)S(1)}, u32[]{:S(2)}, u32[]{:S(2)}) collective-permute-start(bf16[64,3584]{1,0:T(8,128)(2,1)S(1)} %collective-permute-done.2), channel_id=1, source_target_pairs={{8,12},{4,0},{9,13},{5,1},{10,14},{6,2},{11,15},{7,3},{24,28},{20,... | collective-permute-start | bytes 1376264 | tf_op jit(solution)/shard_map/ppermute | solution.py:95
  29.8 21.8 %slice-start = ((s8[14680064]{0:T(1024)(128)(4,1)}), s8[4194304]{0:T(1024)(128)(4,1)S(1)}, s32[]{:S(2)}) async-start(s8[14680064]{0:T(1024)(128)(4,1)} %bitcast.29), calls=%async_computation | async-start | bytes 8388608
  29.8 21.7 %collective-permute-start.8 = (f32[64,256]{1,0:T(8,128)S(1)}, f32[64,256]{1,0:T(8,128)S(1)}, u32[]{:S(2)}, u32[]{:S(2)}) collective-permute-start(f32[64,256]{1,0:T(8,128)S(1)} %get-tuple-element.20), channel_id=1, source_target_pairs={{0,1},{1,0},{2,3},{3,2},{4,5},{5,4},{6,7},{7,6},{8,9},{9,8},{10,11... | collective-permute-start | bytes 196616 | tf_op jit(solution)/shard_map/ppermute | solution.py:95
  43.1 8.5 %slice-start.1 = ((s8[14680064]{0:T(1024)(128)(4,1)}), s8[4194304]{0:T(1024)(128)(4,1)S(1)}, s32[]{:S(2)}) async-start(s8[14680064]{0:T(1024)(128)(4,1)} %bitcast.29), calls=%async_computation.1 | async-start | bytes 8388608
  43.1 8.5 %slice-start.2 = ((s8[14680064]{0:T(1024)(128)(4,1)}), s8[4194304]{0:T(1024)(128)(4,1)S(1)}, s32[]{:S(2)}) async-start(s8[14680064]{0:T(1024)(128)(4,1)} %bitcast.29), calls=%async_computation.2 | async-start | bytes 8388608
  43.1 8.5 %slice-start.3 = ((s8[14680064]{0:T(1024)(128)(4,1)}), s8[2097152]{0:T(1024)(128)(4,1)S(1)}, s32[]{:S(2)}) async-start(s8[14680064]{0:T(1024)(128)(4,1)} %bitcast.29), calls=%async_computation.3 | async-start | bytes 4194304
  43.2 8.3 %collective-permute-start.9 = (f32[64,256]{1,0:T(8,128)S(1)}, f32[64,256]{1,0:T(8,128)S(1)}, u32[]{:S(2)}, u32[]{:S(2)}) collective-permute-start(f32[64,256]{1,0:T(8,128)S(1)} %get-tuple-element.22), channel_id=1, source_target_pairs={{0,1},{1,0},{2,3},{3,2},{4,5},{5,4},{6,7},{7,6},{8,9},{9,8},{10,11... | collective-permute-start | bytes 196616 | tf_op jit(solution)/shard_map/ppermute | solution.py:95
  51.5 4.5 %collective-permute-start.10 = (f32[64,256]{1,0:T(8,128)S(1)}, f32[64,256]{1,0:T(8,128)S(1)}, u32[]{:S(2)}, u32[]{:S(2)}) collective-permute-start(f32[64,256]{1,0:T(8,128)S(1)} %get-tuple-element.9), channel_id=1, source_target_pairs={{0,2},{2,0},{1,3},{3,1},{4,6},{6,4},{5,7},{7,5},{8,10},{10,8},{9,1... | collective-permute-start | bytes 196616 | tf_op jit(solution)/shard_map/ppermute | solution.py:95
  54.4 9.9 %copy-start.2 = (bf16[4,64,2048]{2,1,0:T(8,128)(2,1)S(1)}, bf16[4,64,2048]{2,1,0:T(8,128)(2,1)}, u32[]{:S(2)}) copy-start(bf16[4,64,2048]{2,1,0:T(8,128)(2,1)} %param.11) | copy-start | bytes 3145732
  56.1 7.2 %collective-permute-start.11 = (bf16[64,256]{1,0:T(8,128)(2,1)S(1)}, bf16[64,256]{1,0:T(8,128)(2,1)S(1)}, u32[]{:S(2)}, u32[]{:S(2)}) collective-permute-start(bf16[64,256]{1,0:T(8,128)(2,1)S(1)} %add_convert_fusion), channel_id=1, source_target_pairs={{0,4},{4,0},{8,12},{12,8},{1,5},{5,1},{9,13},{13,9},{2,6},{6,2},{1... | collective-permute-start | bytes 98312 | tf_op jit(solution)/shard_map/ppermute | solution.py:95
  56.2 7.7 %collective-permute-start.12 = (bf16[64,256]{1,0:T(8,128)(2,1)S(1)}, bf16[64,256]{1,0:T(8,128)(2,1)S(1)}, u32[]{:S(2)}, u32[]{:S(2)}) collective-permute-start(bf16[64,256]{1,0:T(8,128)(2,1)S(1)} %add_convert_fusion), channel_id=1, source_target_pairs={{0,8},{8,0},{4,12},{12,4},{1,9},{9,1},{5,13},{13,5},{2,10},{10,2},... | collective-permute-start | bytes 98312 | tf_op jit(solution)/shard_map/ppermute | solution.py:95
  58.4 5.7 %collective-permute-start.13 = (bf16[64,256]{1,0:T(8,128)(2,1)S(1)}, bf16[64,256]{1,0:T(8,128)(2,1)S(1)}, u32[]{:S(2)}, u32[]{:S(2)}) collective-permute-start(bf16[64,256]{1,0:T(8,128)(2,1)S(1)} %add_convert_fusion), channel_id=1, source_target_pairs={{0,12},{12,0},{4,8},{8,4},{1,13},{13,1},{5,9},{9,5},{2,14},{14,2},... | collective-permute-start | bytes 98312 | tf_op jit(solution)/shard_map/ppermute | solution.py:95
  63.2 3.0 %collective-permute-start.1 = (bf16[64,2048]{1,0:T(8,128)(2,1)S(1)}, bf16[64,2048]{1,0:T(8,128)(2,1)S(1)}, u32[]{:S(2)}, u32[]{:S(2)}) collective-permute-start(bf16[64,2048]{1,0:T(8,128)(2,1)S(1)} %get-tuple-element.24), channel_id=1, source_target_pairs={{0,1},{1,0},{2,3},{3,2},{4,5},{5,4},{6,7},{7,6},{8,9},{9,8},{10,11... | collective-permute-start | bytes 786440 | tf_op jit(solution)/shard_map/ppermute | solution.py:95
  63.3 2.9 %collective-permute-start.5 = (bf16[64,2048]{1,0:T(8,128)(2,1)S(1)}, bf16[64,2048]{1,0:T(8,128)(2,1)S(1)}, u32[]{:S(2)}, u32[]{:S(2)}) collective-permute-start(bf16[64,2048]{1,0:T(8,128)(2,1)S(1)} %get-tuple-element.26), channel_id=1, source_target_pairs={{0,1},{1,0},{2,3},{3,2},{4,5},{5,4},{6,7},{7,6},{8,9},{9,8},{10,11... | collective-permute-start | bytes 786440 | tf_op jit(solution)/shard_map/ppermute | solution.py:95
  63.8 11.1 %collective-permute-start.16 = (bf16[4,64,2048]{2,1,0:T(8,128)(2,1)}, bf16[4,64,2048]{2,1,0:T(8,128)(2,1)S(1)}, u32[]{:S(2)}, u32[]{:S(2)}) collective-permute-start(bf16[4,64,2048]{2,1,0:T(8,128)(2,1)} %collective-permute-done.14), channel_id=1, source_target_pairs={{0,1},{1,0},{2,3},{3,2},{4,5},{5,4},{6,7},{7,6},{8,9},{9,8},{10,11... | collective-permute-start | bytes 3145736 | tf_op jit(solution)/shard_map/ppermute | solution.py:95
  66.5 8.5 %collective-permute-start.6 = (bf16[64,2048]{1,0:T(8,128)(2,1)S(1)}, bf16[64,2048]{1,0:T(8,128)(2,1)S(1)}, u32[]{:S(2)}, u32[]{:S(2)}) collective-permute-start(bf16[64,2048]{1,0:T(8,128)(2,1)S(1)} %select_convert_fusion), channel_id=1, source_target_pairs={{0,2},{2,0},{1,3},{3,1},{4,6},{6,4},{5,7},{7,5},{8,10},{10,8},{9,1... | collective-permute-start | bytes 786440 | tf_op jit(solution)/shard_map/ppermute | solution.py:95

commit v2 on v0

--- a/solution.py
+++ b/solution.py
@@ -1,6 +1,10 @@
+import functools
+
 import jax
 import jax.numpy as jnp
 from jax import lax
+from jax.experimental import pallas as pl
+from jax.experimental.pallas import tpu as pltpu
 from jax.sharding import PartitionSpec as P
 
 
@@ -9,7 +13,7 @@
     return jnp.sum(jnp.where(matches, mapping[None, :], 0), axis=1)
 
 
-def on_device(hidden_states, tenant_ids, owner_map, down_weight, adapter_down, adapter_up):
+def on_device_general(hidden_states, tenant_ids, owner_map, down_weight, adapter_down, adapter_up):
     rows_dev = hidden_states.shape[0]
     ten_dev = adapter_down.shape[0]
     low_rank = adapter_down.shape[2]
@@ -79,9 +83,254 @@
     return layer_out.astype(jnp.bfloat16)
 
 
+def dot(a, b):
+    return jnp.dot(a, b, preferred_element_type=jnp.float32)
+
+
+def dot_t(a, b):
+    return lax.dot_general(a, b, (((1,), (1,)), ((), ())), preferred_element_type=jnp.float32)
+
+
+CHEAP = pl.CostEstimate(flops=1, bytes_accessed=1, transcendentals=0)
+HERE = pl.BlockSpec(memory_space=pltpu.VMEM)
+TILE = 256
+
+
+def call(kernel, outs, *operands, scratch=()):
+    return pl.pallas_call(
+        kernel,
+        in_specs=[HERE] * len(operands),
+        out_specs=[HERE] * len(outs),
+        out_shape=list(outs),
+        scratch_shapes=list(scratch),
+        cost_estimate=CHEAP,
+        compiler_params=pltpu.CompilerParams(vmem_limit_bytes=8 * 2**20),
+    )(*operands)
+
+
+def tiles(length):
+    return [slice(i, i + TILE) for i in range(0, length, TILE)]
+
+
+def is_even():
+    return lax.axis_index("tenant") % 2 == lax.axis_index("tensor") % 2
+
+
+def is_near():
+    return lax.axis_index("tenant") // 2 == lax.axis_index("tensor") // 2
+
+
+def arrived(end, inner):
+    t = lax.axis_index("tenant")
+    return jnp.where((t == 1) | (t == 2), inner[...], end[...])
+
+
+def own_kernel(x, w, down, base0, low0, a, b):
+    half = a.shape[1]
+    a[...] = x[:, :half]
+    b[...] = x[:, half:]
+    low0[...] = dot_t(x[...], down[...])
+    for part in tiles(w.shape[1]):
+        base0[:, part] = dot(x[...], w[:, part])
+
+
+def middle_kernel(pair, two_a, two_b, w, down, base0, low0, ids, *outs):
+    give, keep, base2, low_give, low_keep, low2, ids_held, both = outs
+    ids_held[...] = ids[...]
+    rows, half = two_a.shape
+    even = is_even()
+    both[:rows] = pair[...]
+    both[rows:, :half] = two_a[...]
+    both[rows:, half:] = two_b[...]
+    low = dot_t(both[...], down[...])
+    low_keep[...] = jnp.where(even, low0[...], low[:rows])
+    low_give[...] = jnp.where(even, low[:rows], low0[...])
+    low2[...] = low[rows:]
+    for part in tiles(w.shape[1]):
+        got = dot(both[...], w[:, part])
+        base1 = got[:rows]
+        base2[:, part] = got[rows:]
+        keep[:, part] = jnp.where(even, base0[:, part], base1)
+        give[:, part] = jnp.where(even, base1, base0[:, part]).astype(give.dtype)
+
+
+def early_kernel(end, inner, w, down, base2, low2, early, low):
+    del base2
+    rows, half = end.shape
+    x = arrived(end, inner)
+    low[:rows] = low2[...]
+    low[rows:] = dot_t(x, down[:, :half])
+    for part in tiles(w.shape[1]):
+        early[:, part] = dot(x, w[:half, part])
+
+
+def low_kernel(end, inner, down, low, keep0, got0, give, keep, both0):
+    rows, half = end.shape
+    even = is_even()
+    low2 = low[:rows]
+    low3 = low[rows:] + dot_t(arrived(end, inner), down[:, half:])
+    keep[...] = jnp.where(even, low2, low3)
+    give[...] = jnp.where(even, low3, low2)
+    both0[...] = keep0[...] + got0[...]
+
+
+def late_kernel(end, inner, w, early, base2, keep0, got0, slots, low_got, give, keep, both0):
+    del slots, low_got
+    half = end.shape[1]
+    x = arrived(end, inner)
+    even = is_even()
+    for part in tiles(w.shape[1]):
+        base3 = early[:, part] + dot(x, w[half:, part])
+        keep[:, part] = jnp.where(even, base2[:, part], base3)
+        give[:, part] = jnp.where(even, base3, base2[:, part]).astype(give.dtype)
+        both0[:, part] = keep0[:, part] + got0[:, part].astype(jnp.float32)
+
+
+def chip_sum_kernel(both0, keep1, got1, mine, other):
+    near = is_near()
+    for part in tiles(mine.shape[1]):
+        both1 = keep1[:, part] + got1[:, part].astype(jnp.float32)
+        mine[:, part] = jnp.where(near, both0[:, part], both1)
+        other[:, part] = jnp.where(near, both1, both0[:, part]).astype(other.dtype)
+
+
+def base_sum_kernel(both0, keep1, got1, low_got, mine, other):
+    del low_got
+    chip_sum_kernel(both0, keep1, got1, mine, other)
+
+
+def low_sum_kernel(both0, keep1, got1, up, mine, other, up_held):
+    chip_sum_kernel(both0, keep1, got1, mine, other)
+    up_held[...] = up[...]
+
+
+def lanes(shape, low_rank):
+    position = lax.broadcasted_iota(jnp.int32, shape, 1)
+    starts = range(low_rank, shape[1], low_rank)
+    return sum((position >= start).astype(jnp.int32) for start in starts)
+
+
+def reduced_kernel(low_rank, mine, got, slots, out):
+    ten_dev = slots.shape[1] // low_rank
+    here = slots[...] - lax.axis_index("tenant") * ten_dev == lanes(slots.shape, low_rank)
+    out[...] = jnp.where(here, mine[...] + got[...], 0.0).astype(out.dtype)
+
+
+def delta_kernel(low_rank, slots, reduced0, reduced1, up0, up1, up2, up3, mine, out):
+    q = lax.axis_index("tensor")
+    f32, bf16 = jnp.float32, jnp.bfloat16
+    wide = slots.shape[1]
+    ten_dev = wide // low_rank
+    lane = lanes(slots.shape, low_rank)
+    i = lax.broadcasted_iota(jnp.int32, (wide, wide), 0)
+    j = lax.broadcasted_iota(jnp.int32, (wide, wide), 1)
+    same = jnp.zeros((wide, wide), f32)
+    for shift in range(-wide + low_rank, wide, low_rank):
+        same = jnp.where(i - j == shift, 1.0, same)
+    spread = dot((reduced0[...].astype(f32) + reduced1[...].astype(f32)).astype(bf16), same.astype(bf16))
+    terms = []
+    for step, up in zip((0, 2, 1, 3), (up0, up1, up2, up3)):
+        here = slots[...] - (q ^ step) * ten_dev == lane
+        terms.append((jnp.where(here, spread, 0.0).astype(bf16), up))
+    for part in tiles(mine.shape[1]):
+        total = mine[:, part]
+        for rows, up in terms:
+            total = total + dot(rows, up[:, part])
+        out[:, part] = total
+
+
+def on_device_4x4(hidden_states, tenant_ids, owner_map, down_weight, adapter_down, adapter_up):
+    rows, depth = hidden_states.shape
+    cols = down_weight.shape[1]
+    half = depth // 2
+    ten_dev, _, low_rank = adapter_down.shape
+    wide = ten_dev * low_rank
+    bf16, f32 = jnp.bfloat16, jnp.float32
+
+    def along(name, pairs):
+        return lambda value: lax.ppermute(value, name, pairs)
+
+    outer_pairs = along("tenant", [(0, 1), (1, 0), (2, 3), (3, 2)])
+    two_apart = along("tenant", [(0, 2), (2, 0), (1, 3), (3, 1)])
+    inner_pair = along("tenant", [(1, 2), (2, 1)])
+    to_ends = along("tenant", [(2, 3), (1, 0)])
+    opposite = along("tenant", [(0, 3), (3, 0), (1, 2), (2, 1)])
+    cores = along("tensor", [(0, 1), (1, 0), (2, 3), (3, 2)])
+    chips = along("tensor", [(0, 2), (2, 0), (1, 3), (3, 1)])
+
+    def out(shape, dtype=f32):
+        return jax.ShapeDtypeStruct(shape, dtype)
+
+    tall, flat, part = (rows, cols), (rows, wide), (rows, half)
+
+    two = [two_apart(hidden_states[:, :half]), two_apart(hidden_states[:, half:])]
+    pair = outer_pairs(hidden_states)
+    up0 = adapter_up.reshape(wide, cols)
+    up1 = chips(up0)
+    down = jnp.transpose(adapter_down, (0, 2, 1)).reshape(wide, depth)
+    base0, low0, *own = call(
+        own_kernel,
+        [out(tall), out(flat), out(part, bf16), out(part, bf16)],
+        hidden_states, down_weight, down,
+    )
+    end = [to_ends(value) for value in two]
+    inner = [inner_pair(value) for value in own]
+    give0, keep0, base2, low_give0, low_keep0, low2, ids = call(
+        middle_kernel,
+        [out(tall, bf16), out(tall), out(tall)] + [out(flat)] * 3 + [out((1, rows), jnp.int32)],
+        pair, *two, down_weight, down, base0, low0, tenant_ids[None],
+        scratch=[pltpu.VMEM((2 * rows, depth), bf16)],
+    )
+    home_ids = lax.ppermute(
+        ids,
+        ("tenant", "tensor"),
+        [(a * 4 + b, b * 4 + a) for a in range(4) for b in range(4)],
+    )
+    slots = jnp.broadcast_to(lookup(home_ids[0], owner_map)[:, None], flat)
+    early, low = call(
+        early_kernel,
+        [out(tall), out((2 * rows, wide))],
+        end[0], inner[0], down_weight, down, base2, low2,
+    )
+    low_give1, low_keep1, low_both0 = call(
+        low_kernel, [out(flat)] * 3, end[1], inner[1], down, low, low_keep0, cores(low_give0)
+    )
+    low_got1 = cores(low_give1)
+    low_mine, low_other, up_held = call(
+        low_sum_kernel,
+        [out(flat)] * 2 + [out((wide, cols), bf16)],
+        low_both0, low_keep1, low_got1, up1,
+    )
+    give1, keep1, both0 = call(
+        late_kernel,
+        [out(tall, bf16), out(tall), out(tall)],
+        end[1], inner[1], down_weight, early, base2, keep0, cores(give0), slots, low_got1,
+    )
+    low_from_chip = chips(low_other)
+    mine, other = call(
+        base_sum_kernel,
+        [out(tall), out(tall, bf16)],
+        both0, keep1, cores(give1), low_from_chip,
+    )
+    from_chip = chips(other)
+    (reduced,) = call(
+        functools.partial(reduced_kernel, low_rank),
+        [out(flat, bf16)],
+        low_mine, low_from_chip, slots,
+    )
+    reduced = reduced + outer_pairs(reduced)
+    (total,) = call(
+        functools.partial(delta_kernel, low_rank),
+        [out(tall)],
+        slots, reduced, two_apart(reduced), up0, up1, cores(up0), cores(up_held), mine,
+    )
+    return (total + from_chip.astype(f32)).astype(bf16)
+
+
 def solution(mesh):
+    small = mesh.shape["tenant"] == 4 and mesh.shape["tensor"] == 4
     return jax.shard_map(
-        on_device,
+        on_device_4x4 if small else on_device_general,
         mesh=mesh,
         in_specs=(
             P(("groups", "tenant"), "tensor"),

time: 155 us -> 65.9 us (0.43)
  blocking collectives: 68.3 us -> 0 us
  waiting for transfers between devices: 39.1 us -> 21.8 us
  between operations: 14.2 us -> 0.24 us
  matrix products: 13 us -> 0 us
  Pallas kernels: 0 us -> 10.6 us
  starting transfers between devices: 13.2 us -> 23.3 us
  local copies, waits for them, and re-layouts: 3.09 us -> 8.86 us
  other arithmetic: 3.89 us -> 0.85 us
    unnamed x1 -> x0, blocking collectives: 44.2 us -> none
    reduce_scatter x1 -> x0, waiting for transfers between devices: 29.8 us -> none  [on_device(): lax.psum_scatter(jnp.dot(everyone, down_weight, preferred_element_type=jn...]
    ppermute x0 -> x19, starting transfers between devices: none -> 23.3 us  [the longest x18 22.6 us: along(): return lambda value: lax.ppermute(value, name, pairs)]
    ppermute x0 -> x19, waiting for transfers between devices: none -> 21.8 us  [the longest x18 21.8 us: along(): return lambda value: lax.ppermute(value, name, pairs)]
    all_gather x1 -> x0, blocking collectives: 13.1 us -> none  [on_device(): lax.all_gather(my_low.astype(jnp.bfloat16), 'tenant', axis=0, tiled=True)]
    all_to_all x3 -> x0, starting transfers between devices: 13.1 us -> none  [the longest x1 6.32 us: on_device(): lax.all_to_all(local_tags, 'tenant', split_axis=0, concat_axis=0, tiled=T...]
    dot_general x4 -> x0, matrix products: 12.3 us -> none  [the longest x1 7.86 us: on_device(): jnp.dot(everyone, down_weight, preferred_element_type=jnp.float32)]
    psum x1 -> x0, blocking collectives: 10.9 us -> none  [on_device(): summed = lax.psum(partial_value, 'tensor')]
  transfers between devices with their start and end apart: 5 -> 19, of which waited for: 3 -> 8; matrix products, arithmetic and copies ran while one was open for 5% -> 2% of each run, Pallas kernels for 0% -> 16%
where the time goes in v2:
time: 65.9 us; the launch traced here: 65.6 us
  starting transfers between devices  23.3 us (35%)
  waiting for transfers between devices  21.8 us (33%)
  Pallas kernels  10.6 us (16%)
  local copies, waits for them, and re-layouts  8.86 us (13%)
  other arithmetic  0.85 us (1%)
    ppermute x18, starting transfers between devices, along(): return lambda value: lax.ppermute(value, name, pairs)  22.6 us
    ppermute x18, waiting for transfers between devices, along(): return lambda value: lax.ppermute(value, name, pairs)  21.8 us
    pallas_call x9, Pallas kernels, call(): pl.pallas_call(kernel, in_specs=[HERE] * len(operands), out_specs=[HERE]...  10.6 us
    unnamed x16, local copies, waits for them, and re-layouts  7.71 us
  transfers between devices with their start and end apart: 19, of which 8 were waited for; matrix products, arithmetic and copies ran while one was open for 2% of the time, Pallas kernels for 16%

profile of v2, /device:TPU:0, one launch (start us, length us, event | category | flops | bytes accessed | tf_op | source)
XLA Modules:
  0.0 65.6 jit_solution(6775385344833364720)
XLA Ops:
  0.0 2.9 %collective-permute-start.10 = (bf16[256,2048]{1,0:T(8,128)(2,1)}, bf16[256,2048]{1,0:T(8,128)(2,1)S(1)}, u32[]{:S(2)}, u32[]{:S(2)}) collective-permute-start(bf16[256,2048]{1,0:T(8,128)(2,1)} %bitcast.10), channel_id=1, source_target_pairs={{0,2},{2,0},{1,3},{3,1},{4,6},{6,4},{5,7},{7,5},{8,10},{10,8},{9,1... | collective-permute-start | bytes 3145736 | tf_op jit(solution)/shard_map/ppermute | solution.py:251
  2.9 1.6 %collective-permute-start = (bf16[64,3584]{1,0:T(8,128)(2,1)}, bf16[64,3584]{1,0:T(8,128)(2,1)S(1)}, u32[]{:S(2)}, u32[]{:S(2)}) collective-permute-start(bf16[64,3584]{1,0:T(8,128)(2,1)} %x.1), channel_id=1, source_target_pairs={{0,4},{4,0},{8,12},{12,8},{1,5},{5,1},{9,13},{13,9},{2,6},{6,2},{1... | collective-permute-start | bytes 1376264 | tf_op jit(solution)/shard_map/ppermute | solution.py:251
  4.5 1.1 %fusion = (bf16[64,1792]{1,0:T(8,128)(2,1)S(1)}, bf16[64,1792]{1,0:T(8,128)(2,1)S(1)}) fusion(bf16[64,3584]{1,0:T(8,128)(2,1)} %x.1), kind=kLoop, calls=%fused_computation.3 | loop fusion | bytes 917504 | tf_op jit(solution)/shard_map/slice | solution.py:266
  5.6 2.7 %collective-permute-start.1 = (bf16[64,1792]{1,0:T(8,128)(2,1)S(1)}, bf16[64,1792]{1,0:T(8,128)(2,1)S(1)}, u32[]{:S(2)}, u32[]{:S(2)}) collective-permute-start(bf16[64,1792]{1,0:T(8,128)(2,1)S(1)} %get-tuple-element.54), channel_id=1, source_target_pairs={{0,8},{8,0},{4,12},{12,4},{1,9},{9,1},{5,13},{13,5},{2,10},{10,2},... | collective-permute-start | bytes 688136 | tf_op jit(solution)/shard_map/ppermute | solution.py:251
  8.3 0.3 collective-permute-start.2
  8.6 0.0 copy-start
  8.6 5.2 %copy-done = bf16[3584,2048]{1,0:T(8,128)(2,1)S(1)} copy-done((bf16[3584,2048]{1,0:T(8,128)(2,1)S(1)}, bf16[3584,2048]{1,0:T(8,128)(2,1)}, u32[]{:S(2)}) %copy-start) | copy-done | bytes 14680088
  13.8 0.0 copy-start.2
  13.8 1.5 %copy-done.2 = bf16[4,3584,64]{1,2,0:T(8,128)(2,1)S(1)} copy-done((bf16[4,3584,64]{1,2,0:T(8,128)(2,1)S(1)}, bf16[4,3584,64]{1,2,0:T(8,128)(2,1)}, u32[]{:S(2)}) %copy-start.2) | copy-done | bytes 1835032
  15.3 0.0 copy-start.4
  15.3 1.0 %copy-done.4 = bf16[64,3584]{1,0:T(8,128)(2,1)S(1)} copy-done((bf16[64,3584]{1,0:T(8,128)(2,1)S(1)}, bf16[64,3584]{1,0:T(8,128)(2,1)}, u32[]{:S(2)}) %copy-start.4) | copy-done | bytes 458776
  16.3 0.0 copy-start.1
  16.3 3.2 %shard_map.64 = (f32[64,2048]{1,0:T(8,128)S(1)}, f32[64,256]{1,0:T(8,128)S(1)}, bf16[64,1792]{1,0:T(8,128)(2,1)S(1)}, bf16[64,1792]{1,0:T(8,128)(2,1)S(1)}) custom-call(bf16[64,3584]{1,0:T(8,128)(2,1)S(1)} %copy-done.4, bf16[3584,2048]{1,0:T(8,128)(2,1)S(1)} %copy-done, bf16[256,3584]{1,0:T(8,128)(2,1)S(1)} %bitcast.6), custom_call_target="tpu_custom_call" | custom-call | flops 1 | bytes 1 | tf_op jit(solution)/shard_map/pallas_call | solution.py:100
  19.5 0.8 %collective-permute-start.7 = (bf16[64,1792]{1,0:T(8,128)(2,1)S(1)}, bf16[64,1792]{1,0:T(8,128)(2,1)S(1)}, u32[]{:S(2)}, u32[]{:S(2)}) collective-permute-start(bf16[64,1792]{1,0:T(8,128)(2,1)S(1)} %get-tuple-element.33), channel_id=1, source_target_pairs={{4,8},{8,4},{5,9},{9,5},{6,10},{10,6},{7,11},{11,7},{20,24},{24,20... | collective-permute-start | bytes 688136 | tf_op jit(solution)/shard_map/ppermute | solution.py:251
  20.3 0.4 collective-permute-done.1.two_a
  20.7 1.4 %collective-permute-start.6 = (bf16[64,1792]{1,0:T(8,128)(2,1)S(1)}, bf16[64,1792]{1,0:T(8,128)(2,1)S(1)}, u32[]{:S(2)}, u32[]{:S(2)}) collective-permute-start(bf16[64,1792]{1,0:T(8,128)(2,1)S(1)} %collective-permute-done.1.two_a), channel_id=1, source_target_pairs={{8,12},{4,0},{9,13},{5,1},{10,14},{6,2},{11,15},{7,3},{24,28},{20,... | collective-permute-start | bytes 688136 | tf_op jit(solution)/shard_map/ppermute | solution.py:251
  22.1 7.1 %collective-permute-done.2.two_b = bf16[64,1792]{1,0:T(8,128)(2,1)S(1)} collective-permute-done((bf16[64,1792]{1,0:T(8,128)(2,1)S(1)}, bf16[64,1792]{1,0:T(8,128)(2,1)S(1)}, u32[]{:S(2)}, u32[]{:S(2)}) %collective-permute-start.2) | collective-permute-done | bytes 229408 | tf_op jit(solution)/shard_map/ppermute | solution.py:251
  29.1 0.7 %collective-permute-start.5 = (bf16[64,1792]{1,0:T(8,128)(2,1)S(1)}, bf16[64,1792]{1,0:T(8,128)(2,1)S(1)}, u32[]{:S(2)}, u32[]{:S(2)}) collective-permute-start(bf16[64,1792]{1,0:T(8,128)(2,1)S(1)} %get-tuple-element.32), channel_id=1, source_target_pairs={{4,8},{8,4},{5,9},{9,5},{6,10},{10,6},{7,11},{11,7},{20,24},{24,20... | collective-permute-start | bytes 688136 | tf_op jit(solution)/shard_map/ppermute | solution.py:251
  29.8 0.0 collective-permute-done.pair
  29.8 1.3 %collective-permute-start.4 = (bf16[64,1792]{1,0:T(8,128)(2,1)S(1)}, bf16[64,1792]{1,0:T(8,128)(2,1)S(1)}, u32[]{:S(2)}, u32[]{:S(2)}) collective-permute-start(bf16[64,1792]{1,0:T(8,128)(2,1)S(1)} %collective-permute-done.2.two_b), channel_id=1, source_target_pairs={{8,12},{4,0},{9,13},{5,1},{10,14},{6,2},{11,15},{7,3},{24,28},{20,... | collective-permute-start | bytes 688136 | tf_op jit(solution)/shard_map/ppermute | solution.py:251
  31.1 0.0 copy-done.6
  31.1 0.0 copy-done.1
  31.1 0.0 copy-done.3
  31.1 0.0 copy-start.5
  31.1 2.7 %shard_map.65 = (bf16[64,2048]{1,0:T(8,128)(2,1)S(1)}, f32[64,2048]{1,0:T(8,128)S(1)}, f32[64,2048]{1,0:T(8,128)S(1)}, f32[64,256]{1,0:T(8,128)S(1)}, f32[64,256...) custom-call(bf16[64,3584]{1,0:T(8,128)(2,1)S(1)} %collective-permute-done.pair, ...), custom_call_target="tpu_custom_call" | custom-call | flops 1 | bytes 1 | tf_op jit(solution)/shard_map/pallas_call | solution.py:100
  33.8 0.0 copy-start.7
  33.8 0.0 collective-permute-done.7.inner
  33.8 0.1 collective-permute-start.8
  33.9 0.0 collective-permute-done.6.end
  33.9 1.7 %shard_map.66 = (f32[64,2048]{1,0:T(8,128)S(1)}, f32[128,256]{1,0:T(8,128)S(1)}) custom-call(bf16[64,1792]{1,0:T(8,128)(2,1)S(1)} %collective-permute-done.6.end, bf16[64,1792]{1,0:T(8,128)(2,1)S(1)} %collective-permute-done.7.inner, bf16[3584,2048]{1,0:T(8,128)(2,1)S(1)} %copy-done.1, bf16[256,3584]{1,0:T(8,128)(2,1)S(1)} %bitcast.8, ...), custom_call_target="tpu_custom_call" | custom-call | flops 1 | bytes 1 | tf_op jit(solution)/shard_map/pallas_call | solution.py:100
  35.6 0.0 collective-permute-done.5.inner
  35.6 2.1 %collective-permute-done.4.end = bf16[64,1792]{1,0:T(8,128)(2,1)S(1)} collective-permute-done((bf16[64,1792]{1,0:T(8,128)(2,1)S(1)}, bf16[64,1792]{1,0:T(8,128)(2,1)S(1)}, u32[]{:S(2)}, u32[]{:S(2)}) %collective-permute-start.4) | collective-permute-done | bytes 229408 | tf_op jit(solution)/shard_map/ppermute | solution.py:251
  37.7 0.0 collective-permute-done.8.got0
  37.7 0.4 shard_map.67
  38.2 0.1 collective-permute-start.9
  38.2 0.0 copy-done.5
  38.2 0.5 collective-permute-start.14
  38.7 0.7 %collective-permute-done.9.got1.low_got = f32[64,256]{1,0:T(8,128)S(1)} collective-permute-done((f32[64,256]{1,0:T(8,128)S(1)}, f32[64,256]{1,0:T(8,128)S(1)}, u32[]{:S(2)}, u32[]{:S(2)}) %collective-permute-start.9) | collective-permute-done | bytes 65568 | tf_op jit(solution)/shard_map/ppermute | solution.py:251
  39.5 0.0 collective-permute-done.10.up.up1
  39.5 0.1 shard_map.68
  39.6 0.2 collective-permute-start.15
  39.8 0.4 collective-permute-start.16
  40.2 0.6 collective-permute-start.3
  40.8 0.0 collective-permute-done.3
  40.8 0.0 copy-done.7
  40.8 0.1 select_reduce_fusion
  40.9 2.0 %collective-permute-done.16.got0 = bf16[64,2048]{1,0:T(8,128)(2,1)S(1)} collective-permute-done((bf16[64,2048]{1,0:T(8,128)(2,1)S(1)}, bf16[64,2048]{1,0:T(8,128)(2,1)S(1)}, u32[]{:S(2)}, u32[]{:S(2)}) %collective-permute-start.16) | collective-permute-done | bytes 262176 | tf_op jit(solution)/shard_map/ppermute | solution.py:251
  42.9 0.1 broadcast_in_dim.26.slots
  43.0 1.5 %shard_map.70 = (bf16[64,2048]{1,0:T(8,128)(2,1)S(1)}, f32[64,2048]{1,0:T(8,128)S(1)}, f32[64,2048]{1,0:T(8,128)S(1)}) custom-call(bf16[64,1792]{1,0:T(8,128)(2,1)S(1)} %collective-permute-done.4.end, bf16[64,1792]{1,0:T(8,128)(2,1)S(1)} %collective-permute-done.5.inner, bf16[3584,2048]{1,0:T(8,128)(2,1)S(1)} %copy-done.1, ...), custom_call_target="tpu_custom_call" | custom-call | flops 1 | bytes 1 | tf_op jit(solution)/shard_map/pallas_call | solution.py:100
  44.5 2.4 %collective-permute-start.17 = (bf16[64,2048]{1,0:T(8,128)(2,1)S(1)}, bf16[64,2048]{1,0:T(8,128)(2,1)S(1)}, u32[]{:S(2)}, u32[]{:S(2)}) collective-permute-start(bf16[64,2048]{1,0:T(8,128)(2,1)S(1)} %get-tuple-element.50), channel_id=1, source_target_pairs={{0,1},{1,0},{2,3},{3,2},{4,5},{5,4},{6,7},{7,6},{8,9},{9,8},{10,11... | collective-permute-start | bytes 786440 | tf_op jit(solution)/shard_map/ppermute | solution.py:251
  46.9 3.2 %collective-permute-start.11 = (f32[64,256]{1,0:T(8,128)S(1)}, f32[64,256]{1,0:T(8,128)S(1)}, u32[]{:S(2)}, u32[]{:S(2)}) collective-permute-start(f32[64,256]{1,0:T(8,128)S(1)} %get-tuple-element.43), channel_id=1, source_target_pairs={{0,2},{2,0},{1,3},{3,1},{4,6},{6,4},{5,7},{7,5},{8,10},{10,8},{9,1... | collective-permute-start | bytes 196616 | tf_op jit(solution)/shard_map/ppermute | solution.py:251
  50.1 0.0 collective-permute-done.17.got1
  50.1 2.3 %collective-permute-done.11.got.low_got = f32[64,256]{1,0:T(8,128)S(1)} collective-permute-done((f32[64,256]{1,0:T(8,128)S(1)}, f32[64,256]{1,0:T(8,128)S(1)}, u32[]{:S(2)}, u32[]{:S(2)}) %collective-permute-start.11) | collective-permute-done | bytes 65568 | tf_op jit(solution)/shard_map/ppermute | solution.py:251
  52.5 0.1 shard_map.71
  52.6 2.0 %collective-permute-start.18 = (bf16[64,2048]{1,0:T(8,128)(2,1)S(1)}, bf16[64,2048]{1,0:T(8,128)(2,1)S(1)}, u32[]{:S(2)}, u32[]{:S(2)}) collective-permute-start(bf16[64,2048]{1,0:T(8,128)(2,1)S(1)} %get-tuple-element.52), channel_id=1, source_target_pairs={{0,2},{2,0},{1,3},{3,1},{4,6},{6,4},{5,7},{7,5},{8,10},{10,8},{9,1... | collective-permute-start | bytes 786440 | tf_op jit(solution)/shard_map/ppermute | solution.py:251
  54.6 0.1 collective-permute-start.12
  54.7 3.9 %collective-permute-done.12 = bf16[64,256]{1,0:T(8,128)(2,1)S(1)} collective-permute-done((bf16[64,256]{1,0:T(8,128)(2,1)S(1)}, bf16[64,256]{1,0:T(8,128)(2,1)S(1)}, u32[]{:S(2)}, u32[]{:S(2)}) %collective-permute-start.12) | collective-permute-done | bytes 32800 | tf_op jit(solution)/shard_map/ppermute | solution.py:251
  58.6 2.0 %collective-permute-start.13 = (bf16[64,256]{1,0:T(8,128)(2,1)S(1)}, bf16[64,256]{1,0:T(8,128)(2,1)S(1)}, u32[]{:S(2)}, u32[]{:S(2)}) collective-permute-start(bf16[64,256]{1,0:T(8,128)(2,1)S(1)} %add.6.reduced0), channel_id=1, source_target_pairs={{0,8},{8,0},{4,12},{12,4},{1,9},{9,1},{5,13},{13,5},{2,10},{10,2},... | collective-permute-start | bytes 98312 | tf_op jit(solution)/shard_map/ppermute | solution.py:251
  60.6 0.0 collective-permute-done.14.up2
  60.6 3.2 %collective-permute-done.13.reduced1 = bf16[64,256]{1,0:T(8,128)(2,1)S(1)} collective-permute-done((bf16[64,256]{1,0:T(8,128)(2,1)S(1)}, bf16[64,256]{1,0:T(8,128)(2,1)S(1)}, u32[]{:S(2)}, u32[]{:S(2)}) %collective-permute-start.13) | collective-permute-done | bytes 32800 | tf_op jit(solution)/shard_map/ppermute | solution.py:251
  63.8 0.0 collective-permute-done.15.up3
  63.8 1.0 %shard_map.72 = f32[64,2048]{1,0:T(8,128)S(1)} custom-call(s32[64,256]{1,0:T(8,128)S(1)} %broadcast_in_dim.26.slots, bf16[64,256]{1,0:T(8,128)(2,1)S(1)} %add.6.reduced0, bf16[64,256]{1,0:T(8,128)(2,1)S(1)} %collective-permute-done.13.reduced1, bf16[256,2048]{1,0:T(8,128)(2,1)S(1)} %bitcast.12, bf16[256,2048]{1,0:T(8,128)(2,1)S(1)} %collective-permute-done.10.up.up1, ...), custom_call_target="tpu_custom_call" | custom-call | flops 1 | bytes 1 | tf_op jit(solution)/shard_map/pallas_call | solution.py:100
  64.8 0.0 collective-permute-done.18
  64.9 0.8 %add_convert_fusion = bf16[64,2048]{1,0:T(8,128)(2,1)} fusion(f32[64,2048]{1,0:T(8,128)S(1)} %shard_map.72, bf16[64,2048]{1,0:T(8,128)(2,1)S(1)} %collective-permute-done.18), kind=kLoop, calls=%fused_computation | loop fusion | flops 393216 | bytes 1048576 | tf_op jit(solution)/shard_map/convert_element_type | solution.py:327
  (4 shorter events, 0.0 us)
Async XLA Ops:
  0.0 31.1 %copy-start.6 = (s32[64]{0:T(128)S(1)}, s32[64]{0:T(128)}, u32[]{:S(2)}) copy-start(s32[64]{0:T(128)} %param.7) | copy-start | bytes 772
  0.0 39.5 %collective-permute-start.10 = (bf16[256,2048]{1,0:T(8,128)(2,1)}, bf16[256,2048]{1,0:T(8,128)(2,1)S(1)}, u32[]{:S(2)}, u32[]{:S(2)}) collective-permute-start(bf16[256,2048]{1,0:T(8,128)(2,1)} %bitcast.10), channel_id=1, source_target_pairs={{0,2},{2,0},{1,3},{3,1},{4,6},{6,4},{5,7},{7,5},{8,10},{10,8},{9,1... | collective-permute-start | bytes 3145736 | tf_op jit(solution)/shard_map/ppermute | solution.py:251
  2.9 26.9 %collective-permute-start = (bf16[64,3584]{1,0:T(8,128)(2,1)}, bf16[64,3584]{1,0:T(8,128)(2,1)S(1)}, u32[]{:S(2)}, u32[]{:S(2)}) collective-permute-start(bf16[64,3584]{1,0:T(8,128)(2,1)} %x.1), channel_id=1, source_target_pairs={{0,4},{4,0},{8,12},{12,8},{1,5},{5,1},{9,13},{13,9},{2,6},{6,2},{1... | collective-permute-start | bytes 1376264 | tf_op jit(solution)/shard_map/ppermute | solution.py:251
  5.6 15.1 %collective-permute-start.1 = (bf16[64,1792]{1,0:T(8,128)(2,1)S(1)}, bf16[64,1792]{1,0:T(8,128)(2,1)S(1)}, u32[]{:S(2)}, u32[]{:S(2)}) collective-permute-start(bf16[64,1792]{1,0:T(8,128)(2,1)S(1)} %get-tuple-element.54), channel_id=1, source_target_pairs={{0,8},{8,0},{4,12},{12,4},{1,9},{9,1},{5,13},{13,5},{2,10},{10,2},... | collective-permute-start | bytes 688136 | tf_op jit(solution)/shard_map/ppermute | solution.py:251
  8.3 20.9 %collective-permute-start.2 = (bf16[64,1792]{1,0:T(8,128)(2,1)S(1)}, bf16[64,1792]{1,0:T(8,128)(2,1)S(1)}, u32[]{:S(2)}, u32[]{:S(2)}) collective-permute-start(bf16[64,1792]{1,0:T(8,128)(2,1)S(1)} %get-tuple-element.53), channel_id=1, source_target_pairs={{0,8},{8,0},{4,12},{12,4},{1,9},{9,1},{5,13},{13,5},{2,10},{10,2},... | collective-permute-start | bytes 688136 | tf_op jit(solution)/shard_map/ppermute | solution.py:251
  8.6 5.2 %copy-start = (bf16[3584,2048]{1,0:T(8,128)(2,1)S(1)}, bf16[3584,2048]{1,0:T(8,128)(2,1)}, u32[]{:S(2)}) copy-start(bf16[3584,2048]{1,0:T(8,128)(2,1)} %w.7) | copy-start | bytes 44040196
  13.8 1.5 %copy-start.2 = (bf16[4,3584,64]{1,2,0:T(8,128)(2,1)S(1)}, bf16[4,3584,64]{1,2,0:T(8,128)(2,1)}, u32[]{:S(2)}) copy-start(bf16[4,3584,64]{1,2,0:T(8,128)(2,1)} %param.10) | copy-start | bytes 5505028
  15.3 1.0 %copy-start.4 = (bf16[64,3584]{1,0:T(8,128)(2,1)S(1)}, bf16[64,3584]{1,0:T(8,128)(2,1)}, u32[]{:S(2)}) copy-start(bf16[64,3584]{1,0:T(8,128)(2,1)} %x.1) | copy-start | bytes 1376260
  16.3 14.8 %copy-start.1 = (bf16[3584,2048]{1,0:T(8,128)(2,1)S(1)}, bf16[3584,2048]{1,0:T(8,128)(2,1)}, u32[]{:S(2)}) copy-start(bf16[3584,2048]{1,0:T(8,128)(2,1)} %w.7) | copy-start | bytes 44040196
  16.3 14.8 %copy-start.3 = (bf16[4,3584,64]{1,2,0:T(8,128)(2,1)S(1)}, bf16[4,3584,64]{1,2,0:T(8,128)(2,1)}, u32[]{:S(2)}) copy-start(bf16[4,3584,64]{1,2,0:T(8,128)(2,1)} %param.10) | copy-start | bytes 5505028
  19.5 14.4 %collective-permute-start.7 = (bf16[64,1792]{1,0:T(8,128)(2,1)S(1)}, bf16[64,1792]{1,0:T(8,128)(2,1)S(1)}, u32[]{:S(2)}, u32[]{:S(2)}) collective-permute-start(bf16[64,1792]{1,0:T(8,128)(2,1)S(1)} %get-tuple-element.33), channel_id=1, source_target_pairs={{4,8},{8,4},{5,9},{9,5},{6,10},{10,6},{7,11},{11,7},{20,24},{24,20... | collective-permute-start | bytes 688136 | tf_op jit(solution)/shard_map/ppermute | solution.py:251
  20.7 13.3 %collective-permute-start.6 = (bf16[64,1792]{1,0:T(8,128)(2,1)S(1)}, bf16[64,1792]{1,0:T(8,128)(2,1)S(1)}, u32[]{:S(2)}, u32[]{:S(2)}) collective-permute-start(bf16[64,1792]{1,0:T(8,128)(2,1)S(1)} %collective-permute-done.1.two_a), channel_id=1, source_target_pairs={{8,12},{4,0},{9,13},{5,1},{10,14},{6,2},{11,15},{7,3},{24,28},{20,... | collective-permute-start | bytes 688136 | tf_op jit(solution)/shard_map/ppermute | solution.py:251
  29.1 6.5 %collective-permute-start.5 = (bf16[64,1792]{1,0:T(8,128)(2,1)S(1)}, bf16[64,1792]{1,0:T(8,128)(2,1)S(1)}, u32[]{:S(2)}, u32[]{:S(2)}) collective-permute-start(bf16[64,1792]{1,0:T(8,128)(2,1)S(1)} %get-tuple-element.32), channel_id=1, source_target_pairs={{4,8},{8,4},{5,9},{9,5},{6,10},{10,6},{7,11},{11,7},{20,24},{24,20... | collective-permute-start | bytes 688136 | tf_op jit(solution)/shard_map/ppermute | solution.py:251
  29.8 7.9 %collective-permute-start.4 = (bf16[64,1792]{1,0:T(8,128)(2,1)S(1)}, bf16[64,1792]{1,0:T(8,128)(2,1)S(1)}, u32[]{:S(2)}, u32[]{:S(2)}) collective-permute-start(bf16[64,1792]{1,0:T(8,128)(2,1)S(1)} %collective-permute-done.2.two_b), channel_id=1, source_target_pairs={{8,12},{4,0},{9,13},{5,1},{10,14},{6,2},{11,15},{7,3},{24,28},{20,... | collective-permute-start | bytes 688136 | tf_op jit(solution)/shard_map/ppermute | solution.py:251
  31.1 7.1 %copy-start.5 = (bf16[4,64,2048]{2,1,0:T(8,128)(2,1)S(1)}, bf16[4,64,2048]{2,1,0:T(8,128)(2,1)}, u32[]{:S(2)}) copy-start(bf16[4,64,2048]{2,1,0:T(8,128)(2,1)} %param.11) | copy-start | bytes 3145732
  33.8 7.0 %copy-start.7 = (s32[16]{0:T(128)S(1)}, s32[16]{0:T(128)}, u32[]{:S(2)}) copy-start(s32[16]{0:T(128)} %param.8) | copy-start | bytes 196
  33.8 3.9 %collective-permute-start.8 = (f32[64,256]{1,0:T(8,128)S(1)}, f32[64,256]{1,0:T(8,128)S(1)}, u32[]{:S(2)}, u32[]{:S(2)}) collective-permute-start(f32[64,256]{1,0:T(8,128)S(1)} %get-tuple-element.38), channel_id=1, source_target_pairs={{0,1},{1,0},{2,3},{3,2},{4,5},{5,4},{6,7},{7,6},{8,9},{9,8},{10,11... | collective-permute-start | bytes 196616 | tf_op jit(solution)/shard_map/ppermute | solution.py:251
  38.2 1.3 %collective-permute-start.9 = (f32[64,256]{1,0:T(8,128)S(1)}, f32[64,256]{1,0:T(8,128)S(1)}, u32[]{:S(2)}, u32[]{:S(2)}) collective-permute-start(f32[64,256]{1,0:T(8,128)S(1)} %get-tuple-element.41), channel_id=1, source_target_pairs={{0,1},{1,0},{2,3},{3,2},{4,5},{5,4},{6,7},{7,6},{8,9},{9,8},{10,11... | collective-permute-start | bytes 196616 | tf_op jit(solution)/shard_map/ppermute | solution.py:251
  38.2 22.3 %collective-permute-start.14 = (bf16[256,2048]{1,0:T(8,128)(2,1)S(1)}, bf16[256,2048]{1,0:T(8,128)(2,1)S(1)}, u32[]{:S(2)}, u32[]{:S(2)}) collective-permute-start(bf16[256,2048]{1,0:T(8,128)(2,1)S(1)} %bitcast.11), channel_id=1, source_target_pairs={{0,1},{1,0},{2,3},{3,2},{4,5},{5,4},{6,7},{7,6},{8,9},{9,8},{10,11... | collective-permute-start | bytes 3145736 | tf_op jit(solution)/shard_map/ppermute | solution.py:251
  39.6 24.2 %collective-permute-start.15 = (bf16[256,2048]{1,0:T(8,128)(2,1)S(1)}, bf16[256,2048]{1,0:T(8,128)(2,1)S(1)}, u32[]{:S(2)}, u32[]{:S(2)}) collective-permute-start(bf16[256,2048]{1,0:T(8,128)(2,1)S(1)} %get-tuple-element.44), channel_id=1, source_target_pairs={{0,1},{1,0},{2,3},{3,2},{4,5},{5,4},{6,7},{7,6},{8,9},{9,8},{10,11... | collective-permute-start | bytes 3145736 | tf_op jit(solution)/shard_map/ppermute | solution.py:251
  39.8 3.1 %collective-permute-start.16 = (bf16[64,2048]{1,0:T(8,128)(2,1)S(1)}, bf16[64,2048]{1,0:T(8,128)(2,1)S(1)}, u32[]{:S(2)}, u32[]{:S(2)}) collective-permute-start(bf16[64,2048]{1,0:T(8,128)(2,1)S(1)} %get-tuple-element.47), channel_id=1, source_target_pairs={{0,1},{1,0},{2,3},{3,2},{4,5},{5,4},{6,7},{7,6},{8,9},{9,8},{10,11... | collective-permute-start | bytes 786440 | tf_op jit(solution)/shard_map/ppermute | solution.py:251
  40.2 0.7 %collective-permute-start.3 = (s32[1,64]{1,0:T(1,128)S(1)}, s32[1,64]{1,0:T(1,128)S(1)}, u32[]{:S(2)}, u32[]{:S(2)}) collective-permute-start(s32[1,64]{1,0:T(1,128)S(1)} %get-tuple-element.31), channel_id=1, source_target_pairs={{0,0},{1,4},{2,8},{3,12},{4,1},{5,5},{6,9},{7,13},{8,2},{9,6},{10,... | collective-permute-start | bytes 776 | tf_op jit(solution)/shard_map/ppermute | solution.py:284
  44.5 5.7 %collective-permute-start.17 = (bf16[64,2048]{1,0:T(8,128)(2,1)S(1)}, bf16[64,2048]{1,0:T(8,128)(2,1)S(1)}, u32[]{:S(2)}, u32[]{:S(2)}) collective-permute-start(bf16[64,2048]{1,0:T(8,128)(2,1)S(1)} %get-tuple-element.50), channel_id=1, source_target_pairs={{0,1},{1,0},{2,3},{3,2},{4,5},{5,4},{6,7},{7,6},{8,9},{9,8},{10,11... | collective-permute-start | bytes 786440 | tf_op jit(solution)/shard_map/ppermute | solution.py:251
  46.9 5.6 %collective-permute-start.11 = (f32[64,256]{1,0:T(8,128)S(1)}, f32[64,256]{1,0:T(8,128)S(1)}, u32[]{:S(2)}, u32[]{:S(2)}) collective-permute-start(f32[64,256]{1,0:T(8,128)S(1)} %get-tuple-element.43), channel_id=1, source_target_pairs={{0,2},{2,0},{1,3},{3,1},{4,6},{6,4},{5,7},{7,5},{8,10},{10,8},{9,1... | collective-permute-start | bytes 196616 | tf_op jit(solution)/shard_map/ppermute | solution.py:251
  52.6 12.3 %collective-permute-start.18 = (bf16[64,2048]{1,0:T(8,128)(2,1)S(1)}, bf16[64,2048]{1,0:T(8,128)(2,1)S(1)}, u32[]{:S(2)}, u32[]{:S(2)}) collective-permute-start(bf16[64,2048]{1,0:T(8,128)(2,1)S(1)} %get-tuple-element.52), channel_id=1, source_target_pairs={{0,2},{2,0},{1,3},{3,1},{4,6},{6,4},{5,7},{7,5},{8,10},{10,8},{9,1... | collective-permute-start | bytes 786440 | tf_op jit(solution)/shard_map/ppermute | solution.py:251
  54.6 4.0 %collective-permute-start.12 = (bf16[64,256]{1,0:T(8,128)(2,1)S(1)}, bf16[64,256]{1,0:T(8,128)(2,1)S(1)}, u32[]{:S(2)}, u32[]{:S(2)}) collective-permute-start(bf16[64,256]{1,0:T(8,128)(2,1)S(1)} %shard_map.69), channel_id=1, source_target_pairs={{0,4},{4,0},{8,12},{12,8},{1,5},{5,1},{9,13},{13,9},{2,6},{6,2},{1... | collective-permute-start | bytes 98312 | tf_op jit(solution)/shard_map/ppermute | solution.py:251
  58.6 5.2 %collective-permute-start.13 = (bf16[64,256]{1,0:T(8,128)(2,1)S(1)}, bf16[64,256]{1,0:T(8,128)(2,1)S(1)}, u32[]{:S(2)}, u32[]{:S(2)}) collective-permute-start(bf16[64,256]{1,0:T(8,128)(2,1)S(1)} %add.6.reduced0), channel_id=1, source_target_pairs={{0,8},{8,0},{4,12},{12,4},{1,9},{9,1},{5,13},{13,5},{2,10},{10,2},... | collective-permute-start | bytes 98312 | tf_op jit(solution)/shard_map/ppermute | solution.py:251

commit v3 on v2

--- a/solution.py
+++ b/solution.py
@@ -91,19 +91,20 @@
     return lax.dot_general(a, b, (((1,), (1,)), ((), ())), preferred_element_type=jnp.float32)
 
 
+LATE = 2**23
 CHEAP = pl.CostEstimate(flops=1, bytes_accessed=1, transcendentals=0)
 HERE = pl.BlockSpec(memory_space=pltpu.VMEM)
 TILE = 256
 
 
-def call(kernel, outs, *operands, scratch=()):
+def call(kernel, outs, *operands, scratch=(), cost=CHEAP):
     return pl.pallas_call(
         kernel,
         in_specs=[HERE] * len(operands),
         out_specs=[HERE] * len(outs),
         out_shape=list(outs),
         scratch_shapes=list(scratch),
-        cost_estimate=CHEAP,
+        cost_estimate=cost,
         compiler_params=pltpu.CompilerParams(vmem_limit_bytes=8 * 2**20),
     )(*operands)
 
@@ -134,73 +135,76 @@
         base0[:, part] = dot(x[...], w[:, part])
 
 
-def middle_kernel(pair, two_a, two_b, w, down, base0, low0, ids, *outs):
-    give, keep, base2, low_give, low_keep, low2, ids_held, both = outs
-    ids_held[...] = ids[...]
+def middle_kernel(pair, two_a, two_b, w, down, base1, base2, low, both):
     rows, half = two_a.shape
-    even = is_even()
     both[:rows] = pair[...]
     both[rows:, :half] = two_a[...]
     both[rows:, half:] = two_b[...]
-    low = dot_t(both[...], down[...])
-    low_keep[...] = jnp.where(even, low0[...], low[:rows])
-    low_give[...] = jnp.where(even, low[:rows], low0[...])
-    low2[...] = low[rows:]
+    low[...] = dot_t(both[...], down[...])
     for part in tiles(w.shape[1]):
         got = dot(both[...], w[:, part])
-        base1 = got[:rows]
+        base1[:, part] = got[:rows]
         base2[:, part] = got[rows:]
-        keep[:, part] = jnp.where(even, base0[:, part], base1)
-        give[:, part] = jnp.where(even, base1, base0[:, part]).astype(give.dtype)
-
-
-def early_kernel(end, inner, w, down, base2, low2, early, low):
+
+
+def early_kernel(end, inner, w, down, base2, low12, early, low_early):
     del base2
     rows, half = end.shape
     x = arrived(end, inner)
-    low[:rows] = low2[...]
-    low[rows:] = dot_t(x, down[:, :half])
+    low_early[:rows] = low12[rows:]
+    low_early[rows:] = dot_t(x, down[:, :half])
     for part in tiles(w.shape[1]):
         early[:, part] = dot(x, w[:half, part])
 
 
-def low_kernel(end, inner, down, low, keep0, got0, give, keep, both0):
+def pick(blocks, part, give, keep):
+    even = is_even()
+    rows = blocks[0].shape[0]
+    for at in (0, 1):
+        first, second = blocks[2 * at], blocks[2 * at + 1]
+        target = slice(at * rows, (at + 1) * rows)
+        keep[target, part] = jnp.where(even, first, second)
+        give[target, part] = jnp.where(even, second, first).astype(give.dtype)
+
+
+def low_kernel(end, inner, down, low0, low12, low_early, give, keep):
     rows, half = end.shape
-    even = is_even()
-    low2 = low[:rows]
-    low3 = low[rows:] + dot_t(arrived(end, inner), down[:, half:])
-    keep[...] = jnp.where(even, low2, low3)
-    give[...] = jnp.where(even, low3, low2)
-    both0[...] = keep0[...] + got0[...]
-
-
-def late_kernel(end, inner, w, early, base2, keep0, got0, slots, low_got, give, keep, both0):
-    del slots, low_got
+    low3 = low_early[rows:] + dot_t(arrived(end, inner), down[:, half:])
+    blocks = (low0[...], low12[:rows], low_early[:rows], low3)
+    pick(blocks, slice(None), give, keep)
+
+
+def late_kernel(end, inner, w, early, low_give, base3):
+    del low_give
     half = end.shape[1]
     x = arrived(end, inner)
-    even = is_even()
     for part in tiles(w.shape[1]):
-        base3 = early[:, part] + dot(x, w[half:, part])
-        keep[:, part] = jnp.where(even, base2[:, part], base3)
-        give[:, part] = jnp.where(even, base3, base2[:, part]).astype(give.dtype)
-        both0[:, part] = keep0[:, part] + got0[:, part].astype(jnp.float32)
-
-
-def chip_sum_kernel(both0, keep1, got1, mine, other):
+        base3[:, part] = early[:, part] + dot(x, w[half:, part])
+
+
+def pick_kernel(base0, base1, base2, base3, low_other, give, keep):
+    del low_other
+    for part in tiles(base0.shape[1]):
+        pick([block[:, part] for block in (base0, base1, base2, base3)], part, give, keep)
+
+
+def chip_sum_kernel(keep, got, mine, other):
     near = is_near()
+    rows = mine.shape[0]
     for part in tiles(mine.shape[1]):
-        both1 = keep1[:, part] + got1[:, part].astype(jnp.float32)
-        mine[:, part] = jnp.where(near, both0[:, part], both1)
-        other[:, part] = jnp.where(near, both1, both0[:, part]).astype(other.dtype)
-
-
-def base_sum_kernel(both0, keep1, got1, low_got, mine, other):
+        both = keep[:, part] + got[:, part].astype(jnp.float32)
+        mine[:, part] = jnp.where(near, both[:rows], both[rows:])
+        other[:, part] = jnp.where(near, both[rows:], both[:rows]).astype(other.dtype)
+
+
+def low_sum_kernel(keep, got, base3, mine, other):
+    del base3
+    chip_sum_kernel(keep, got, mine, other)
+
+
+def base_sum_kernel(keep, got, up, low_got, mine, other, up_held):
     del low_got
-    chip_sum_kernel(both0, keep1, got1, mine, other)
-
-
-def low_sum_kernel(both0, keep1, got1, up, mine, other, up_held):
-    chip_sum_kernel(both0, keep1, got1, mine, other)
+    chip_sum_kernel(keep, got, mine, other)
     up_held[...] = up[...]
 
 
@@ -210,27 +214,39 @@
     return sum((position >= start).astype(jnp.int32) for start in starts)
 
 
-def reduced_kernel(low_rank, mine, got, slots, out):
-    ten_dev = slots.shape[1] // low_rank
-    here = slots[...] - lax.axis_index("tenant") * ten_dev == lanes(slots.shape, low_rank)
-    out[...] = jnp.where(here, mine[...] + got[...], 0.0).astype(out.dtype)
-
-
-def delta_kernel(low_rank, slots, reduced0, reduced1, up0, up1, up2, up3, mine, out):
-    q = lax.axis_index("tensor")
+def reduced_kernel(mine, got, slots, up2, out):
+    wide = mine.shape[1]
+    out[:, :wide] = (mine[...] + got[...]).astype(out.dtype)
+    out[:, wide:] = slots[...].astype(jnp.float32).astype(out.dtype)
+
+
+def hold_kernel(first, second, out0, out1):
+    out0[...] = first[...]
+    out1[...] = second[...]
+
+
+def delta_kernel(low_rank, owner0, owner1, owner2, owner3, up0, up1, up2, up3, mine, out):
+    t, q = lax.axis_index("tenant"), lax.axis_index("tensor")
     f32, bf16 = jnp.float32, jnp.bfloat16
-    wide = slots.shape[1]
+    wide = up0.shape[0]
     ten_dev = wide // low_rank
+    owners = [owner0[...], owner1[...], owner2[...], owner3[...]]
+    owners = [owner.astype(f32) for owner in owners]
+    tags = sum(jnp.where((t ^ step) == q, owner[:, wide:], 0.0) for step, owner in enumerate(owners))
+    slots = jnp.concatenate([tags] * (wide // tags.shape[1]), axis=1).astype(jnp.int32)
     lane = lanes(slots.shape, low_rank)
+    chosen = jnp.zeros(slots.shape, f32)
+    for step, owner in enumerate(owners):
+        chosen = chosen + jnp.where(slots - (t ^ step) * ten_dev == lane, owner[:, :wide], 0.0)
     i = lax.broadcasted_iota(jnp.int32, (wide, wide), 0)
     j = lax.broadcasted_iota(jnp.int32, (wide, wide), 1)
     same = jnp.zeros((wide, wide), f32)
     for shift in range(-wide + low_rank, wide, low_rank):
         same = jnp.where(i - j == shift, 1.0, same)
-    spread = dot((reduced0[...].astype(f32) + reduced1[...].astype(f32)).astype(bf16), same.astype(bf16))
+    spread = dot(chosen.astype(bf16), same.astype(bf16))
     terms = []
     for step, up in zip((0, 2, 1, 3), (up0, up1, up2, up3)):
-        here = slots[...] - (q ^ step) * ten_dev == lane
+        here = slots - (q ^ step) * ten_dev == lane
         terms.append((jnp.where(here, spread, 0.0).astype(bf16), up))
     for part in tiles(mine.shape[1]):
         total = mine[:, part]
@@ -275,54 +291,48 @@
     )
     end = [to_ends(value) for value in two]
     inner = [inner_pair(value) for value in own]
-    give0, keep0, base2, low_give0, low_keep0, low2, ids = call(
+    base1, base2, low12 = call(
         middle_kernel,
-        [out(tall, bf16), out(tall), out(tall)] + [out(flat)] * 3 + [out((1, rows), jnp.int32)],
-        pair, *two, down_weight, down, base0, low0, tenant_ids[None],
+        [out(tall), out(tall), out((2 * rows, wide))],
+        pair, *two, down_weight, down,
         scratch=[pltpu.VMEM((2 * rows, depth), bf16)],
     )
-    home_ids = lax.ppermute(
-        ids,
-        ("tenant", "tensor"),
-        [(a * 4 + b, b * 4 + a) for a in range(4) for b in range(4)],
-    )
-    slots = jnp.broadcast_to(lookup(home_ids[0], owner_map)[:, None], flat)
-    early, low = call(
+    early, low_early = call(
         early_kernel,
         [out(tall), out((2 * rows, wide))],
-        end[0], inner[0], down_weight, down, base2, low2,
-    )
-    low_give1, low_keep1, low_both0 = call(
-        low_kernel, [out(flat)] * 3, end[1], inner[1], down, low, low_keep0, cores(low_give0)
-    )
-    low_got1 = cores(low_give1)
-    low_mine, low_other, up_held = call(
-        low_sum_kernel,
-        [out(flat)] * 2 + [out((wide, cols), bf16)],
-        low_both0, low_keep1, low_got1, up1,
-    )
-    give1, keep1, both0 = call(
-        late_kernel,
-        [out(tall, bf16), out(tall), out(tall)],
-        end[1], inner[1], down_weight, early, base2, keep0, cores(give0), slots, low_got1,
+        end[0], inner[0], down_weight, down, base2, low12,
+    )
+    low_give, low_keep = call(
+        low_kernel, [out((2 * rows, wide))] * 2, end[1], inner[1], down, low0, low12, low_early
+    )
+    (base3,) = call(late_kernel, [out(tall)], end[1], inner[1], down_weight, early, low_give)
+    low_mine, low_other = call(
+        low_sum_kernel, [out(flat)] * 2, low_keep, cores(low_give), base3
     )
     low_from_chip = chips(low_other)
-    mine, other = call(
+    give, keep = call(
+        pick_kernel,
+        [out((2 * rows, cols), bf16), out((2 * rows, cols))],
+        base0, base1, base2, base3, low_other,
+    )
+    mine, other, up_held = call(
         base_sum_kernel,
-        [out(tall), out(tall, bf16)],
-        both0, keep1, cores(give1), low_from_chip,
+        [out(tall), out(tall, bf16), out((wide, cols), bf16)],
+        keep, cores(give), up1, low_from_chip,
     )
     from_chip = chips(other)
+    up2 = cores(up0)
+    slots = jnp.broadcast_to(lookup(tenant_ids, owner_map)[:, None], (rows, 128))
     (reduced,) = call(
-        functools.partial(reduced_kernel, low_rank),
-        [out(flat, bf16)],
-        low_mine, low_from_chip, slots,
-    )
-    reduced = reduced + outer_pairs(reduced)
+        reduced_kernel, [out((rows, wide + 128), bf16)], low_mine, low_from_chip, slots, up2
+    )
+    shape = out((rows, wide + 128), bf16)
+    held, two = call(hold_kernel, [shape] * 2, reduced, two_apart(reduced))
+    owners = [held, outer_pairs(reduced), two, opposite(reduced)]
     (total,) = call(
         functools.partial(delta_kernel, low_rank),
         [out(tall)],
-        slots, reduced, two_apart(reduced), up0, up1, cores(up0), cores(up_held), mine,
+        *owners, up0, up1, up2, cores(up_held), mine,
     )
     return (total + from_chip.astype(f32)).astype(bf16)
 

time: 65.9 us -> 55.5 us (0.84)
  waiting for transfers between devices: 21.8 us -> 15.7 us
  starting transfers between devices: 23.3 us -> 19 us
    ppermute x18 -> x17, waiting for transfers between devices: 21.8 us -> 15.7 us  [along(): return lambda value: lax.ppermute(value, name, pairs)]
    ppermute x18 -> x17, starting transfers between devices: 22.6 us -> 19 us  [along(): return lambda value: lax.ppermute(value, name, pairs)]
    pallas_call x9 -> x11, Pallas kernels: 10.6 us -> 10.7 us  [call(): pl.pallas_call(kernel, in_specs=[HERE] * len(operands), out_specs=[HERE]...]
  transfers between devices with their start and end apart: 19 -> 17, of which waited for: 8 -> 6; matrix products, arithmetic and copies ran while one was open for 2% -> 2% of each run, Pallas kernels for 16% -> 19%
where the time goes in v3:
time: 55.5 us; the launch traced here: 55.3 us
  starting transfers between devices  19 us (34%)
  waiting for transfers between devices  15.7 us (28%)
  Pallas kernels  10.7 us (19%)
  local copies, waits for them, and re-layouts  8.86 us (16%)
  other arithmetic  0.85 us (2%)
    ppermute x17, starting transfers between devices, along(): return lambda value: lax.ppermute(value, name, pairs)  19 us
    ppermute x17, waiting for transfers between devices, along(): return lambda value: lax.ppermute(value, name, pairs)  15.7 us
    pallas_call x11, Pallas kernels, call(): pl.pallas_call(kernel, in_specs=[HERE] * len(operands), out_specs=[HERE]...  10.7 us
    unnamed x16, local copies, waits for them, and re-layouts  7.71 us
  transfers between devices with their start and end apart: 17, of which 6 were waited for; matrix products, arithmetic and copies ran while one was open for 2% of the time, Pallas kernels for 19%

profile of v3, /device:TPU:0, one launch (start us, length us, event | category | flops | bytes accessed | tf_op | source)
XLA Modules:
  0.0 55.3 jit_solution(2506096712377281955)
XLA Ops:
  0.0 3.0 %collective-permute-start.3 = (bf16[64,3584]{1,0:T(8,128)(2,1)}, bf16[64,3584]{1,0:T(8,128)(2,1)S(1)}, u32[]{:S(2)}, u32[]{:S(2)}) collective-permute-start(bf16[64,3584]{1,0:T(8,128)(2,1)} %x.1), channel_id=1, source_target_pairs={{0,4},{4,0},{8,12},{12,8},{1,5},{5,1},{9,13},{13,9},{2,6},{6,2},{1... | collective-permute-start | bytes 1376264 | tf_op jit(solution)/shard_map/ppermute | solution.py:267
  3.0 1.1 %fusion = (bf16[64,1792]{1,0:T(8,128)(2,1)S(1)}, bf16[64,1792]{1,0:T(8,128)(2,1)S(1)}) fusion(bf16[64,3584]{1,0:T(8,128)(2,1)} %x.1), kind=kLoop, calls=%fused_computation.3 | loop fusion | bytes 917504 | tf_op jit(solution)/shard_map/slice | solution.py:282
  4.1 2.7 %collective-permute-start.4 = (bf16[64,1792]{1,0:T(8,128)(2,1)S(1)}, bf16[64,1792]{1,0:T(8,128)(2,1)S(1)}, u32[]{:S(2)}, u32[]{:S(2)}) collective-permute-start(bf16[64,1792]{1,0:T(8,128)(2,1)S(1)} %get-tuple-element.45), channel_id=1, source_target_pairs={{0,8},{8,0},{4,12},{12,4},{1,9},{9,1},{5,13},{13,5},{2,10},{10,2},... | collective-permute-start | bytes 688136 | tf_op jit(solution)/shard_map/ppermute | solution.py:267
  6.8 0.3 collective-permute-start
  7.1 1.5 %collective-permute-start.13 = (bf16[256,2048]{1,0:T(8,128)(2,1)}, bf16[256,2048]{1,0:T(8,128)(2,1)S(1)}, u32[]{:S(2)}, u32[]{:S(2)}) collective-permute-start(bf16[256,2048]{1,0:T(8,128)(2,1)} %bitcast.8), channel_id=1, source_target_pairs={{0,2},{2,0},{1,3},{3,1},{4,6},{6,4},{5,7},{7,5},{8,10},{10,8},{9,1... | collective-permute-start | bytes 3145736 | tf_op jit(solution)/shard_map/ppermute | solution.py:267
  8.6 0.0 copy-start
  8.6 5.2 %copy-done = bf16[3584,2048]{1,0:T(8,128)(2,1)S(1)} copy-done((bf16[3584,2048]{1,0:T(8,128)(2,1)S(1)}, bf16[3584,2048]{1,0:T(8,128)(2,1)}, u32[]{:S(2)}) %copy-start) | copy-done | bytes 14680088
  13.8 0.0 copy-start.2
  13.8 1.5 %copy-done.2 = bf16[4,3584,64]{1,2,0:T(8,128)(2,1)S(1)} copy-done((bf16[4,3584,64]{1,2,0:T(8,128)(2,1)S(1)}, bf16[4,3584,64]{1,2,0:T(8,128)(2,1)}, u32[]{:S(2)}) %copy-start.2) | copy-done | bytes 1835032
  15.3 0.0 copy-start.4
  15.3 1.0 %copy-done.4 = bf16[64,3584]{1,0:T(8,128)(2,1)S(1)} copy-done((bf16[64,3584]{1,0:T(8,128)(2,1)S(1)}, bf16[64,3584]{1,0:T(8,128)(2,1)}, u32[]{:S(2)}) %copy-start.4) | copy-done | bytes 458776
  16.3 0.0 copy-start.1
  16.3 0.0 copy-start.3
  16.3 3.2 %shard_map.64 = (f32[64,2048]{1,0:T(8,128)S(1)}, f32[64,256]{1,0:T(8,128)S(1)}, bf16[64,1792]{1,0:T(8,128)(2,1)S(1)}, bf16[64,1792]{1,0:T(8,128)(2,1)S(1)}) custom-call(bf16[64,3584]{1,0:T(8,128)(2,1)S(1)} %copy-done.4, bf16[3584,2048]{1,0:T(8,128)(2,1)S(1)} %copy-done, bf16[256,3584]{1,0:T(8,128)(2,1)S(1)} %bitcast.4), custom_call_target="tpu_custom_call" | custom-call | flops 1 | bytes 1 | tf_op jit(solution)/shard_map/pallas_call | solution.py:101
  19.5 0.8 %collective-permute-start.6 = (bf16[64,1792]{1,0:T(8,128)(2,1)S(1)}, bf16[64,1792]{1,0:T(8,128)(2,1)S(1)}, u32[]{:S(2)}, u32[]{:S(2)}) collective-permute-start(bf16[64,1792]{1,0:T(8,128)(2,1)S(1)} %get-tuple-element.28), channel_id=1, source_target_pairs={{4,8},{8,4},{5,9},{9,5},{6,10},{10,6},{7,11},{11,7},{20,24},{24,20... | collective-permute-start | bytes 688136 | tf_op jit(solution)/shard_map/ppermute | solution.py:267
  20.3 0.0 collective-permute-done.4.two_a
  20.3 1.4 %collective-permute-start.5 = (bf16[64,1792]{1,0:T(8,128)(2,1)S(1)}, bf16[64,1792]{1,0:T(8,128)(2,1)S(1)}, u32[]{:S(2)}, u32[]{:S(2)}) collective-permute-start(bf16[64,1792]{1,0:T(8,128)(2,1)S(1)} %collective-permute-done.4.two_a), channel_id=1, source_target_pairs={{8,12},{4,0},{9,13},{5,1},{10,14},{6,2},{11,15},{7,3},{24,28},{20,... | collective-permute-start | bytes 688136 | tf_op jit(solution)/shard_map/ppermute | solution.py:267
  21.7 6.2 %collective-permute-done.two_b = bf16[64,1792]{1,0:T(8,128)(2,1)S(1)} collective-permute-done((bf16[64,1792]{1,0:T(8,128)(2,1)S(1)}, bf16[64,1792]{1,0:T(8,128)(2,1)S(1)}, u32[]{:S(2)}, u32[]{:S(2)}) %collective-permute-start) | collective-permute-done | bytes 229408 | tf_op jit(solution)/shard_map/ppermute | solution.py:267
  27.9 0.7 %collective-permute-start.2 = (bf16[64,1792]{1,0:T(8,128)(2,1)S(1)}, bf16[64,1792]{1,0:T(8,128)(2,1)S(1)}, u32[]{:S(2)}, u32[]{:S(2)}) collective-permute-start(bf16[64,1792]{1,0:T(8,128)(2,1)S(1)} %get-tuple-element.25), channel_id=1, source_target_pairs={{4,8},{8,4},{5,9},{9,5},{6,10},{10,6},{7,11},{11,7},{20,24},{24,20... | collective-permute-start | bytes 688136 | tf_op jit(solution)/shard_map/ppermute | solution.py:267
  28.6 0.0 collective-permute-done.3.pair
  28.6 1.3 %collective-permute-start.1 = (bf16[64,1792]{1,0:T(8,128)(2,1)S(1)}, bf16[64,1792]{1,0:T(8,128)(2,1)S(1)}, u32[]{:S(2)}, u32[]{:S(2)}) collective-permute-start(bf16[64,1792]{1,0:T(8,128)(2,1)S(1)} %collective-permute-done.two_b), channel_id=1, source_target_pairs={{8,12},{4,0},{9,13},{5,1},{10,14},{6,2},{11,15},{7,3},{24,28},{20,... | collective-permute-start | bytes 688136 | tf_op jit(solution)/shard_map/ppermute | solution.py:267
  29.9 0.0 copy-done.1
  29.9 0.0 copy-done.3
  29.9 2.6 %shard_map.65 = (f32[64,2048]{1,0:T(8,128)S(1)}, f32[64,2048]{1,0:T(8,128)S(1)}, f32[128,256]{1,0:T(8,128)S(1)}) custom-call(bf16[64,3584]{1,0:T(8,128)(2,1)S(1)} %collective-permute-done.3.pair, bf16[64,1792]{1,0:T(8,128)(2,1)S(1)} %collective-permute-done.4.two_a, bf16[64,1792]{1,0:T(8,128)(2,1)S(1)} %collective-permute-done.two_b, ...), custom_call_target="tpu_custom_call" | custom-call | flops 1 | bytes 1 | tf_op jit(solution)/shard_map/pallas_call | solution.py:101
  32.5 0.0 collective-permute-done.6.inner
  32.5 0.2 collective-permute-done.5.end
  32.8 1.7 %shard_map.66 = (f32[64,2048]{1,0:T(8,128)S(1)}, f32[128,256]{1,0:T(8,128)S(1)}) custom-call(bf16[64,1792]{1,0:T(8,128)(2,1)S(1)} %collective-permute-done.5.end, bf16[64,1792]{1,0:T(8,128)(2,1)S(1)} %collective-permute-done.6.inner, bf16[3584,2048]{1,0:T(8,128)(2,1)S(1)} %copy-done.1, bf16[256,3584]{1,0:T(8,128)(2,1)S(1)} %bitcast.6, ...), custom_call_target="tpu_custom_call" | custom-call | flops 1 | bytes 1 | tf_op jit(solution)/shard_map/pallas_call | solution.py:101
  34.4 0.0 copy-start.5
  34.4 0.0 copy-start.6
  34.4 0.0 copy-start.7
  34.4 0.0 collective-permute-done.2.inner
  34.5 2.1 %collective-permute-done.1.end = bf16[64,1792]{1,0:T(8,128)(2,1)S(1)} collective-permute-done((bf16[64,1792]{1,0:T(8,128)(2,1)S(1)}, bf16[64,1792]{1,0:T(8,128)(2,1)S(1)}, u32[]{:S(2)}, u32[]{:S(2)}) %collective-permute-start.1) | collective-permute-done | bytes 229408 | tf_op jit(solution)/shard_map/ppermute | solution.py:267
  36.5 0.4 shard_map.67
  37.0 0.1 collective-permute-start.7
  37.0 1.4 %shard_map.68.base3 = f32[64,2048]{1,0:T(8,128)S(1)} custom-call(bf16[64,1792]{1,0:T(8,128)(2,1)S(1)} %collective-permute-done.1.end, bf16[64,1792]{1,0:T(8,128)(2,1)S(1)} %collective-permute-done.2.inner, bf16[3584,2048]{1,0:T(8,128)(2,1)S(1)} %copy-done.1, f32[64,2048]{1,0:T(8,128)S(1)} %get-tuple-element.33.early, f32[128,256]{1,0:T(8,128)S(1)} %get-tuple-element.32.low_give), custom_call_target="tpu_custom_call" | custom-call | flops 1 | bytes 1 | tf_op jit(solution)/shard_map/pallas_call | solution.py:101
  38.4 0.0 collective-permute-done.7.got
  38.5 0.2 shard_map.72
  38.7 0.6 %collective-permute-start.14 = (bf16[128,2048]{1,0:T(8,128)(2,1)S(1)}, bf16[128,2048]{1,0:T(8,128)(2,1)S(1)}, u32[]{:S(2)}, u32[]{:S(2)}) collective-permute-start(bf16[128,2048]{1,0:T(8,128)(2,1)S(1)} %get-tuple-element.41), channel_id=1, source_target_pairs={{0,1},{1,0},{2,3},{3,2},{4,5},{5,4},{6,7},{7,6},{8,9},{9,8},{10,11... | collective-permute-start | bytes 1572872 | tf_op jit(solution)/shard_map/ppermute | solution.py:267
  39.2 1.5 %collective-permute-start.8 = (f32[64,256]{1,0:T(8,128)S(1)}, f32[64,256]{1,0:T(8,128)S(1)}, u32[]{:S(2)}, u32[]{:S(2)}) collective-permute-start(f32[64,256]{1,0:T(8,128)S(1)} %get-tuple-element.35.low_other), channel_id=1, source_target_pairs={{0,2},{2,0},{1,3},{3,1},{4,6},{6,4},{5,7},{7,5},{8,10},{10,8},{9,1... | collective-permute-start | bytes 196616 | tf_op jit(solution)/shard_map/ppermute | solution.py:267
  40.7 0.0 copy-done.5
  40.7 0.0 collective-permute-start.9
  40.7 2.8 %collective-permute-done.8.got.low_got = f32[64,256]{1,0:T(8,128)S(1)} collective-permute-done((f32[64,256]{1,0:T(8,128)S(1)}, f32[64,256]{1,0:T(8,128)S(1)}, u32[]{:S(2)}, u32[]{:S(2)}) %collective-permute-start.8) | collective-permute-done | bytes 65568 | tf_op jit(solution)/shard_map/ppermute | solution.py:267
  43.5 0.0 collective-permute-done.13.up.up1
  43.5 0.0 collective-permute-done.14.got
  43.5 0.2 shard_map.73
  43.7 0.1 collective-permute-start.15
  43.8 1.5 %collective-permute-start.16 = (bf16[64,2048]{1,0:T(8,128)(2,1)S(1)}, bf16[64,2048]{1,0:T(8,128)(2,1)S(1)}, u32[]{:S(2)}, u32[]{:S(2)}) collective-permute-start(bf16[64,2048]{1,0:T(8,128)(2,1)S(1)} %get-tuple-element.44), channel_id=1, source_target_pairs={{0,2},{2,0},{1,3},{3,1},{4,6},{6,4},{5,7},{7,5},{8,10},{10,8},{9,1... | collective-permute-start | bytes 786440 | tf_op jit(solution)/shard_map/ppermute | solution.py:267
  45.3 0.0 copy-done.6
  45.3 0.0 copy-done.7
  45.3 0.1 select_reduce_fusion
  45.4 0.0 collective-permute-done.9.up2
  45.4 0.1 broadcast_in_dim.23.slots
  45.5 1.9 %collective-permute-start.10 = (bf16[64,384]{1,0:T(8,128)(2,1)S(1)}, bf16[64,384]{1,0:T(8,128)(2,1)S(1)}, u32[]{:S(2)}, u32[]{:S(2)}) collective-permute-start(bf16[64,384]{1,0:T(8,128)(2,1)S(1)} %shard_map.70.first), channel_id=1, source_target_pairs={{0,8},{8,0},{4,12},{12,4},{1,9},{9,1},{5,13},{13,5},{2,10},{10,2},... | collective-permute-start | bytes 147464 | tf_op jit(solution)/shard_map/ppermute | solution.py:267
  47.4 1.3 %collective-permute-start.12 = (bf16[64,384]{1,0:T(8,128)(2,1)S(1)}, bf16[64,384]{1,0:T(8,128)(2,1)S(1)}, u32[]{:S(2)}, u32[]{:S(2)}) collective-permute-start(bf16[64,384]{1,0:T(8,128)(2,1)S(1)} %shard_map.70.first), channel_id=1, source_target_pairs={{0,12},{12,0},{4,8},{8,4},{1,13},{13,1},{5,9},{9,5},{2,14},{14,2},... | collective-permute-start | bytes 147464 | tf_op jit(solution)/shard_map/ppermute | solution.py:267
  48.7 0.3 collective-permute-start.11
  49.0 2.6 %collective-permute-done.10.second = bf16[64,384]{1,0:T(8,128)(2,1)S(1)} collective-permute-done((bf16[64,384]{1,0:T(8,128)(2,1)S(1)}, bf16[64,384]{1,0:T(8,128)(2,1)S(1)}, u32[]{:S(2)}, u32[]{:S(2)}) %collective-permute-start.10) | collective-permute-done | bytes 49184 | tf_op jit(solution)/shard_map/ppermute | solution.py:267
  51.7 1.8 %collective-permute-done.12.owner3 = bf16[64,384]{1,0:T(8,128)(2,1)S(1)} collective-permute-done((bf16[64,384]{1,0:T(8,128)(2,1)S(1)}, bf16[64,384]{1,0:T(8,128)(2,1)S(1)}, u32[]{:S(2)}, u32[]{:S(2)}) %collective-permute-start.12) | collective-permute-done | bytes 49184 | tf_op jit(solution)/shard_map/ppermute | solution.py:267
  53.4 0.0 collective-permute-done.11.owner1
  53.5 0.0 collective-permute-done.15.up3
  53.5 1.0 %shard_map.74 = f32[64,2048]{1,0:T(8,128)S(1)} custom-call(bf16[64,384]{1,0:T(8,128)(2,1)S(1)} %get-tuple-element.36.owner0, bf16[64,384]{1,0:T(8,128)(2,1)S(1)} %collective-permute-done.11.owner1, bf16[64,384]{1,0:T(8,128)(2,1)S(1)} %get-tuple-element.37.owner2, bf16[64,384]{1,0:T(8,128)(2,1)S(1)} %collective-permute-done.12.owner3, ...), custom_call_target="tpu_custom_call" | custom-call | flops 1 | bytes 1 | tf_op jit(solution)/shard_map/pallas_call | solution.py:101
  54.5 0.0 collective-permute-done.16
  54.5 0.8 %add_convert_fusion = bf16[64,2048]{1,0:T(8,128)(2,1)} fusion(f32[64,2048]{1,0:T(8,128)S(1)} %shard_map.74, bf16[64,2048]{1,0:T(8,128)(2,1)S(1)} %collective-permute-done.16), kind=kLoop, calls=%fused_computation | loop fusion | flops 393216 | bytes 1048576 | tf_op jit(solution)/shard_map/convert_element_type | solution.py:337
  (3 shorter events, 0.1 us)
Async XLA Ops:
  0.0 28.6 %collective-permute-start.3 = (bf16[64,3584]{1,0:T(8,128)(2,1)}, bf16[64,3584]{1,0:T(8,128)(2,1)S(1)}, u32[]{:S(2)}, u32[]{:S(2)}) collective-permute-start(bf16[64,3584]{1,0:T(8,128)(2,1)} %x.1), channel_id=1, source_target_pairs={{0,4},{4,0},{8,12},{12,8},{1,5},{5,1},{9,13},{13,9},{2,6},{6,2},{1... | collective-permute-start | bytes 1376264 | tf_op jit(solution)/shard_map/ppermute | solution.py:267
  4.1 16.2 %collective-permute-start.4 = (bf16[64,1792]{1,0:T(8,128)(2,1)S(1)}, bf16[64,1792]{1,0:T(8,128)(2,1)S(1)}, u32[]{:S(2)}, u32[]{:S(2)}) collective-permute-start(bf16[64,1792]{1,0:T(8,128)(2,1)S(1)} %get-tuple-element.45), channel_id=1, source_target_pairs={{0,8},{8,0},{4,12},{12,4},{1,9},{9,1},{5,13},{13,5},{2,10},{10,2},... | collective-permute-start | bytes 688136 | tf_op jit(solution)/shard_map/ppermute | solution.py:267
  6.8 21.2 %collective-permute-start = (bf16[64,1792]{1,0:T(8,128)(2,1)S(1)}, bf16[64,1792]{1,0:T(8,128)(2,1)S(1)}, u32[]{:S(2)}, u32[]{:S(2)}) collective-permute-start(bf16[64,1792]{1,0:T(8,128)(2,1)S(1)} %get-tuple-element.46), channel_id=1, source_target_pairs={{0,8},{8,0},{4,12},{12,4},{1,9},{9,1},{5,13},{13,5},{2,10},{10,2},... | collective-permute-start | bytes 688136 | tf_op jit(solution)/shard_map/ppermute | solution.py:267
  7.1 36.4 %collective-permute-start.13 = (bf16[256,2048]{1,0:T(8,128)(2,1)}, bf16[256,2048]{1,0:T(8,128)(2,1)S(1)}, u32[]{:S(2)}, u32[]{:S(2)}) collective-permute-start(bf16[256,2048]{1,0:T(8,128)(2,1)} %bitcast.8), channel_id=1, source_target_pairs={{0,2},{2,0},{1,3},{3,1},{4,6},{6,4},{5,7},{7,5},{8,10},{10,8},{9,1... | collective-permute-start | bytes 3145736 | tf_op jit(solution)/shard_map/ppermute | solution.py:267
  8.6 5.2 %copy-start = (bf16[3584,2048]{1,0:T(8,128)(2,1)S(1)}, bf16[3584,2048]{1,0:T(8,128)(2,1)}, u32[]{:S(2)}) copy-start(bf16[3584,2048]{1,0:T(8,128)(2,1)} %w.7) | copy-start | bytes 44040196
  13.8 1.5 %copy-start.2 = (bf16[4,3584,64]{1,2,0:T(8,128)(2,1)S(1)}, bf16[4,3584,64]{1,2,0:T(8,128)(2,1)}, u32[]{:S(2)}) copy-start(bf16[4,3584,64]{1,2,0:T(8,128)(2,1)} %param.10) | copy-start | bytes 5505028
  15.3 1.0 %copy-start.4 = (bf16[64,3584]{1,0:T(8,128)(2,1)S(1)}, bf16[64,3584]{1,0:T(8,128)(2,1)}, u32[]{:S(2)}) copy-start(bf16[64,3584]{1,0:T(8,128)(2,1)} %x.1) | copy-start | bytes 1376260
  16.3 13.6 %copy-start.1 = (bf16[3584,2048]{1,0:T(8,128)(2,1)S(1)}, bf16[3584,2048]{1,0:T(8,128)(2,1)}, u32[]{:S(2)}) copy-start(bf16[3584,2048]{1,0:T(8,128)(2,1)} %w.7) | copy-start | bytes 44040196
  16.3 13.6 %copy-start.3 = (bf16[4,3584,64]{1,2,0:T(8,128)(2,1)S(1)}, bf16[4,3584,64]{1,2,0:T(8,128)(2,1)}, u32[]{:S(2)}) copy-start(bf16[4,3584,64]{1,2,0:T(8,128)(2,1)} %param.10) | copy-start | bytes 5505028
  19.5 13.0 %collective-permute-start.6 = (bf16[64,1792]{1,0:T(8,128)(2,1)S(1)}, bf16[64,1792]{1,0:T(8,128)(2,1)S(1)}, u32[]{:S(2)}, u32[]{:S(2)}) collective-permute-start(bf16[64,1792]{1,0:T(8,128)(2,1)S(1)} %get-tuple-element.28), channel_id=1, source_target_pairs={{4,8},{8,4},{5,9},{9,5},{6,10},{10,6},{7,11},{11,7},{20,24},{24,20... | collective-permute-start | bytes 688136 | tf_op jit(solution)/shard_map/ppermute | solution.py:267
  20.3 12.5 %collective-permute-start.5 = (bf16[64,1792]{1,0:T(8,128)(2,1)S(1)}, bf16[64,1792]{1,0:T(8,128)(2,1)S(1)}, u32[]{:S(2)}, u32[]{:S(2)}) collective-permute-start(bf16[64,1792]{1,0:T(8,128)(2,1)S(1)} %collective-permute-done.4.two_a), channel_id=1, source_target_pairs={{8,12},{4,0},{9,13},{5,1},{10,14},{6,2},{11,15},{7,3},{24,28},{20,... | collective-permute-start | bytes 688136 | tf_op jit(solution)/shard_map/ppermute | solution.py:267
  27.9 6.5 %collective-permute-start.2 = (bf16[64,1792]{1,0:T(8,128)(2,1)S(1)}, bf16[64,1792]{1,0:T(8,128)(2,1)S(1)}, u32[]{:S(2)}, u32[]{:S(2)}) collective-permute-start(bf16[64,1792]{1,0:T(8,128)(2,1)S(1)} %get-tuple-element.25), channel_id=1, source_target_pairs={{4,8},{8,4},{5,9},{9,5},{6,10},{10,6},{7,11},{11,7},{20,24},{24,20... | collective-permute-start | bytes 688136 | tf_op jit(solution)/shard_map/ppermute | solution.py:267
  28.6 7.9 %collective-permute-start.1 = (bf16[64,1792]{1,0:T(8,128)(2,1)S(1)}, bf16[64,1792]{1,0:T(8,128)(2,1)S(1)}, u32[]{:S(2)}, u32[]{:S(2)}) collective-permute-start(bf16[64,1792]{1,0:T(8,128)(2,1)S(1)} %collective-permute-done.two_b), channel_id=1, source_target_pairs={{8,12},{4,0},{9,13},{5,1},{10,14},{6,2},{11,15},{7,3},{24,28},{20,... | collective-permute-start | bytes 688136 | tf_op jit(solution)/shard_map/ppermute | solution.py:267
  34.4 6.3 %copy-start.5 = (bf16[4,64,2048]{2,1,0:T(8,128)(2,1)S(1)}, bf16[4,64,2048]{2,1,0:T(8,128)(2,1)}, u32[]{:S(2)}) copy-start(bf16[4,64,2048]{2,1,0:T(8,128)(2,1)} %param.11) | copy-start | bytes 3145732
  34.4 10.9 %copy-start.6 = (s32[16]{0:T(128)S(1)}, s32[16]{0:T(128)}, u32[]{:S(2)}) copy-start(s32[16]{0:T(128)} %param.8) | copy-start | bytes 196
  34.4 10.9 %copy-start.7 = (s32[64]{0:T(128)S(1)}, s32[64]{0:T(128)}, u32[]{:S(2)}) copy-start(s32[64]{0:T(128)} %param.7) | copy-start | bytes 772
  37.0 1.5 %collective-permute-start.7 = (f32[128,256]{1,0:T(8,128)S(1)}, f32[128,256]{1,0:T(8,128)S(1)}, u32[]{:S(2)}, u32[]{:S(2)}) collective-permute-start(f32[128,256]{1,0:T(8,128)S(1)} %get-tuple-element.32.low_give), channel_id=1, source_target_pairs={{0,1},{1,0},{2,3},{3,2},{4,5},{5,4},{6,7},{7,6},{8,9},{9,8},{10,11... | collective-permute-start | bytes 393224 | tf_op jit(solution)/shard_map/ppermute | solution.py:267
  38.7 4.8 %collective-permute-start.14 = (bf16[128,2048]{1,0:T(8,128)(2,1)S(1)}, bf16[128,2048]{1,0:T(8,128)(2,1)S(1)}, u32[]{:S(2)}, u32[]{:S(2)}) collective-permute-start(bf16[128,2048]{1,0:T(8,128)(2,1)S(1)} %get-tuple-element.41), channel_id=1, source_target_pairs={{0,1},{1,0},{2,3},{3,2},{4,5},{5,4},{6,7},{7,6},{8,9},{9,8},{10,11... | collective-permute-start | bytes 1572872 | tf_op jit(solution)/shard_map/ppermute | solution.py:267
  39.2 4.3 %collective-permute-start.8 = (f32[64,256]{1,0:T(8,128)S(1)}, f32[64,256]{1,0:T(8,128)S(1)}, u32[]{:S(2)}, u32[]{:S(2)}) collective-permute-start(f32[64,256]{1,0:T(8,128)S(1)} %get-tuple-element.35.low_other), channel_id=1, source_target_pairs={{0,2},{2,0},{1,3},{3,1},{4,6},{6,4},{5,7},{7,5},{8,10},{10,8},{9,1... | collective-permute-start | bytes 196616 | tf_op jit(solution)/shard_map/ppermute | solution.py:267
  40.7 4.7 %collective-permute-start.9 = (bf16[256,2048]{1,0:T(8,128)(2,1)S(1)}, bf16[256,2048]{1,0:T(8,128)(2,1)S(1)}, u32[]{:S(2)}, u32[]{:S(2)}) collective-permute-start(bf16[256,2048]{1,0:T(8,128)(2,1)S(1)} %bitcast.9), channel_id=1, source_target_pairs={{0,1},{1,0},{2,3},{3,2},{4,5},{5,4},{6,7},{7,6},{8,9},{9,8},{10,11... | collective-permute-start | bytes 3145736 | tf_op jit(solution)/shard_map/ppermute | solution.py:267
  43.7 9.8 %collective-permute-start.15 = (bf16[256,2048]{1,0:T(8,128)(2,1)S(1)}, bf16[256,2048]{1,0:T(8,128)(2,1)S(1)}, u32[]{:S(2)}, u32[]{:S(2)}) collective-permute-start(bf16[256,2048]{1,0:T(8,128)(2,1)S(1)} %get-tuple-element.42), channel_id=1, source_target_pairs={{0,1},{1,0},{2,3},{3,2},{4,5},{5,4},{6,7},{7,6},{8,9},{9,8},{10,11... | collective-permute-start | bytes 3145736 | tf_op jit(solution)/shard_map/ppermute | solution.py:267
  43.8 10.7 %collective-permute-start.16 = (bf16[64,2048]{1,0:T(8,128)(2,1)S(1)}, bf16[64,2048]{1,0:T(8,128)(2,1)S(1)}, u32[]{:S(2)}, u32[]{:S(2)}) collective-permute-start(bf16[64,2048]{1,0:T(8,128)(2,1)S(1)} %get-tuple-element.44), channel_id=1, source_target_pairs={{0,2},{2,0},{1,3},{3,1},{4,6},{6,4},{5,7},{7,5},{8,10},{10,8},{9,1... | collective-permute-start | bytes 786440 | tf_op jit(solution)/shard_map/ppermute | solution.py:267
  45.5 6.2 %collective-permute-start.10 = (bf16[64,384]{1,0:T(8,128)(2,1)S(1)}, bf16[64,384]{1,0:T(8,128)(2,1)S(1)}, u32[]{:S(2)}, u32[]{:S(2)}) collective-permute-start(bf16[64,384]{1,0:T(8,128)(2,1)S(1)} %shard_map.70.first), channel_id=1, source_target_pairs={{0,8},{8,0},{4,12},{12,4},{1,9},{9,1},{5,13},{13,5},{2,10},{10,2},... | collective-permute-start | bytes 147464 | tf_op jit(solution)/shard_map/ppermute | solution.py:267
  47.4 6.0 %collective-permute-start.12 = (bf16[64,384]{1,0:T(8,128)(2,1)S(1)}, bf16[64,384]{1,0:T(8,128)(2,1)S(1)}, u32[]{:S(2)}, u32[]{:S(2)}) collective-permute-start(bf16[64,384]{1,0:T(8,128)(2,1)S(1)} %shard_map.70.first), channel_id=1, source_target_pairs={{0,12},{12,0},{4,8},{8,4},{1,13},{13,1},{5,9},{9,5},{2,14},{14,2},... | collective-permute-start | bytes 147464 | tf_op jit(solution)/shard_map/ppermute | solution.py:267
  48.7 4.7 %collective-permute-start.11 = (bf16[64,384]{1,0:T(8,128)(2,1)S(1)}, bf16[64,384]{1,0:T(8,128)(2,1)S(1)}, u32[]{:S(2)}, u32[]{:S(2)}) collective-permute-start(bf16[64,384]{1,0:T(8,128)(2,1)S(1)} %shard_map.70.first), channel_id=1, source_target_pairs={{0,4},{4,0},{8,12},{12,8},{1,5},{5,1},{9,13},{13,9},{2,6},{6,2},{1... | collective-permute-start | bytes 147464 | tf_op jit(solution)/shard_map/ppermute | solution.py:267

commit v4 on v3

--- a/solution.py
+++ b/solution.py
@@ -167,7 +167,8 @@
         give[target, part] = jnp.where(even, second, first).astype(give.dtype)
 
 
-def low_kernel(end, inner, down, low0, low12, low_early, give, keep):
+def low_kernel(end, inner, down, low0, low12, low_early, slots, give, keep):
+    del slots
     rows, half = end.shape
     low3 = low_early[rows:] + dot_t(arrived(end, inner), down[:, half:])
     blocks = (low0[...], low12[:rows], low_early[:rows], low3)
@@ -215,9 +216,10 @@
 
 
 def reduced_kernel(mine, got, slots, up2, out):
-    wide = mine.shape[1]
-    out[:, :wide] = (mine[...] + got[...]).astype(out.dtype)
-    out[:, wide:] = slots[...].astype(jnp.float32).astype(out.dtype)
+    del up2
+    rows = mine.shape[0]
+    out[:rows] = (mine[...] + got[...].astype(jnp.float32)).astype(out.dtype)
+    out[rows:] = slots[...].astype(jnp.float32).astype(out.dtype)
 
 
 def hold_kernel(first, second, out0, out1):
@@ -232,12 +234,16 @@
     ten_dev = wide // low_rank
     owners = [owner0[...], owner1[...], owner2[...], owner3[...]]
     owners = [owner.astype(f32) for owner in owners]
-    tags = sum(jnp.where((t ^ step) == q, owner[:, wide:], 0.0) for step, owner in enumerate(owners))
-    slots = jnp.concatenate([tags] * (wide // tags.shape[1]), axis=1).astype(jnp.int32)
+    rows = mine.shape[0]
+    tags = sum(jnp.where((t ^ step) == q, owner[rows:], 0.0) for step, owner in enumerate(owners))
+    i = lax.broadcasted_iota(jnp.int32, (rows, wide), 0)
+    j = lax.broadcasted_iota(jnp.int32, (rows, wide), 1)
+    column = jnp.sum(jnp.where(i == j, tags[:1], 0.0), axis=1, keepdims=True)
+    slots = jnp.broadcast_to(column, (rows, wide)).astype(jnp.int32)
     lane = lanes(slots.shape, low_rank)
     chosen = jnp.zeros(slots.shape, f32)
     for step, owner in enumerate(owners):
-        chosen = chosen + jnp.where(slots - (t ^ step) * ten_dev == lane, owner[:, :wide], 0.0)
+        chosen = chosen + jnp.where(slots - (t ^ step) * ten_dev == lane, owner[:rows], 0.0)
     i = lax.broadcasted_iota(jnp.int32, (wide, wide), 0)
     j = lax.broadcasted_iota(jnp.int32, (wide, wide), 1)
     same = jnp.zeros((wide, wide), f32)
@@ -302,12 +308,16 @@
         [out(tall), out((2 * rows, wide))],
         end[0], inner[0], down_weight, down, base2, low12,
     )
+    slots = jnp.pad(lookup(tenant_ids, owner_map), (0, wide - rows))
+    slots = jnp.broadcast_to(slots[None], (16, wide))
     low_give, low_keep = call(
-        low_kernel, [out((2 * rows, wide))] * 2, end[1], inner[1], down, low0, low12, low_early
+        low_kernel,
+        [out((2 * rows, wide))] * 2,
+        end[1], inner[1], down, low0, low12, low_early, slots,
     )
     (base3,) = call(late_kernel, [out(tall)], end[1], inner[1], down_weight, early, low_give)
     low_mine, low_other = call(
-        low_sum_kernel, [out(flat)] * 2, low_keep, cores(low_give), base3
+        low_sum_kernel, [out(flat), out(flat, bf16)], low_keep, cores(low_give), base3
     )
     low_from_chip = chips(low_other)
     give, keep = call(
@@ -322,11 +332,8 @@
     )
     from_chip = chips(other)
     up2 = cores(up0)
-    slots = jnp.broadcast_to(lookup(tenant_ids, owner_map)[:, None], (rows, 128))
-    (reduced,) = call(
-        reduced_kernel, [out((rows, wide + 128), bf16)], low_mine, low_from_chip, slots, up2
-    )
-    shape = out((rows, wide + 128), bf16)
+    shape = out((rows + 16, wide), bf16)
+    (reduced,) = call(reduced_kernel, [shape], low_mine, low_from_chip, slots, up2)
     held, two = call(hold_kernel, [shape] * 2, reduced, two_apart(reduced))
     owners = [held, outer_pairs(reduced), two, opposite(reduced)]
     (total,) = call(

time: 55.5 us -> 55 us (level)
  waiting for transfers between devices: 15.7 us -> 15.1 us
    ppermute x17, waiting for transfers between devices: 15.7 us -> 15.1 us  [along(): return lambda value: lax.ppermute(value, name, pairs)]
  transfers between devices with their start and end apart: 17 -> 17, of which waited for: 6 -> 6; matrix products, arithmetic and copies ran while one was open for 2% -> 2% of each run, Pallas kernels for 19% -> 20%
where the time goes in v4:
time: 55 us; the launch traced here: 54.7 us
  starting transfers between devices  19.1 us (35%)
  waiting for transfers between devices  15.1 us (27%)
  Pallas kernels  10.7 us (19%)
  local copies, waits for them, and re-layouts  8.79 us (16%)
  other arithmetic  0.85 us (2%)
    ppermute x17, starting transfers between devices, along(): return lambda value: lax.ppermute(value, name, pairs)  19.1 us
    ppermute x17, waiting for transfers between devices, along(): return lambda value: lax.ppermute(value, name, pairs)  15.1 us
    pallas_call x11, Pallas kernels, call(): pl.pallas_call(kernel, in_specs=[HERE] * len(operands), out_specs=[HERE]...  10.7 us
    unnamed x16, local copies, waits for them, and re-layouts  7.71 us
  transfers between devices with their start and end apart: 17, of which 6 were waited for; matrix products, arithmetic and copies ran while one was open for 2% of the time, Pallas kernels for 20%

profile of v4, /device:TPU:0, one launch (start us, length us, event | category | flops | bytes accessed | tf_op | source)
XLA Modules:
  0.0 54.7 jit_solution(5639314947158852720)
XLA Ops:
  0.0 0.0 copy-start.6
  0.0 0.0 copy-start.7
  0.0 3.0 %collective-permute-start.3 = (bf16[64,3584]{1,0:T(8,128)(2,1)}, bf16[64,3584]{1,0:T(8,128)(2,1)S(1)}, u32[]{:S(2)}, u32[]{:S(2)}) collective-permute-start(bf16[64,3584]{1,0:T(8,128)(2,1)} %x.3), channel_id=1, source_target_pairs={{0,4},{4,0},{8,12},{12,8},{1,5},{5,1},{9,13},{13,9},{2,6},{6,2},{1... | collective-permute-start | bytes 1376264 | tf_op jit(solution)/shard_map/ppermute | solution.py:273
  3.0 1.1 %fusion = (bf16[64,1792]{1,0:T(8,128)(2,1)S(1)}, bf16[64,1792]{1,0:T(8,128)(2,1)S(1)}) fusion(bf16[64,3584]{1,0:T(8,128)(2,1)} %x.3), kind=kLoop, calls=%fused_computation.3 | loop fusion | bytes 917504 | tf_op jit(solution)/shard_map/slice | solution.py:288
  4.1 2.7 %collective-permute-start.4 = (bf16[64,1792]{1,0:T(8,128)(2,1)S(1)}, bf16[64,1792]{1,0:T(8,128)(2,1)S(1)}, u32[]{:S(2)}, u32[]{:S(2)}) collective-permute-start(bf16[64,1792]{1,0:T(8,128)(2,1)S(1)} %get-tuple-element.45), channel_id=1, source_target_pairs={{0,8},{8,0},{4,12},{12,4},{1,9},{9,1},{5,13},{13,5},{2,10},{10,2},... | collective-permute-start | bytes 688136 | tf_op jit(solution)/shard_map/ppermute | solution.py:273
  6.8 0.3 collective-permute-start
  7.1 1.5 %collective-permute-start.13 = (bf16[256,2048]{1,0:T(8,128)(2,1)}, bf16[256,2048]{1,0:T(8,128)(2,1)S(1)}, u32[]{:S(2)}, u32[]{:S(2)}) collective-permute-start(bf16[256,2048]{1,0:T(8,128)(2,1)} %bitcast.8), channel_id=1, source_target_pairs={{0,2},{2,0},{1,3},{3,1},{4,6},{6,4},{5,7},{7,5},{8,10},{10,8},{9,1... | collective-permute-start | bytes 3145736 | tf_op jit(solution)/shard_map/ppermute | solution.py:273
  8.6 0.0 copy-start
  8.6 5.2 %copy-done = bf16[3584,2048]{1,0:T(8,128)(2,1)S(1)} copy-done((bf16[3584,2048]{1,0:T(8,128)(2,1)S(1)}, bf16[3584,2048]{1,0:T(8,128)(2,1)}, u32[]{:S(2)}) %copy-start) | copy-done | bytes 14680088
  13.8 0.0 copy-start.2
  13.8 1.5 %copy-done.2 = bf16[4,3584,64]{1,2,0:T(8,128)(2,1)S(1)} copy-done((bf16[4,3584,64]{1,2,0:T(8,128)(2,1)S(1)}, bf16[4,3584,64]{1,2,0:T(8,128)(2,1)}, u32[]{:S(2)}) %copy-start.2) | copy-done | bytes 1835032
  15.3 0.0 copy-start.4
  15.3 1.0 %copy-done.4 = bf16[64,3584]{1,0:T(8,128)(2,1)S(1)} copy-done((bf16[64,3584]{1,0:T(8,128)(2,1)S(1)}, bf16[64,3584]{1,0:T(8,128)(2,1)}, u32[]{:S(2)}) %copy-start.4) | copy-done | bytes 458776
  16.3 0.0 copy-start.1
  16.3 0.0 copy-start.3
  16.3 3.2 %shard_map.64 = (f32[64,2048]{1,0:T(8,128)S(1)}, f32[64,256]{1,0:T(8,128)S(1)}, bf16[64,1792]{1,0:T(8,128)(2,1)S(1)}, bf16[64,1792]{1,0:T(8,128)(2,1)S(1)}) custom-call(bf16[64,3584]{1,0:T(8,128)(2,1)S(1)} %copy-done.4, bf16[3584,2048]{1,0:T(8,128)(2,1)S(1)} %copy-done, bf16[256,3584]{1,0:T(8,128)(2,1)S(1)} %bitcast.4), custom_call_target="tpu_custom_call" | custom-call | flops 1 | bytes 1 | tf_op jit(solution)/shard_map/pallas_call | solution.py:101
  19.5 0.8 %collective-permute-start.6 = (bf16[64,1792]{1,0:T(8,128)(2,1)S(1)}, bf16[64,1792]{1,0:T(8,128)(2,1)S(1)}, u32[]{:S(2)}, u32[]{:S(2)}) collective-permute-start(bf16[64,1792]{1,0:T(8,128)(2,1)S(1)} %get-tuple-element.28), channel_id=1, source_target_pairs={{4,8},{8,4},{5,9},{9,5},{6,10},{10,6},{7,11},{11,7},{20,24},{24,20... | collective-permute-start | bytes 688136 | tf_op jit(solution)/shard_map/ppermute | solution.py:273
  20.3 0.0 collective-permute-done.4.two_a
  20.3 1.4 %collective-permute-start.5 = (bf16[64,1792]{1,0:T(8,128)(2,1)S(1)}, bf16[64,1792]{1,0:T(8,128)(2,1)S(1)}, u32[]{:S(2)}, u32[]{:S(2)}) collective-permute-start(bf16[64,1792]{1,0:T(8,128)(2,1)S(1)} %collective-permute-done.4.two_a), channel_id=1, source_target_pairs={{8,12},{4,0},{9,13},{5,1},{10,14},{6,2},{11,15},{7,3},{24,28},{20,... | collective-permute-start | bytes 688136 | tf_op jit(solution)/shard_map/ppermute | solution.py:273
  21.7 6.2 %collective-permute-done.two_b = bf16[64,1792]{1,0:T(8,128)(2,1)S(1)} collective-permute-done((bf16[64,1792]{1,0:T(8,128)(2,1)S(1)}, bf16[64,1792]{1,0:T(8,128)(2,1)S(1)}, u32[]{:S(2)}, u32[]{:S(2)}) %collective-permute-start) | collective-permute-done | bytes 229408 | tf_op jit(solution)/shard_map/ppermute | solution.py:273
  27.9 0.7 %collective-permute-start.2 = (bf16[64,1792]{1,0:T(8,128)(2,1)S(1)}, bf16[64,1792]{1,0:T(8,128)(2,1)S(1)}, u32[]{:S(2)}, u32[]{:S(2)}) collective-permute-start(bf16[64,1792]{1,0:T(8,128)(2,1)S(1)} %get-tuple-element.25), channel_id=1, source_target_pairs={{4,8},{8,4},{5,9},{9,5},{6,10},{10,6},{7,11},{11,7},{20,24},{24,20... | collective-permute-start | bytes 688136 | tf_op jit(solution)/shard_map/ppermute | solution.py:273
  28.6 0.0 collective-permute-done.3.pair
  28.6 1.3 %collective-permute-start.1 = (bf16[64,1792]{1,0:T(8,128)(2,1)S(1)}, bf16[64,1792]{1,0:T(8,128)(2,1)S(1)}, u32[]{:S(2)}, u32[]{:S(2)}) collective-permute-start(bf16[64,1792]{1,0:T(8,128)(2,1)S(1)} %collective-permute-done.two_b), channel_id=1, source_target_pairs={{8,12},{4,0},{9,13},{5,1},{10,14},{6,2},{11,15},{7,3},{24,28},{20,... | collective-permute-start | bytes 688136 | tf_op jit(solution)/shard_map/ppermute | solution.py:273
  29.9 0.0 copy-done.6
  29.9 0.0 copy-done.7
  29.9 0.1 select_reduce_fusion
  30.0 0.0 copy-done.1
  30.0 0.0 copy-done.3
  30.0 2.6 %shard_map.65 = (f32[64,2048]{1,0:T(8,128)S(1)}, f32[64,2048]{1,0:T(8,128)S(1)}, f32[128,256]{1,0:T(8,128)S(1)}) custom-call(bf16[64,3584]{1,0:T(8,128)(2,1)S(1)} %collective-permute-done.3.pair, bf16[64,1792]{1,0:T(8,128)(2,1)S(1)} %collective-permute-done.4.two_a, bf16[64,1792]{1,0:T(8,128)(2,1)S(1)} %collective-permute-done.two_b, ...), custom_call_target="tpu_custom_call" | custom-call | flops 1 | bytes 1 | tf_op jit(solution)/shard_map/pallas_call | solution.py:101
  32.6 0.0 collective-permute-done.6.inner
  32.6 0.1 collective-permute-done.5.end
  32.8 1.7 %shard_map.66 = (f32[64,2048]{1,0:T(8,128)S(1)}, f32[128,256]{1,0:T(8,128)S(1)}) custom-call(bf16[64,1792]{1,0:T(8,128)(2,1)S(1)} %collective-permute-done.5.end, bf16[64,1792]{1,0:T(8,128)(2,1)S(1)} %collective-permute-done.6.inner, bf16[3584,2048]{1,0:T(8,128)(2,1)S(1)} %copy-done.1, bf16[256,3584]{1,0:T(8,128)(2,1)S(1)} %bitcast.6, ...), custom_call_target="tpu_custom_call" | custom-call | flops 1 | bytes 1 | tf_op jit(solution)/shard_map/pallas_call | solution.py:101
  34.4 0.0 copy-start.5
  34.4 0.0 collective-permute-done.2.inner
  34.4 2.1 %collective-permute-done.1.end = bf16[64,1792]{1,0:T(8,128)(2,1)S(1)} collective-permute-done((bf16[64,1792]{1,0:T(8,128)(2,1)S(1)}, bf16[64,1792]{1,0:T(8,128)(2,1)S(1)}, u32[]{:S(2)}, u32[]{:S(2)}) %collective-permute-start.1) | collective-permute-done | bytes 229408 | tf_op jit(solution)/shard_map/ppermute | solution.py:273
  36.5 0.4 shard_map.67
  37.0 0.1 collective-permute-start.7
  37.0 1.4 %shard_map.68.base3 = f32[64,2048]{1,0:T(8,128)S(1)} custom-call(bf16[64,1792]{1,0:T(8,128)(2,1)S(1)} %collective-permute-done.1.end, bf16[64,1792]{1,0:T(8,128)(2,1)S(1)} %collective-permute-done.2.inner, bf16[3584,2048]{1,0:T(8,128)(2,1)S(1)} %copy-done.1, f32[64,2048]{1,0:T(8,128)S(1)} %get-tuple-element.33.early, f32[128,256]{1,0:T(8,128)S(1)} %get-tuple-element.32.low_give), custom_call_target="tpu_custom_call" | custom-call | flops 1 | bytes 1 | tf_op jit(solution)/shard_map/pallas_call | solution.py:101
  38.4 0.0 collective-permute-done.7.got
  38.5 0.2 shard_map.72
  38.6 0.6 %collective-permute-start.14 = (bf16[128,2048]{1,0:T(8,128)(2,1)S(1)}, bf16[128,2048]{1,0:T(8,128)(2,1)S(1)}, u32[]{:S(2)}, u32[]{:S(2)}) collective-permute-start(bf16[128,2048]{1,0:T(8,128)(2,1)S(1)} %get-tuple-element.41), channel_id=1, source_target_pairs={{0,1},{1,0},{2,3},{3,2},{4,5},{5,4},{6,7},{7,6},{8,9},{9,8},{10,11... | collective-permute-start | bytes 1572872 | tf_op jit(solution)/shard_map/ppermute | solution.py:273
  39.2 0.0 copy-done.5
  39.2 0.1 collective-permute-start.9
  39.3 1.5 %collective-permute-start.8 = (bf16[64,256]{1,0:T(8,128)(2,1)S(1)}, bf16[64,256]{1,0:T(8,128)(2,1)S(1)}, u32[]{:S(2)}, u32[]{:S(2)}) collective-permute-start(bf16[64,256]{1,0:T(8,128)(2,1)S(1)} %get-tuple-element.35.low_other), channel_id=1, source_target_pairs={{0,2},{2,0},{1,3},{3,1},{4,6},{6,4},{5,7},{7,5},{8,10},{10,8},{9,1... | collective-permute-start | bytes 98312 | tf_op jit(solution)/shard_map/ppermute | solution.py:273
  40.8 2.4 %collective-permute-done.8.got.low_got = bf16[64,256]{1,0:T(8,128)(2,1)S(1)} collective-permute-done((bf16[64,256]{1,0:T(8,128)(2,1)S(1)}, bf16[64,256]{1,0:T(8,128)(2,1)S(1)}, u32[]{:S(2)}, u32[]{:S(2)}) %collective-permute-start.8) | collective-permute-done | bytes 32800 | tf_op jit(solution)/shard_map/ppermute | solution.py:273
  43.2 0.0 collective-permute-done.13.up.up1
  43.2 0.0 collective-permute-done.14.got
  43.2 0.2 shard_map.73
  43.4 0.1 collective-permute-start.15
  43.5 1.6 %collective-permute-start.16 = (bf16[64,2048]{1,0:T(8,128)(2,1)S(1)}, bf16[64,2048]{1,0:T(8,128)(2,1)S(1)}, u32[]{:S(2)}, u32[]{:S(2)}) collective-permute-start(bf16[64,2048]{1,0:T(8,128)(2,1)S(1)} %get-tuple-element.44), channel_id=1, source_target_pairs={{0,2},{2,0},{1,3},{3,1},{4,6},{6,4},{5,7},{7,5},{8,10},{10,8},{9,1... | collective-permute-start | bytes 786440 | tf_op jit(solution)/shard_map/ppermute | solution.py:273
  45.0 0.0 collective-permute-done.9.up2
  45.1 2.0 %collective-permute-start.10 = (bf16[80,256]{1,0:T(8,128)(2,1)S(1)}, bf16[80,256]{1,0:T(8,128)(2,1)S(1)}, u32[]{:S(2)}, u32[]{:S(2)}) collective-permute-start(bf16[80,256]{1,0:T(8,128)(2,1)S(1)} %shard_map.70.first), channel_id=1, source_target_pairs={{0,8},{8,0},{4,12},{12,4},{1,9},{9,1},{5,13},{13,5},{2,10},{10,2},... | collective-permute-start | bytes 122888 | tf_op jit(solution)/shard_map/ppermute | solution.py:273
  47.0 1.3 %collective-permute-start.12 = (bf16[80,256]{1,0:T(8,128)(2,1)S(1)}, bf16[80,256]{1,0:T(8,128)(2,1)S(1)}, u32[]{:S(2)}, u32[]{:S(2)}) collective-permute-start(bf16[80,256]{1,0:T(8,128)(2,1)S(1)} %shard_map.70.first), channel_id=1, source_target_pairs={{0,12},{12,0},{4,8},{8,4},{1,13},{13,1},{5,9},{9,5},{2,14},{14,2},... | collective-permute-start | bytes 122888 | tf_op jit(solution)/shard_map/ppermute | solution.py:273
  48.3 0.3 collective-permute-start.11
  48.6 2.0 %collective-permute-done.10.second = bf16[80,256]{1,0:T(8,128)(2,1)S(1)} collective-permute-done((bf16[80,256]{1,0:T(8,128)(2,1)S(1)}, bf16[80,256]{1,0:T(8,128)(2,1)S(1)}, u32[]{:S(2)}, u32[]{:S(2)}) %collective-permute-start.10) | collective-permute-done | bytes 40992 | tf_op jit(solution)/shard_map/ppermute | solution.py:273
  50.6 2.3 %collective-permute-done.12.owner3 = bf16[80,256]{1,0:T(8,128)(2,1)S(1)} collective-permute-done((bf16[80,256]{1,0:T(8,128)(2,1)S(1)}, bf16[80,256]{1,0:T(8,128)(2,1)S(1)}, u32[]{:S(2)}, u32[]{:S(2)}) %collective-permute-start.12) | collective-permute-done | bytes 40992 | tf_op jit(solution)/shard_map/ppermute | solution.py:273
  52.8 0.0 collective-permute-done.11.owner1
  52.8 0.0 collective-permute-done.15.up3
  52.8 1.1 %shard_map.74 = f32[64,2048]{1,0:T(8,128)S(1)} custom-call(bf16[80,256]{1,0:T(8,128)(2,1)S(1)} %get-tuple-element.36.owner0, bf16[80,256]{1,0:T(8,128)(2,1)S(1)} %collective-permute-done.11.owner1, bf16[80,256]{1,0:T(8,128)(2,1)S(1)} %get-tuple-element.37.owner2, bf16[80,256]{1,0:T(8,128)(2,1)S(1)} %collective-permute-done.12.owner3, ...), custom_call_target="tpu_custom_call" | custom-call | flops 1 | bytes 1 | tf_op jit(solution)/shard_map/pallas_call | solution.py:101
  53.9 0.0 collective-permute-done.16
  53.9 0.8 %add_convert_fusion = bf16[64,2048]{1,0:T(8,128)(2,1)} fusion(f32[64,2048]{1,0:T(8,128)S(1)} %shard_map.74, bf16[64,2048]{1,0:T(8,128)(2,1)S(1)} %collective-permute-done.16), kind=kLoop, calls=%fused_computation | loop fusion | flops 393216 | bytes 1048576 | tf_op jit(solution)/shard_map/convert_element_type | solution.py:344
  (5 shorter events, 0.1 us)
Async XLA Ops:
  0.0 29.9 %copy-start.6 = (s32[16]{0:T(128)S(1)}, s32[16]{0:T(128)}, u32[]{:S(2)}) copy-start(s32[16]{0:T(128)} %param.8) | copy-start | bytes 196
  0.0 29.9 %copy-start.7 = (s32[64]{0:T(128)S(1)}, s32[64]{0:T(128)}, u32[]{:S(2)}) copy-start(s32[64]{0:T(128)} %param.7) | copy-start | bytes 772
  0.0 28.6 %collective-permute-start.3 = (bf16[64,3584]{1,0:T(8,128)(2,1)}, bf16[64,3584]{1,0:T(8,128)(2,1)S(1)}, u32[]{:S(2)}, u32[]{:S(2)}) collective-permute-start(bf16[64,3584]{1,0:T(8,128)(2,1)} %x.3), channel_id=1, source_target_pairs={{0,4},{4,0},{8,12},{12,8},{1,5},{5,1},{9,13},{13,9},{2,6},{6,2},{1... | collective-permute-start | bytes 1376264 | tf_op jit(solution)/shard_map/ppermute | solution.py:273
  4.1 16.2 %collective-permute-start.4 = (bf16[64,1792]{1,0:T(8,128)(2,1)S(1)}, bf16[64,1792]{1,0:T(8,128)(2,1)S(1)}, u32[]{:S(2)}, u32[]{:S(2)}) collective-permute-start(bf16[64,1792]{1,0:T(8,128)(2,1)S(1)} %get-tuple-element.45), channel_id=1, source_target_pairs={{0,8},{8,0},{4,12},{12,4},{1,9},{9,1},{5,13},{13,5},{2,10},{10,2},... | collective-permute-start | bytes 688136 | tf_op jit(solution)/shard_map/ppermute | solution.py:273
  6.8 21.2 %collective-permute-start = (bf16[64,1792]{1,0:T(8,128)(2,1)S(1)}, bf16[64,1792]{1,0:T(8,128)(2,1)S(1)}, u32[]{:S(2)}, u32[]{:S(2)}) collective-permute-start(bf16[64,1792]{1,0:T(8,128)(2,1)S(1)} %get-tuple-element.46), channel_id=1, source_target_pairs={{0,8},{8,0},{4,12},{12,4},{1,9},{9,1},{5,13},{13,5},{2,10},{10,2},... | collective-permute-start | bytes 688136 | tf_op jit(solution)/shard_map/ppermute | solution.py:273
  7.1 36.1 %collective-permute-start.13 = (bf16[256,2048]{1,0:T(8,128)(2,1)}, bf16[256,2048]{1,0:T(8,128)(2,1)S(1)}, u32[]{:S(2)}, u32[]{:S(2)}) collective-permute-start(bf16[256,2048]{1,0:T(8,128)(2,1)} %bitcast.8), channel_id=1, source_target_pairs={{0,2},{2,0},{1,3},{3,1},{4,6},{6,4},{5,7},{7,5},{8,10},{10,8},{9,1... | collective-permute-start | bytes 3145736 | tf_op jit(solution)/shard_map/ppermute | solution.py:273
  8.6 5.2 %copy-start = (bf16[3584,2048]{1,0:T(8,128)(2,1)S(1)}, bf16[3584,2048]{1,0:T(8,128)(2,1)}, u32[]{:S(2)}) copy-start(bf16[3584,2048]{1,0:T(8,128)(2,1)} %w.7) | copy-start | bytes 44040196
  13.8 1.5 %copy-start.2 = (bf16[4,3584,64]{1,2,0:T(8,128)(2,1)S(1)}, bf16[4,3584,64]{1,2,0:T(8,128)(2,1)}, u32[]{:S(2)}) copy-start(bf16[4,3584,64]{1,2,0:T(8,128)(2,1)} %param.10) | copy-start | bytes 5505028
  15.3 1.0 %copy-start.4 = (bf16[64,3584]{1,0:T(8,128)(2,1)S(1)}, bf16[64,3584]{1,0:T(8,128)(2,1)}, u32[]{:S(2)}) copy-start(bf16[64,3584]{1,0:T(8,128)(2,1)} %x.3) | copy-start | bytes 1376260
  16.3 13.7 %copy-start.1 = (bf16[3584,2048]{1,0:T(8,128)(2,1)S(1)}, bf16[3584,2048]{1,0:T(8,128)(2,1)}, u32[]{:S(2)}) copy-start(bf16[3584,2048]{1,0:T(8,128)(2,1)} %w.7) | copy-start | bytes 44040196
  16.3 13.7 %copy-start.3 = (bf16[4,3584,64]{1,2,0:T(8,128)(2,1)S(1)}, bf16[4,3584,64]{1,2,0:T(8,128)(2,1)}, u32[]{:S(2)}) copy-start(bf16[4,3584,64]{1,2,0:T(8,128)(2,1)} %param.10) | copy-start | bytes 5505028
  19.5 13.1 %collective-permute-start.6 = (bf16[64,1792]{1,0:T(8,128)(2,1)S(1)}, bf16[64,1792]{1,0:T(8,128)(2,1)S(1)}, u32[]{:S(2)}, u32[]{:S(2)}) collective-permute-start(bf16[64,1792]{1,0:T(8,128)(2,1)S(1)} %get-tuple-element.28), channel_id=1, source_target_pairs={{4,8},{8,4},{5,9},{9,5},{6,10},{10,6},{7,11},{11,7},{20,24},{24,20... | collective-permute-start | bytes 688136 | tf_op jit(solution)/shard_map/ppermute | solution.py:273
  20.3 12.5 %collective-permute-start.5 = (bf16[64,1792]{1,0:T(8,128)(2,1)S(1)}, bf16[64,1792]{1,0:T(8,128)(2,1)S(1)}, u32[]{:S(2)}, u32[]{:S(2)}) collective-permute-start(bf16[64,1792]{1,0:T(8,128)(2,1)S(1)} %collective-permute-done.4.two_a), channel_id=1, source_target_pairs={{8,12},{4,0},{9,13},{5,1},{10,14},{6,2},{11,15},{7,3},{24,28},{20,... | collective-permute-start | bytes 688136 | tf_op jit(solution)/shard_map/ppermute | solution.py:273
  27.9 6.5 %collective-permute-start.2 = (bf16[64,1792]{1,0:T(8,128)(2,1)S(1)}, bf16[64,1792]{1,0:T(8,128)(2,1)S(1)}, u32[]{:S(2)}, u32[]{:S(2)}) collective-permute-start(bf16[64,1792]{1,0:T(8,128)(2,1)S(1)} %get-tuple-element.25), channel_id=1, source_target_pairs={{4,8},{8,4},{5,9},{9,5},{6,10},{10,6},{7,11},{11,7},{20,24},{24,20... | collective-permute-start | bytes 688136 | tf_op jit(solution)/shard_map/ppermute | solution.py:273
  28.6 7.9 %collective-permute-start.1 = (bf16[64,1792]{1,0:T(8,128)(2,1)S(1)}, bf16[64,1792]{1,0:T(8,128)(2,1)S(1)}, u32[]{:S(2)}, u32[]{:S(2)}) collective-permute-start(bf16[64,1792]{1,0:T(8,128)(2,1)S(1)} %collective-permute-done.two_b), channel_id=1, source_target_pairs={{8,12},{4,0},{9,13},{5,1},{10,14},{6,2},{11,15},{7,3},{24,28},{20,... | collective-permute-start | bytes 688136 | tf_op jit(solution)/shard_map/ppermute | solution.py:273
  34.4 4.8 %copy-start.5 = (bf16[4,64,2048]{2,1,0:T(8,128)(2,1)S(1)}, bf16[4,64,2048]{2,1,0:T(8,128)(2,1)}, u32[]{:S(2)}) copy-start(bf16[4,64,2048]{2,1,0:T(8,128)(2,1)} %param.11) | copy-start | bytes 3145732
  37.0 1.5 %collective-permute-start.7 = (f32[128,256]{1,0:T(8,128)S(1)}, f32[128,256]{1,0:T(8,128)S(1)}, u32[]{:S(2)}, u32[]{:S(2)}) collective-permute-start(f32[128,256]{1,0:T(8,128)S(1)} %get-tuple-element.32.low_give), channel_id=1, source_target_pairs={{0,1},{1,0},{2,3},{3,2},{4,5},{5,4},{6,7},{7,6},{8,9},{9,8},{10,11... | collective-permute-start | bytes 393224 | tf_op jit(solution)/shard_map/ppermute | solution.py:273
  38.6 4.6 %collective-permute-start.14 = (bf16[128,2048]{1,0:T(8,128)(2,1)S(1)}, bf16[128,2048]{1,0:T(8,128)(2,1)S(1)}, u32[]{:S(2)}, u32[]{:S(2)}) collective-permute-start(bf16[128,2048]{1,0:T(8,128)(2,1)S(1)} %get-tuple-element.41), channel_id=1, source_target_pairs={{0,1},{1,0},{2,3},{3,2},{4,5},{5,4},{6,7},{7,6},{8,9},{9,8},{10,11... | collective-permute-start | bytes 1572872 | tf_op jit(solution)/shard_map/ppermute | solution.py:273
  39.2 5.8 %collective-permute-start.9 = (bf16[256,2048]{1,0:T(8,128)(2,1)S(1)}, bf16[256,2048]{1,0:T(8,128)(2,1)S(1)}, u32[]{:S(2)}, u32[]{:S(2)}) collective-permute-start(bf16[256,2048]{1,0:T(8,128)(2,1)S(1)} %bitcast.9), channel_id=1, source_target_pairs={{0,1},{1,0},{2,3},{3,2},{4,5},{5,4},{6,7},{7,6},{8,9},{9,8},{10,11... | collective-permute-start | bytes 3145736 | tf_op jit(solution)/shard_map/ppermute | solution.py:273
  39.3 3.9 %collective-permute-start.8 = (bf16[64,256]{1,0:T(8,128)(2,1)S(1)}, bf16[64,256]{1,0:T(8,128)(2,1)S(1)}, u32[]{:S(2)}, u32[]{:S(2)}) collective-permute-start(bf16[64,256]{1,0:T(8,128)(2,1)S(1)} %get-tuple-element.35.low_other), channel_id=1, source_target_pairs={{0,2},{2,0},{1,3},{3,1},{4,6},{6,4},{5,7},{7,5},{8,10},{10,8},{9,1... | collective-permute-start | bytes 98312 | tf_op jit(solution)/shard_map/ppermute | solution.py:273
  43.4 9.4 %collective-permute-start.15 = (bf16[256,2048]{1,0:T(8,128)(2,1)S(1)}, bf16[256,2048]{1,0:T(8,128)(2,1)S(1)}, u32[]{:S(2)}, u32[]{:S(2)}) collective-permute-start(bf16[256,2048]{1,0:T(8,128)(2,1)S(1)} %get-tuple-element.42), channel_id=1, source_target_pairs={{0,1},{1,0},{2,3},{3,2},{4,5},{5,4},{6,7},{7,6},{8,9},{9,8},{10,11... | collective-permute-start | bytes 3145736 | tf_op jit(solution)/shard_map/ppermute | solution.py:273
  43.5 10.4 %collective-permute-start.16 = (bf16[64,2048]{1,0:T(8,128)(2,1)S(1)}, bf16[64,2048]{1,0:T(8,128)(2,1)S(1)}, u32[]{:S(2)}, u32[]{:S(2)}) collective-permute-start(bf16[64,2048]{1,0:T(8,128)(2,1)S(1)} %get-tuple-element.44), channel_id=1, source_target_pairs={{0,2},{2,0},{1,3},{3,1},{4,6},{6,4},{5,7},{7,5},{8,10},{10,8},{9,1... | collective-permute-start | bytes 786440 | tf_op jit(solution)/shard_map/ppermute | solution.py:273
  45.1 5.5 %collective-permute-start.10 = (bf16[80,256]{1,0:T(8,128)(2,1)S(1)}, bf16[80,256]{1,0:T(8,128)(2,1)S(1)}, u32[]{:S(2)}, u32[]{:S(2)}) collective-permute-start(bf16[80,256]{1,0:T(8,128)(2,1)S(1)} %shard_map.70.first), channel_id=1, source_target_pairs={{0,8},{8,0},{4,12},{12,4},{1,9},{9,1},{5,13},{13,5},{2,10},{10,2},... | collective-permute-start | bytes 122888 | tf_op jit(solution)/shard_map/ppermute | solution.py:273
  47.0 5.8 %collective-permute-start.12 = (bf16[80,256]{1,0:T(8,128)(2,1)S(1)}, bf16[80,256]{1,0:T(8,128)(2,1)S(1)}, u32[]{:S(2)}, u32[]{:S(2)}) collective-permute-start(bf16[80,256]{1,0:T(8,128)(2,1)S(1)} %shard_map.70.first), channel_id=1, source_target_pairs={{0,12},{12,0},{4,8},{8,4},{1,13},{13,1},{5,9},{9,5},{2,14},{14,2},... | collective-permute-start | bytes 122888 | tf_op jit(solution)/shard_map/ppermute | solution.py:273
  48.3 4.5 %collective-permute-start.11 = (bf16[80,256]{1,0:T(8,128)(2,1)S(1)}, bf16[80,256]{1,0:T(8,128)(2,1)S(1)}, u32[]{:S(2)}, u32[]{:S(2)}) collective-permute-start(bf16[80,256]{1,0:T(8,128)(2,1)S(1)} %shard_map.70.first), channel_id=1, source_target_pairs={{0,4},{4,0},{8,12},{12,8},{1,5},{5,1},{9,13},{13,9},{2,6},{6,2},{1... | collective-permute-start | bytes 122888 | tf_op jit(solution)/shard_map/ppermute | solution.py:273

commit v5 on v4

--- a/solution.py
+++ b/solution.py
@@ -91,20 +91,19 @@
     return lax.dot_general(a, b, (((1,), (1,)), ((), ())), preferred_element_type=jnp.float32)
 
 
-LATE = 2**23
 CHEAP = pl.CostEstimate(flops=1, bytes_accessed=1, transcendentals=0)
 HERE = pl.BlockSpec(memory_space=pltpu.VMEM)
 TILE = 256
 
 
-def call(kernel, outs, *operands, scratch=(), cost=CHEAP):
+def call(kernel, outs, *operands, scratch=()):
     return pl.pallas_call(
         kernel,
         in_specs=[HERE] * len(operands),
         out_specs=[HERE] * len(outs),
         out_shape=list(outs),
         scratch_shapes=list(scratch),
-        cost_estimate=cost,
+        cost_estimate=CHEAP,
         compiler_params=pltpu.CompilerParams(vmem_limit_bytes=8 * 2**20),
     )(*operands)
 
@@ -227,7 +226,7 @@
     out1[...] = second[...]
 
 
-def delta_kernel(low_rank, owner0, owner1, owner2, owner3, up0, up1, up2, up3, mine, out):
+def delta_kernel(low_rank, owner0, owner1, owner2, owner3, up0, up1, up2, up3, mine, got, out):
     t, q = lax.axis_index("tenant"), lax.axis_index("tensor")
     f32, bf16 = jnp.float32, jnp.bfloat16
     wide = up0.shape[0]
@@ -241,24 +240,19 @@
     column = jnp.sum(jnp.where(i == j, tags[:1], 0.0), axis=1, keepdims=True)
     slots = jnp.broadcast_to(column, (rows, wide)).astype(jnp.int32)
     lane = lanes(slots.shape, low_rank)
-    chosen = jnp.zeros(slots.shape, f32)
-    for step, owner in enumerate(owners):
-        chosen = chosen + jnp.where(slots - (t ^ step) * ten_dev == lane, owner[:rows], 0.0)
-    i = lax.broadcasted_iota(jnp.int32, (wide, wide), 0)
-    j = lax.broadcasted_iota(jnp.int32, (wide, wide), 1)
-    same = jnp.zeros((wide, wide), f32)
-    for shift in range(-wide + low_rank, wide, low_rank):
-        same = jnp.where(i - j == shift, 1.0, same)
-    spread = dot(chosen.astype(bf16), same.astype(bf16))
+    kept = [
+        jnp.where(slots - (t ^ step) * ten_dev == lane, owner[:rows], 0.0)
+        for step, owner in enumerate(owners)
+    ]
     terms = []
     for step, up in zip((0, 2, 1, 3), (up0, up1, up2, up3)):
-        here = slots - (q ^ step) * ten_dev == lane
-        terms.append((jnp.where(here, spread, 0.0).astype(bf16), up))
+        mixed = sum(jnp.where((t ^ at) == (q ^ step), value, 0.0) for at, value in enumerate(kept))
+        terms.append((mixed.astype(bf16), up))
     for part in tiles(mine.shape[1]):
-        total = mine[:, part]
+        total = mine[:, part] + got[:, part].astype(f32)
         for rows, up in terms:
             total = total + dot(rows, up[:, part])
-        out[:, part] = total
+        out[:, part] = total.astype(out.dtype)
 
 
 def on_device_4x4(hidden_states, tenant_ids, owner_map, down_weight, adapter_down, adapter_up):
@@ -338,10 +332,10 @@
     owners = [held, outer_pairs(reduced), two, opposite(reduced)]
     (total,) = call(
         functools.partial(delta_kernel, low_rank),
-        [out(tall)],
-        *owners, up0, up1, up2, cores(up_held), mine,
-    )
-    return (total + from_chip.astype(f32)).astype(bf16)
+        [out(tall, bf16)],
+        *owners, up0, up1, up2, cores(up_held), mine, from_chip,
+    )
+    return total
 
 
 def solution(mesh):

time: 55 us -> 54.8 us (level)
  other arithmetic: 0.85 us -> 0.09 us
  Pallas kernels: 10.7 us -> 11.3 us
    convert_element_type x1 -> x0, other arithmetic: 0.77 us -> none  [on_device_4x4(): return (total + from_chip.astype(f32)).astype(bf16)]
    pallas_call x11, Pallas kernels: 10.7 us -> 11.3 us  [call(): pl.pallas_call(kernel, in_specs=[HERE] * len(operands), out_specs=[HERE]...]
  transfers between devices with their start and end apart: 17 -> 17, of which waited for: 6 -> 6; matrix products, arithmetic and copies ran while one was open for 2% -> 2% of each run, Pallas kernels for 20% -> 18%
where the time goes in v5:
time: 54.8 us; the launch traced here: 54.6 us
  starting transfers between devices  19.1 us (35%)
  waiting for transfers between devices  15.1 us (28%)
  Pallas kernels  11.3 us (21%)
  local copies, waits for them, and re-layouts  8.79 us (16%)
    ppermute x17, starting transfers between devices, along(): return lambda value: lax.ppermute(value, name, pairs)  19.1 us
    ppermute x17, waiting for transfers between devices, along(): return lambda value: lax.ppermute(value, name, pairs)  15.1 us
    pallas_call x11, Pallas kernels, call(): pl.pallas_call(kernel, in_specs=[HERE] * len(operands), out_specs=[HERE]...  11.3 us
    unnamed x16, local copies, waits for them, and re-layouts  7.71 us
  transfers between devices with their start and end apart: 17, of which 6 were waited for; matrix products, arithmetic and copies ran while one was open for 2% of the time, Pallas kernels for 18%

profile of v5, /device:TPU:0, one launch (start us, length us, event | category | flops | bytes accessed | tf_op | source)
XLA Modules:
  0.0 54.6 jit_solution(17792305766727635513)
XLA Ops:
  0.0 0.0 copy-start.6
  0.0 0.0 copy-start.7
  0.0 3.0 %collective-permute-start.3 = (bf16[64,3584]{1,0:T(8,128)(2,1)}, bf16[64,3584]{1,0:T(8,128)(2,1)S(1)}, u32[]{:S(2)}, u32[]{:S(2)}) collective-permute-start(bf16[64,3584]{1,0:T(8,128)(2,1)} %x.3), channel_id=1, source_target_pairs={{0,4},{4,0},{8,12},{12,8},{1,5},{5,1},{9,13},{13,9},{2,6},{6,2},{1... | collective-permute-start | bytes 1376264 | tf_op jit(solution)/shard_map/ppermute | solution.py:267
  3.0 1.1 %fusion = (bf16[64,1792]{1,0:T(8,128)(2,1)S(1)}, bf16[64,1792]{1,0:T(8,128)(2,1)S(1)}) fusion(bf16[64,3584]{1,0:T(8,128)(2,1)} %x.3), kind=kLoop, calls=%fused_computation.2 | loop fusion | bytes 917504 | tf_op jit(solution)/shard_map/slice | solution.py:282
  4.1 2.7 %collective-permute-start.4 = (bf16[64,1792]{1,0:T(8,128)(2,1)S(1)}, bf16[64,1792]{1,0:T(8,128)(2,1)S(1)}, u32[]{:S(2)}, u32[]{:S(2)}) collective-permute-start(bf16[64,1792]{1,0:T(8,128)(2,1)S(1)} %get-tuple-element.45), channel_id=1, source_target_pairs={{0,8},{8,0},{4,12},{12,4},{1,9},{9,1},{5,13},{13,5},{2,10},{10,2},... | collective-permute-start | bytes 688136 | tf_op jit(solution)/shard_map/ppermute | solution.py:267
  6.8 0.3 collective-permute-start
  7.1 1.5 %collective-permute-start.13 = (bf16[256,2048]{1,0:T(8,128)(2,1)}, bf16[256,2048]{1,0:T(8,128)(2,1)S(1)}, u32[]{:S(2)}, u32[]{:S(2)}) collective-permute-start(bf16[256,2048]{1,0:T(8,128)(2,1)} %bitcast.8), channel_id=1, source_target_pairs={{0,2},{2,0},{1,3},{3,1},{4,6},{6,4},{5,7},{7,5},{8,10},{10,8},{9,1... | collective-permute-start | bytes 3145736 | tf_op jit(solution)/shard_map/ppermute | solution.py:267
  8.6 0.0 copy-start
  8.6 5.2 %copy-done = bf16[3584,2048]{1,0:T(8,128)(2,1)S(1)} copy-done((bf16[3584,2048]{1,0:T(8,128)(2,1)S(1)}, bf16[3584,2048]{1,0:T(8,128)(2,1)}, u32[]{:S(2)}) %copy-start) | copy-done | bytes 14680088
  13.8 0.0 copy-start.2
  13.8 1.5 %copy-done.2 = bf16[4,3584,64]{1,2,0:T(8,128)(2,1)S(1)} copy-done((bf16[4,3584,64]{1,2,0:T(8,128)(2,1)S(1)}, bf16[4,3584,64]{1,2,0:T(8,128)(2,1)}, u32[]{:S(2)}) %copy-start.2) | copy-done | bytes 1835032
  15.3 0.0 copy-start.4
  15.3 1.0 %copy-done.4 = bf16[64,3584]{1,0:T(8,128)(2,1)S(1)} copy-done((bf16[64,3584]{1,0:T(8,128)(2,1)S(1)}, bf16[64,3584]{1,0:T(8,128)(2,1)}, u32[]{:S(2)}) %copy-start.4) | copy-done | bytes 458776
  16.3 0.0 copy-start.1
  16.3 0.0 copy-start.3
  16.3 3.2 %shard_map.64 = (f32[64,2048]{1,0:T(8,128)S(1)}, f32[64,256]{1,0:T(8,128)S(1)}, bf16[64,1792]{1,0:T(8,128)(2,1)S(1)}, bf16[64,1792]{1,0:T(8,128)(2,1)S(1)}) custom-call(bf16[64,3584]{1,0:T(8,128)(2,1)S(1)} %copy-done.4, bf16[3584,2048]{1,0:T(8,128)(2,1)S(1)} %copy-done, bf16[256,3584]{1,0:T(8,128)(2,1)S(1)} %bitcast.4), custom_call_target="tpu_custom_call" | custom-call | flops 1 | bytes 1 | tf_op jit(solution)/shard_map/pallas_call | solution.py:100
  19.5 0.8 %collective-permute-start.6 = (bf16[64,1792]{1,0:T(8,128)(2,1)S(1)}, bf16[64,1792]{1,0:T(8,128)(2,1)S(1)}, u32[]{:S(2)}, u32[]{:S(2)}) collective-permute-start(bf16[64,1792]{1,0:T(8,128)(2,1)S(1)} %get-tuple-element.28), channel_id=1, source_target_pairs={{4,8},{8,4},{5,9},{9,5},{6,10},{10,6},{7,11},{11,7},{20,24},{24,20... | collective-permute-start | bytes 688136 | tf_op jit(solution)/shard_map/ppermute | solution.py:267
  20.3 0.0 collective-permute-done.4.two_a
  20.3 1.4 %collective-permute-start.5 = (bf16[64,1792]{1,0:T(8,128)(2,1)S(1)}, bf16[64,1792]{1,0:T(8,128)(2,1)S(1)}, u32[]{:S(2)}, u32[]{:S(2)}) collective-permute-start(bf16[64,1792]{1,0:T(8,128)(2,1)S(1)} %collective-permute-done.4.two_a), channel_id=1, source_target_pairs={{8,12},{4,0},{9,13},{5,1},{10,14},{6,2},{11,15},{7,3},{24,28},{20,... | collective-permute-start | bytes 688136 | tf_op jit(solution)/shard_map/ppermute | solution.py:267
  21.7 6.2 %collective-permute-done.two_b = bf16[64,1792]{1,0:T(8,128)(2,1)S(1)} collective-permute-done((bf16[64,1792]{1,0:T(8,128)(2,1)S(1)}, bf16[64,1792]{1,0:T(8,128)(2,1)S(1)}, u32[]{:S(2)}, u32[]{:S(2)}) %collective-permute-start) | collective-permute-done | bytes 229408 | tf_op jit(solution)/shard_map/ppermute | solution.py:267
  27.9 0.7 %collective-permute-start.2 = (bf16[64,1792]{1,0:T(8,128)(2,1)S(1)}, bf16[64,1792]{1,0:T(8,128)(2,1)S(1)}, u32[]{:S(2)}, u32[]{:S(2)}) collective-permute-start(bf16[64,1792]{1,0:T(8,128)(2,1)S(1)} %get-tuple-element.25), channel_id=1, source_target_pairs={{4,8},{8,4},{5,9},{9,5},{6,10},{10,6},{7,11},{11,7},{20,24},{24,20... | collective-permute-start | bytes 688136 | tf_op jit(solution)/shard_map/ppermute | solution.py:267
  28.6 0.0 collective-permute-done.3.pair
  28.6 1.3 %collective-permute-start.1 = (bf16[64,1792]{1,0:T(8,128)(2,1)S(1)}, bf16[64,1792]{1,0:T(8,128)(2,1)S(1)}, u32[]{:S(2)}, u32[]{:S(2)}) collective-permute-start(bf16[64,1792]{1,0:T(8,128)(2,1)S(1)} %collective-permute-done.two_b), channel_id=1, source_target_pairs={{8,12},{4,0},{9,13},{5,1},{10,14},{6,2},{11,15},{7,3},{24,28},{20,... | collective-permute-start | bytes 688136 | tf_op jit(solution)/shard_map/ppermute | solution.py:267
  29.9 0.0 copy-done.6
  29.9 0.0 copy-done.7
  29.9 0.1 select_reduce_fusion
  30.0 0.0 copy-done.1
  30.0 0.0 copy-done.3
  30.0 2.6 %shard_map.65 = (f32[64,2048]{1,0:T(8,128)S(1)}, f32[64,2048]{1,0:T(8,128)S(1)}, f32[128,256]{1,0:T(8,128)S(1)}) custom-call(bf16[64,3584]{1,0:T(8,128)(2,1)S(1)} %collective-permute-done.3.pair, bf16[64,1792]{1,0:T(8,128)(2,1)S(1)} %collective-permute-done.4.two_a, bf16[64,1792]{1,0:T(8,128)(2,1)S(1)} %collective-permute-done.two_b, ...), custom_call_target="tpu_custom_call" | custom-call | flops 1 | bytes 1 | tf_op jit(solution)/shard_map/pallas_call | solution.py:100
  32.6 0.0 collective-permute-done.6.inner
  32.6 0.1 collective-permute-done.5.end
  32.8 1.7 %shard_map.66 = (f32[64,2048]{1,0:T(8,128)S(1)}, f32[128,256]{1,0:T(8,128)S(1)}) custom-call(bf16[64,1792]{1,0:T(8,128)(2,1)S(1)} %collective-permute-done.5.end, bf16[64,1792]{1,0:T(8,128)(2,1)S(1)} %collective-permute-done.6.inner, bf16[3584,2048]{1,0:T(8,128)(2,1)S(1)} %copy-done.1, bf16[256,3584]{1,0:T(8,128)(2,1)S(1)} %bitcast.6, ...), custom_call_target="tpu_custom_call" | custom-call | flops 1 | bytes 1 | tf_op jit(solution)/shard_map/pallas_call | solution.py:100
  34.4 0.0 copy-start.5
  34.4 0.0 collective-permute-done.2.inner
  34.4 2.1 %collective-permute-done.1.end = bf16[64,1792]{1,0:T(8,128)(2,1)S(1)} collective-permute-done((bf16[64,1792]{1,0:T(8,128)(2,1)S(1)}, bf16[64,1792]{1,0:T(8,128)(2,1)S(1)}, u32[]{:S(2)}, u32[]{:S(2)}) %collective-permute-start.1) | collective-permute-done | bytes 229408 | tf_op jit(solution)/shard_map/ppermute | solution.py:267
  36.5 0.4 shard_map.67
  37.0 0.1 collective-permute-start.7
  37.0 1.4 %shard_map.68.base3 = f32[64,2048]{1,0:T(8,128)S(1)} custom-call(bf16[64,1792]{1,0:T(8,128)(2,1)S(1)} %collective-permute-done.1.end, bf16[64,1792]{1,0:T(8,128)(2,1)S(1)} %collective-permute-done.2.inner, bf16[3584,2048]{1,0:T(8,128)(2,1)S(1)} %copy-done.1, f32[64,2048]{1,0:T(8,128)S(1)} %get-tuple-element.33.early, f32[128,256]{1,0:T(8,128)S(1)} %get-tuple-element.32.low_give), custom_call_target="tpu_custom_call" | custom-call | flops 1 | bytes 1 | tf_op jit(solution)/shard_map/pallas_call | solution.py:100
  38.4 0.0 collective-permute-done.7.got
  38.5 0.2 shard_map.72
  38.7 0.6 %collective-permute-start.14 = (bf16[128,2048]{1,0:T(8,128)(2,1)S(1)}, bf16[128,2048]{1,0:T(8,128)(2,1)S(1)}, u32[]{:S(2)}, u32[]{:S(2)}) collective-permute-start(bf16[128,2048]{1,0:T(8,128)(2,1)S(1)} %get-tuple-element.41), channel_id=1, source_target_pairs={{0,1},{1,0},{2,3},{3,2},{4,5},{5,4},{6,7},{7,6},{8,9},{9,8},{10,11... | collective-permute-start | bytes 1572872 | tf_op jit(solution)/shard_map/ppermute | solution.py:267
  39.2 0.0 copy-done.5
  39.2 0.1 collective-permute-start.9
  39.3 1.5 %collective-permute-start.8 = (bf16[64,256]{1,0:T(8,128)(2,1)S(1)}, bf16[64,256]{1,0:T(8,128)(2,1)S(1)}, u32[]{:S(2)}, u32[]{:S(2)}) collective-permute-start(bf16[64,256]{1,0:T(8,128)(2,1)S(1)} %get-tuple-element.35.low_other), channel_id=1, source_target_pairs={{0,2},{2,0},{1,3},{3,1},{4,6},{6,4},{5,7},{7,5},{8,10},{10,8},{9,1... | collective-permute-start | bytes 98312 | tf_op jit(solution)/shard_map/ppermute | solution.py:267
  40.8 2.4 %collective-permute-done.8.got.low_got = bf16[64,256]{1,0:T(8,128)(2,1)S(1)} collective-permute-done((bf16[64,256]{1,0:T(8,128)(2,1)S(1)}, bf16[64,256]{1,0:T(8,128)(2,1)S(1)}, u32[]{:S(2)}, u32[]{:S(2)}) %collective-permute-start.8) | collective-permute-done | bytes 32800 | tf_op jit(solution)/shard_map/ppermute | solution.py:267
  43.2 0.0 collective-permute-done.13.up.up1
  43.2 0.0 collective-permute-done.14.got
  43.2 0.2 shard_map.73
  43.4 0.1 collective-permute-start.15
  43.5 1.6 %collective-permute-start.16 = (bf16[64,2048]{1,0:T(8,128)(2,1)S(1)}, bf16[64,2048]{1,0:T(8,128)(2,1)S(1)}, u32[]{:S(2)}, u32[]{:S(2)}) collective-permute-start(bf16[64,2048]{1,0:T(8,128)(2,1)S(1)} %get-tuple-element.44), channel_id=1, source_target_pairs={{0,2},{2,0},{1,3},{3,1},{4,6},{6,4},{5,7},{7,5},{8,10},{10,8},{9,1... | collective-permute-start | bytes 786440 | tf_op jit(solution)/shard_map/ppermute | solution.py:267
  45.0 0.0 collective-permute-done.9.up2
  45.1 2.0 %collective-permute-start.10 = (bf16[80,256]{1,0:T(8,128)(2,1)S(1)}, bf16[80,256]{1,0:T(8,128)(2,1)S(1)}, u32[]{:S(2)}, u32[]{:S(2)}) collective-permute-start(bf16[80,256]{1,0:T(8,128)(2,1)S(1)} %shard_map.70.first), channel_id=1, source_target_pairs={{0,8},{8,0},{4,12},{12,4},{1,9},{9,1},{5,13},{13,5},{2,10},{10,2},... | collective-permute-start | bytes 122888 | tf_op jit(solution)/shard_map/ppermute | solution.py:267
  47.0 1.3 %collective-permute-start.12 = (bf16[80,256]{1,0:T(8,128)(2,1)S(1)}, bf16[80,256]{1,0:T(8,128)(2,1)S(1)}, u32[]{:S(2)}, u32[]{:S(2)}) collective-permute-start(bf16[80,256]{1,0:T(8,128)(2,1)S(1)} %shard_map.70.first), channel_id=1, source_target_pairs={{0,12},{12,0},{4,8},{8,4},{1,13},{13,1},{5,9},{9,5},{2,14},{14,2},... | collective-permute-start | bytes 122888 | tf_op jit(solution)/shard_map/ppermute | solution.py:267
  48.3 0.3 collective-permute-start.11
  48.6 2.0 %collective-permute-done.10.second = bf16[80,256]{1,0:T(8,128)(2,1)S(1)} collective-permute-done((bf16[80,256]{1,0:T(8,128)(2,1)S(1)}, bf16[80,256]{1,0:T(8,128)(2,1)S(1)}, u32[]{:S(2)}, u32[]{:S(2)}) %collective-permute-start.10) | collective-permute-done | bytes 40992 | tf_op jit(solution)/shard_map/ppermute | solution.py:267
  50.6 2.3 %collective-permute-done.12.owner3 = bf16[80,256]{1,0:T(8,128)(2,1)S(1)} collective-permute-done((bf16[80,256]{1,0:T(8,128)(2,1)S(1)}, bf16[80,256]{1,0:T(8,128)(2,1)S(1)}, u32[]{:S(2)}, u32[]{:S(2)}) %collective-permute-start.12) | collective-permute-done | bytes 40992 | tf_op jit(solution)/shard_map/ppermute | solution.py:267
  52.8 0.0 collective-permute-done.11.owner1
  52.9 0.0 collective-permute-done.16.got
  52.9 0.0 collective-permute-done.15.up3
  52.9 1.7 %shard_map.74 = bf16[64,2048]{1,0:T(8,128)(2,1)} custom-call(bf16[80,256]{1,0:T(8,128)(2,1)S(1)} %get-tuple-element.36.owner0, bf16[80,256]{1,0:T(8,128)(2,1)S(1)} %collective-permute-done.11.owner1, bf16[80,256]{1,0:T(8,128)(2,1)S(1)} %get-tuple-element.37.owner2, bf16[80,256]{1,0:T(8,128)(2,1)S(1)} %collective-permute-done.12.owner3, ...), custom_call_target="tpu_custom_call" | custom-call | flops 1 | bytes 1 | tf_op jit(solution)/shard_map/pallas_call | solution.py:100
  (5 shorter events, 0.1 us)
Async XLA Ops:
  0.0 29.9 %copy-start.6 = (s32[16]{0:T(128)S(1)}, s32[16]{0:T(128)}, u32[]{:S(2)}) copy-start(s32[16]{0:T(128)} %param.8) | copy-start | bytes 196
  0.0 29.9 %copy-start.7 = (s32[64]{0:T(128)S(1)}, s32[64]{0:T(128)}, u32[]{:S(2)}) copy-start(s32[64]{0:T(128)} %param.7) | copy-start | bytes 772
  0.0 28.6 %collective-permute-start.3 = (bf16[64,3584]{1,0:T(8,128)(2,1)}, bf16[64,3584]{1,0:T(8,128)(2,1)S(1)}, u32[]{:S(2)}, u32[]{:S(2)}) collective-permute-start(bf16[64,3584]{1,0:T(8,128)(2,1)} %x.3), channel_id=1, source_target_pairs={{0,4},{4,0},{8,12},{12,8},{1,5},{5,1},{9,13},{13,9},{2,6},{6,2},{1... | collective-permute-start | bytes 1376264 | tf_op jit(solution)/shard_map/ppermute | solution.py:267
  4.1 16.2 %collective-permute-start.4 = (bf16[64,1792]{1,0:T(8,128)(2,1)S(1)}, bf16[64,1792]{1,0:T(8,128)(2,1)S(1)}, u32[]{:S(2)}, u32[]{:S(2)}) collective-permute-start(bf16[64,1792]{1,0:T(8,128)(2,1)S(1)} %get-tuple-element.45), channel_id=1, source_target_pairs={{0,8},{8,0},{4,12},{12,4},{1,9},{9,1},{5,13},{13,5},{2,10},{10,2},... | collective-permute-start | bytes 688136 | tf_op jit(solution)/shard_map/ppermute | solution.py:267
  6.8 21.2 %collective-permute-start = (bf16[64,1792]{1,0:T(8,128)(2,1)S(1)}, bf16[64,1792]{1,0:T(8,128)(2,1)S(1)}, u32[]{:S(2)}, u32[]{:S(2)}) collective-permute-start(bf16[64,1792]{1,0:T(8,128)(2,1)S(1)} %get-tuple-element.46), channel_id=1, source_target_pairs={{0,8},{8,0},{4,12},{12,4},{1,9},{9,1},{5,13},{13,5},{2,10},{10,2},... | collective-permute-start | bytes 688136 | tf_op jit(solution)/shard_map/ppermute | solution.py:267
  7.1 36.1 %collective-permute-start.13 = (bf16[256,2048]{1,0:T(8,128)(2,1)}, bf16[256,2048]{1,0:T(8,128)(2,1)S(1)}, u32[]{:S(2)}, u32[]{:S(2)}) collective-permute-start(bf16[256,2048]{1,0:T(8,128)(2,1)} %bitcast.8), channel_id=1, source_target_pairs={{0,2},{2,0},{1,3},{3,1},{4,6},{6,4},{5,7},{7,5},{8,10},{10,8},{9,1... | collective-permute-start | bytes 3145736 | tf_op jit(solution)/shard_map/ppermute | solution.py:267
  8.6 5.2 %copy-start = (bf16[3584,2048]{1,0:T(8,128)(2,1)S(1)}, bf16[3584,2048]{1,0:T(8,128)(2,1)}, u32[]{:S(2)}) copy-start(bf16[3584,2048]{1,0:T(8,128)(2,1)} %w.7) | copy-start | bytes 44040196
  13.8 1.5 %copy-start.2 = (bf16[4,3584,64]{1,2,0:T(8,128)(2,1)S(1)}, bf16[4,3584,64]{1,2,0:T(8,128)(2,1)}, u32[]{:S(2)}) copy-start(bf16[4,3584,64]{1,2,0:T(8,128)(2,1)} %param.10) | copy-start | bytes 5505028
  15.3 1.0 %copy-start.4 = (bf16[64,3584]{1,0:T(8,128)(2,1)S(1)}, bf16[64,3584]{1,0:T(8,128)(2,1)}, u32[]{:S(2)}) copy-start(bf16[64,3584]{1,0:T(8,128)(2,1)} %x.3) | copy-start | bytes 1376260
  16.3 13.7 %copy-start.1 = (bf16[3584,2048]{1,0:T(8,128)(2,1)S(1)}, bf16[3584,2048]{1,0:T(8,128)(2,1)}, u32[]{:S(2)}) copy-start(bf16[3584,2048]{1,0:T(8,128)(2,1)} %w.7) | copy-start | bytes 44040196
  16.3 13.7 %copy-start.3 = (bf16[4,3584,64]{1,2,0:T(8,128)(2,1)S(1)}, bf16[4,3584,64]{1,2,0:T(8,128)(2,1)}, u32[]{:S(2)}) copy-start(bf16[4,3584,64]{1,2,0:T(8,128)(2,1)} %param.10) | copy-start | bytes 5505028
  19.5 13.1 %collective-permute-start.6 = (bf16[64,1792]{1,0:T(8,128)(2,1)S(1)}, bf16[64,1792]{1,0:T(8,128)(2,1)S(1)}, u32[]{:S(2)}, u32[]{:S(2)}) collective-permute-start(bf16[64,1792]{1,0:T(8,128)(2,1)S(1)} %get-tuple-element.28), channel_id=1, source_target_pairs={{4,8},{8,4},{5,9},{9,5},{6,10},{10,6},{7,11},{11,7},{20,24},{24,20... | collective-permute-start | bytes 688136 | tf_op jit(solution)/shard_map/ppermute | solution.py:267
  20.3 12.5 %collective-permute-start.5 = (bf16[64,1792]{1,0:T(8,128)(2,1)S(1)}, bf16[64,1792]{1,0:T(8,128)(2,1)S(1)}, u32[]{:S(2)}, u32[]{:S(2)}) collective-permute-start(bf16[64,1792]{1,0:T(8,128)(2,1)S(1)} %collective-permute-done.4.two_a), channel_id=1, source_target_pairs={{8,12},{4,0},{9,13},{5,1},{10,14},{6,2},{11,15},{7,3},{24,28},{20,... | collective-permute-start | bytes 688136 | tf_op jit(solution)/shard_map/ppermute | solution.py:267
  27.9 6.5 %collective-permute-start.2 = (bf16[64,1792]{1,0:T(8,128)(2,1)S(1)}, bf16[64,1792]{1,0:T(8,128)(2,1)S(1)}, u32[]{:S(2)}, u32[]{:S(2)}) collective-permute-start(bf16[64,1792]{1,0:T(8,128)(2,1)S(1)} %get-tuple-element.25), channel_id=1, source_target_pairs={{4,8},{8,4},{5,9},{9,5},{6,10},{10,6},{7,11},{11,7},{20,24},{24,20... | collective-permute-start | bytes 688136 | tf_op jit(solution)/shard_map/ppermute | solution.py:267
  28.6 7.9 %collective-permute-start.1 = (bf16[64,1792]{1,0:T(8,128)(2,1)S(1)}, bf16[64,1792]{1,0:T(8,128)(2,1)S(1)}, u32[]{:S(2)}, u32[]{:S(2)}) collective-permute-start(bf16[64,1792]{1,0:T(8,128)(2,1)S(1)} %collective-permute-done.two_b), channel_id=1, source_target_pairs={{8,12},{4,0},{9,13},{5,1},{10,14},{6,2},{11,15},{7,3},{24,28},{20,... | collective-permute-start | bytes 688136 | tf_op jit(solution)/shard_map/ppermute | solution.py:267
  34.4 4.8 %copy-start.5 = (bf16[4,64,2048]{2,1,0:T(8,128)(2,1)S(1)}, bf16[4,64,2048]{2,1,0:T(8,128)(2,1)}, u32[]{:S(2)}) copy-start(bf16[4,64,2048]{2,1,0:T(8,128)(2,1)} %param.11) | copy-start | bytes 3145732
  37.0 1.5 %collective-permute-start.7 = (f32[128,256]{1,0:T(8,128)S(1)}, f32[128,256]{1,0:T(8,128)S(1)}, u32[]{:S(2)}, u32[]{:S(2)}) collective-permute-start(f32[128,256]{1,0:T(8,128)S(1)} %get-tuple-element.32.low_give), channel_id=1, source_target_pairs={{0,1},{1,0},{2,3},{3,2},{4,5},{5,4},{6,7},{7,6},{8,9},{9,8},{10,11... | collective-permute-start | bytes 393224 | tf_op jit(solution)/shard_map/ppermute | solution.py:267
  38.7 4.6 %collective-permute-start.14 = (bf16[128,2048]{1,0:T(8,128)(2,1)S(1)}, bf16[128,2048]{1,0:T(8,128)(2,1)S(1)}, u32[]{:S(2)}, u32[]{:S(2)}) collective-permute-start(bf16[128,2048]{1,0:T(8,128)(2,1)S(1)} %get-tuple-element.41), channel_id=1, source_target_pairs={{0,1},{1,0},{2,3},{3,2},{4,5},{5,4},{6,7},{7,6},{8,9},{9,8},{10,11... | collective-permute-start | bytes 1572872 | tf_op jit(solution)/shard_map/ppermute | solution.py:267
  39.2 5.8 %collective-permute-start.9 = (bf16[256,2048]{1,0:T(8,128)(2,1)S(1)}, bf16[256,2048]{1,0:T(8,128)(2,1)S(1)}, u32[]{:S(2)}, u32[]{:S(2)}) collective-permute-start(bf16[256,2048]{1,0:T(8,128)(2,1)S(1)} %bitcast.9), channel_id=1, source_target_pairs={{0,1},{1,0},{2,3},{3,2},{4,5},{5,4},{6,7},{7,6},{8,9},{9,8},{10,11... | collective-permute-start | bytes 3145736 | tf_op jit(solution)/shard_map/ppermute | solution.py:267
  39.3 3.9 %collective-permute-start.8 = (bf16[64,256]{1,0:T(8,128)(2,1)S(1)}, bf16[64,256]{1,0:T(8,128)(2,1)S(1)}, u32[]{:S(2)}, u32[]{:S(2)}) collective-permute-start(bf16[64,256]{1,0:T(8,128)(2,1)S(1)} %get-tuple-element.35.low_other), channel_id=1, source_target_pairs={{0,2},{2,0},{1,3},{3,1},{4,6},{6,4},{5,7},{7,5},{8,10},{10,8},{9,1... | collective-permute-start | bytes 98312 | tf_op jit(solution)/shard_map/ppermute | solution.py:267
  43.4 9.4 %collective-permute-start.15 = (bf16[256,2048]{1,0:T(8,128)(2,1)S(1)}, bf16[256,2048]{1,0:T(8,128)(2,1)S(1)}, u32[]{:S(2)}, u32[]{:S(2)}) collective-permute-start(bf16[256,2048]{1,0:T(8,128)(2,1)S(1)} %get-tuple-element.42), channel_id=1, source_target_pairs={{0,1},{1,0},{2,3},{3,2},{4,5},{5,4},{6,7},{7,6},{8,9},{9,8},{10,11... | collective-permute-start | bytes 3145736 | tf_op jit(solution)/shard_map/ppermute | solution.py:267
  43.5 9.4 %collective-permute-start.16 = (bf16[64,2048]{1,0:T(8,128)(2,1)S(1)}, bf16[64,2048]{1,0:T(8,128)(2,1)S(1)}, u32[]{:S(2)}, u32[]{:S(2)}) collective-permute-start(bf16[64,2048]{1,0:T(8,128)(2,1)S(1)} %get-tuple-element.44), channel_id=1, source_target_pairs={{0,2},{2,0},{1,3},{3,1},{4,6},{6,4},{5,7},{7,5},{8,10},{10,8},{9,1... | collective-permute-start | bytes 786440 | tf_op jit(solution)/shard_map/ppermute | solution.py:267
  45.1 5.5 %collective-permute-start.10 = (bf16[80,256]{1,0:T(8,128)(2,1)S(1)}, bf16[80,256]{1,0:T(8,128)(2,1)S(1)}, u32[]{:S(2)}, u32[]{:S(2)}) collective-permute-start(bf16[80,256]{1,0:T(8,128)(2,1)S(1)} %shard_map.70.first), channel_id=1, source_target_pairs={{0,8},{8,0},{4,12},{12,4},{1,9},{9,1},{5,13},{13,5},{2,10},{10,2},... | collective-permute-start | bytes 122888 | tf_op jit(solution)/shard_map/ppermute | solution.py:267
  47.0 5.8 %collective-permute-start.12 = (bf16[80,256]{1,0:T(8,128)(2,1)S(1)}, bf16[80,256]{1,0:T(8,128)(2,1)S(1)}, u32[]{:S(2)}, u32[]{:S(2)}) collective-permute-start(bf16[80,256]{1,0:T(8,128)(2,1)S(1)} %shard_map.70.first), channel_id=1, source_target_pairs={{0,12},{12,0},{4,8},{8,4},{1,13},{13,1},{5,9},{9,5},{2,14},{14,2},... | collective-permute-start | bytes 122888 | tf_op jit(solution)/shard_map/ppermute | solution.py:267
  48.3 4.5 %collective-permute-start.11 = (bf16[80,256]{1,0:T(8,128)(2,1)S(1)}, bf16[80,256]{1,0:T(8,128)(2,1)S(1)}, u32[]{:S(2)}, u32[]{:S(2)}) collective-permute-start(bf16[80,256]{1,0:T(8,128)(2,1)S(1)} %shard_map.70.first), channel_id=1, source_target_pairs={{0,4},{4,0},{8,12},{12,8},{1,5},{5,1},{9,13},{13,9},{2,6},{6,2},{1... | collective-permute-start | bytes 122888 | tf_op jit(solution)/shard_map/ppermute | solution.py:267

commit v6 on v5

--- a/solution.py
+++ b/solution.py
@@ -219,11 +219,6 @@
     rows = mine.shape[0]
     out[:rows] = (mine[...] + got[...].astype(jnp.float32)).astype(out.dtype)
     out[rows:] = slots[...].astype(jnp.float32).astype(out.dtype)
-
-
-def hold_kernel(first, second, out0, out1):
-    out0[...] = first[...]
-    out1[...] = second[...]
 
 
 def delta_kernel(low_rank, owner0, owner1, owner2, owner3, up0, up1, up2, up3, mine, got, out):
@@ -328,8 +323,7 @@
     up2 = cores(up0)
     shape = out((rows + 16, wide), bf16)
     (reduced,) = call(reduced_kernel, [shape], low_mine, low_from_chip, slots, up2)
-    held, two = call(hold_kernel, [shape] * 2, reduced, two_apart(reduced))
-    owners = [held, outer_pairs(reduced), two, opposite(reduced)]
+    owners = [reduced, outer_pairs(reduced), two_apart(reduced), opposite(reduced)]
     (total,) = call(
         functools.partial(delta_kernel, low_rank),
         [out(tall, bf16)],

time: 54.8 us -> 54.9 us (level)
  starting transfers between devices: 19.1 us -> 20 us
  waiting for transfers between devices: 15.1 us -> 14.3 us
    ppermute x17, starting transfers between devices: 19.1 us -> 20 us  [along(): return lambda value: lax.ppermute(value, name, pairs)]
    ppermute x17, waiting for transfers between devices: 15.1 us -> 14.3 us  [along(): return lambda value: lax.ppermute(value, name, pairs)]
    pallas_call x11 -> x10, Pallas kernels: 11.3 us -> 11.3 us  [call(): pl.pallas_call(kernel, in_specs=[HERE] * len(operands), out_specs=[HERE]...]
where the time goes in v6:
time: 54.9 us; the launch traced here: 54.7 us
  starting transfers between devices  20 us (36%)
  waiting for transfers between devices  14.3 us (26%)
  Pallas kernels  11.3 us (21%)
  local copies, waits for them, and re-layouts  8.79 us (16%)
    ppermute x17, starting transfers between devices, along(): return lambda value: lax.ppermute(value, name, pairs)  20 us
    ppermute x17, waiting for transfers between devices, along(): return lambda value: lax.ppermute(value, name, pairs)  14.3 us
    pallas_call x10, Pallas kernels, call(): pl.pallas_call(kernel, in_specs=[HERE] * len(operands), out_specs=[HERE]...  11.3 us
    unnamed x16, local copies, waits for them, and re-layouts  7.71 us
  transfers between devices with their start and end apart: 17, of which 6 were waited for; matrix products, arithmetic and copies ran while one was open for 2% of the time, Pallas kernels for 18%

profile of v6, /device:TPU:0, one launch (start us, length us, event | category | flops | bytes accessed | tf_op | source)
XLA Modules:
  0.0 54.7 jit_solution(7094207983929030421)
XLA Ops:
  0.0 0.0 copy-start.6
  0.0 0.0 copy-start.7
  0.0 3.0 %collective-permute-start.3 = (bf16[64,3584]{1,0:T(8,128)(2,1)}, bf16[64,3584]{1,0:T(8,128)(2,1)S(1)}, u32[]{:S(2)}, u32[]{:S(2)}) collective-permute-start(bf16[64,3584]{1,0:T(8,128)(2,1)} %x.3), channel_id=1, source_target_pairs={{0,4},{4,0},{8,12},{12,8},{1,5},{5,1},{9,13},{13,9},{2,6},{6,2},{1... | collective-permute-start | bytes 1376264 | tf_op jit(solution)/shard_map/ppermute | solution.py:262
  3.0 1.1 %fusion = (bf16[64,1792]{1,0:T(8,128)(2,1)S(1)}, bf16[64,1792]{1,0:T(8,128)(2,1)S(1)}) fusion(bf16[64,3584]{1,0:T(8,128)(2,1)} %x.3), kind=kLoop, calls=%fused_computation.2 | loop fusion | bytes 917504 | tf_op jit(solution)/shard_map/slice | solution.py:277
  4.1 2.7 %collective-permute-start.4 = (bf16[64,1792]{1,0:T(8,128)(2,1)S(1)}, bf16[64,1792]{1,0:T(8,128)(2,1)S(1)}, u32[]{:S(2)}, u32[]{:S(2)}) collective-permute-start(bf16[64,1792]{1,0:T(8,128)(2,1)S(1)} %get-tuple-element.41), channel_id=1, source_target_pairs={{0,8},{8,0},{4,12},{12,4},{1,9},{9,1},{5,13},{13,5},{2,10},{10,2},... | collective-permute-start | bytes 688136 | tf_op jit(solution)/shard_map/ppermute | solution.py:262
  6.8 0.3 collective-permute-start
  7.1 1.5 %collective-permute-start.13 = (bf16[256,2048]{1,0:T(8,128)(2,1)}, bf16[256,2048]{1,0:T(8,128)(2,1)S(1)}, u32[]{:S(2)}, u32[]{:S(2)}) collective-permute-start(bf16[256,2048]{1,0:T(8,128)(2,1)} %bitcast.8), channel_id=1, source_target_pairs={{0,2},{2,0},{1,3},{3,1},{4,6},{6,4},{5,7},{7,5},{8,10},{10,8},{9,1... | collective-permute-start | bytes 3145736 | tf_op jit(solution)/shard_map/ppermute | solution.py:262
  8.6 0.0 copy-start
  8.6 5.2 %copy-done = bf16[3584,2048]{1,0:T(8,128)(2,1)S(1)} copy-done((bf16[3584,2048]{1,0:T(8,128)(2,1)S(1)}, bf16[3584,2048]{1,0:T(8,128)(2,1)}, u32[]{:S(2)}) %copy-start) | copy-done | bytes 14680088
  13.8 0.0 copy-start.2
  13.8 1.5 %copy-done.2 = bf16[4,3584,64]{1,2,0:T(8,128)(2,1)S(1)} copy-done((bf16[4,3584,64]{1,2,0:T(8,128)(2,1)S(1)}, bf16[4,3584,64]{1,2,0:T(8,128)(2,1)}, u32[]{:S(2)}) %copy-start.2) | copy-done | bytes 1835032
  15.3 0.0 copy-start.4
  15.3 1.0 %copy-done.4 = bf16[64,3584]{1,0:T(8,128)(2,1)S(1)} copy-done((bf16[64,3584]{1,0:T(8,128)(2,1)S(1)}, bf16[64,3584]{1,0:T(8,128)(2,1)}, u32[]{:S(2)}) %copy-start.4) | copy-done | bytes 458776
  16.3 0.0 copy-start.1
  16.3 0.0 copy-start.3
  16.3 3.2 %shard_map.64 = (f32[64,2048]{1,0:T(8,128)S(1)}, f32[64,256]{1,0:T(8,128)S(1)}, bf16[64,1792]{1,0:T(8,128)(2,1)S(1)}, bf16[64,1792]{1,0:T(8,128)(2,1)S(1)}) custom-call(bf16[64,3584]{1,0:T(8,128)(2,1)S(1)} %copy-done.4, bf16[3584,2048]{1,0:T(8,128)(2,1)S(1)} %copy-done, bf16[256,3584]{1,0:T(8,128)(2,1)S(1)} %bitcast.4), custom_call_target="tpu_custom_call" | custom-call | flops 1 | bytes 1 | tf_op jit(solution)/shard_map/pallas_call | solution.py:100
  19.5 0.8 %collective-permute-start.6 = (bf16[64,1792]{1,0:T(8,128)(2,1)S(1)}, bf16[64,1792]{1,0:T(8,128)(2,1)S(1)}, u32[]{:S(2)}, u32[]{:S(2)}) collective-permute-start(bf16[64,1792]{1,0:T(8,128)(2,1)S(1)} %get-tuple-element.26), channel_id=1, source_target_pairs={{4,8},{8,4},{5,9},{9,5},{6,10},{10,6},{7,11},{11,7},{20,24},{24,20... | collective-permute-start | bytes 688136 | tf_op jit(solution)/shard_map/ppermute | solution.py:262
  20.3 0.0 collective-permute-done.4.two_a
  20.3 1.4 %collective-permute-start.5 = (bf16[64,1792]{1,0:T(8,128)(2,1)S(1)}, bf16[64,1792]{1,0:T(8,128)(2,1)S(1)}, u32[]{:S(2)}, u32[]{:S(2)}) collective-permute-start(bf16[64,1792]{1,0:T(8,128)(2,1)S(1)} %collective-permute-done.4.two_a), channel_id=1, source_target_pairs={{8,12},{4,0},{9,13},{5,1},{10,14},{6,2},{11,15},{7,3},{24,28},{20,... | collective-permute-start | bytes 688136 | tf_op jit(solution)/shard_map/ppermute | solution.py:262
  21.7 6.2 %collective-permute-done.two_b = bf16[64,1792]{1,0:T(8,128)(2,1)S(1)} collective-permute-done((bf16[64,1792]{1,0:T(8,128)(2,1)S(1)}, bf16[64,1792]{1,0:T(8,128)(2,1)S(1)}, u32[]{:S(2)}, u32[]{:S(2)}) %collective-permute-start) | collective-permute-done | bytes 229408 | tf_op jit(solution)/shard_map/ppermute | solution.py:262
  27.9 0.7 %collective-permute-start.2 = (bf16[64,1792]{1,0:T(8,128)(2,1)S(1)}, bf16[64,1792]{1,0:T(8,128)(2,1)S(1)}, u32[]{:S(2)}, u32[]{:S(2)}) collective-permute-start(bf16[64,1792]{1,0:T(8,128)(2,1)S(1)} %get-tuple-element.23), channel_id=1, source_target_pairs={{4,8},{8,4},{5,9},{9,5},{6,10},{10,6},{7,11},{11,7},{20,24},{24,20... | collective-permute-start | bytes 688136 | tf_op jit(solution)/shard_map/ppermute | solution.py:262
  28.6 0.0 collective-permute-done.3.pair
  28.6 1.3 %collective-permute-start.1 = (bf16[64,1792]{1,0:T(8,128)(2,1)S(1)}, bf16[64,1792]{1,0:T(8,128)(2,1)S(1)}, u32[]{:S(2)}, u32[]{:S(2)}) collective-permute-start(bf16[64,1792]{1,0:T(8,128)(2,1)S(1)} %collective-permute-done.two_b), channel_id=1, source_target_pairs={{8,12},{4,0},{9,13},{5,1},{10,14},{6,2},{11,15},{7,3},{24,28},{20,... | collective-permute-start | bytes 688136 | tf_op jit(solution)/shard_map/ppermute | solution.py:262
  29.9 0.0 copy-done.6
  29.9 0.0 copy-done.7
  29.9 0.1 select_reduce_fusion
  30.0 0.0 copy-done.1
  30.0 0.0 copy-done.3
  30.0 2.6 %shard_map.65 = (f32[64,2048]{1,0:T(8,128)S(1)}, f32[64,2048]{1,0:T(8,128)S(1)}, f32[128,256]{1,0:T(8,128)S(1)}) custom-call(bf16[64,3584]{1,0:T(8,128)(2,1)S(1)} %collective-permute-done.3.pair, bf16[64,1792]{1,0:T(8,128)(2,1)S(1)} %collective-permute-done.4.two_a, bf16[64,1792]{1,0:T(8,128)(2,1)S(1)} %collective-permute-done.two_b, ...), custom_call_target="tpu_custom_call" | custom-call | flops 1 | bytes 1 | tf_op jit(solution)/shard_map/pallas_call | solution.py:100
  32.6 0.0 collective-permute-done.6.inner
  32.6 0.1 collective-permute-done.5.end
  32.8 1.7 %shard_map.66 = (f32[64,2048]{1,0:T(8,128)S(1)}, f32[128,256]{1,0:T(8,128)S(1)}) custom-call(bf16[64,1792]{1,0:T(8,128)(2,1)S(1)} %collective-permute-done.5.end, bf16[64,1792]{1,0:T(8,128)(2,1)S(1)} %collective-permute-done.6.inner, bf16[3584,2048]{1,0:T(8,128)(2,1)S(1)} %copy-done.1, bf16[256,3584]{1,0:T(8,128)(2,1)S(1)} %bitcast.6, ...), custom_call_target="tpu_custom_call" | custom-call | flops 1 | bytes 1 | tf_op jit(solution)/shard_map/pallas_call | solution.py:100
  34.4 0.0 copy-start.5
  34.4 0.0 collective-permute-done.2.inner
  34.4 2.1 %collective-permute-done.1.end = bf16[64,1792]{1,0:T(8,128)(2,1)S(1)} collective-permute-done((bf16[64,1792]{1,0:T(8,128)(2,1)S(1)}, bf16[64,1792]{1,0:T(8,128)(2,1)S(1)}, u32[]{:S(2)}, u32[]{:S(2)}) %collective-permute-start.1) | collective-permute-done | bytes 229408 | tf_op jit(solution)/shard_map/ppermute | solution.py:262
  36.5 0.4 shard_map.67
  37.0 0.1 collective-permute-start.7
  37.0 1.4 %shard_map.68.base3 = f32[64,2048]{1,0:T(8,128)S(1)} custom-call(bf16[64,1792]{1,0:T(8,128)(2,1)S(1)} %collective-permute-done.1.end, bf16[64,1792]{1,0:T(8,128)(2,1)S(1)} %collective-permute-done.2.inner, bf16[3584,2048]{1,0:T(8,128)(2,1)S(1)} %copy-done.1, f32[64,2048]{1,0:T(8,128)S(1)} %get-tuple-element.31.early, f32[128,256]{1,0:T(8,128)S(1)} %get-tuple-element.30.low_give), custom_call_target="tpu_custom_call" | custom-call | flops 1 | bytes 1 | tf_op jit(solution)/shard_map/pallas_call | solution.py:100
  38.4 0.0 collective-permute-done.7.got
  38.5 0.2 shard_map.71
  38.6 0.6 %collective-permute-start.14 = (bf16[128,2048]{1,0:T(8,128)(2,1)S(1)}, bf16[128,2048]{1,0:T(8,128)(2,1)S(1)}, u32[]{:S(2)}, u32[]{:S(2)}) collective-permute-start(bf16[128,2048]{1,0:T(8,128)(2,1)S(1)} %get-tuple-element.37), channel_id=1, source_target_pairs={{0,1},{1,0},{2,3},{3,2},{4,5},{5,4},{6,7},{7,6},{8,9},{9,8},{10,11... | collective-permute-start | bytes 1572872 | tf_op jit(solution)/shard_map/ppermute | solution.py:262
  39.2 0.0 copy-done.5
  39.2 0.1 collective-permute-start.9
  39.3 1.5 %collective-permute-start.8 = (bf16[64,256]{1,0:T(8,128)(2,1)S(1)}, bf16[64,256]{1,0:T(8,128)(2,1)S(1)}, u32[]{:S(2)}, u32[]{:S(2)}) collective-permute-start(bf16[64,256]{1,0:T(8,128)(2,1)S(1)} %get-tuple-element.33.low_other), channel_id=1, source_target_pairs={{0,2},{2,0},{1,3},{3,1},{4,6},{6,4},{5,7},{7,5},{8,10},{10,8},{9,1... | collective-permute-start | bytes 98312 | tf_op jit(solution)/shard_map/ppermute | solution.py:262
  40.8 2.4 %collective-permute-done.8.got.low_got = bf16[64,256]{1,0:T(8,128)(2,1)S(1)} collective-permute-done((bf16[64,256]{1,0:T(8,128)(2,1)S(1)}, bf16[64,256]{1,0:T(8,128)(2,1)S(1)}, u32[]{:S(2)}, u32[]{:S(2)}) %collective-permute-start.8) | collective-permute-done | bytes 32800 | tf_op jit(solution)/shard_map/ppermute | solution.py:262
  43.2 0.0 collective-permute-done.13.up.up1
  43.2 0.0 collective-permute-done.14.got
  43.2 0.2 shard_map.72
  43.4 0.1 collective-permute-start.15
  43.5 1.6 %collective-permute-start.16 = (bf16[64,2048]{1,0:T(8,128)(2,1)S(1)}, bf16[64,2048]{1,0:T(8,128)(2,1)S(1)}, u32[]{:S(2)}, u32[]{:S(2)}) collective-permute-start(bf16[64,2048]{1,0:T(8,128)(2,1)S(1)} %get-tuple-element.40), channel_id=1, source_target_pairs={{0,2},{2,0},{1,3},{3,1},{4,6},{6,4},{5,7},{7,5},{8,10},{10,8},{9,1... | collective-permute-start | bytes 786440 | tf_op jit(solution)/shard_map/ppermute | solution.py:262
  45.0 0.0 collective-permute-done.9.up2
  45.1 3.0 %collective-permute-start.12 = (bf16[80,256]{1,0:T(8,128)(2,1)S(1)}, bf16[80,256]{1,0:T(8,128)(2,1)S(1)}, u32[]{:S(2)}, u32[]{:S(2)}) collective-permute-start(bf16[80,256]{1,0:T(8,128)(2,1)S(1)} %shard_map.70.owner0), channel_id=1, source_target_pairs={{0,12},{12,0},{4,8},{8,4},{1,13},{13,1},{5,9},{9,5},{2,14},{14,2},... | collective-permute-start | bytes 122888 | tf_op jit(solution)/shard_map/ppermute | solution.py:262
  48.0 0.0 collective-permute-start.11
  48.0 1.5 %collective-permute-start.10 = (bf16[80,256]{1,0:T(8,128)(2,1)S(1)}, bf16[80,256]{1,0:T(8,128)(2,1)S(1)}, u32[]{:S(2)}, u32[]{:S(2)}) collective-permute-start(bf16[80,256]{1,0:T(8,128)(2,1)S(1)} %shard_map.70.owner0), channel_id=1, source_target_pairs={{0,4},{4,0},{8,12},{12,8},{1,5},{5,1},{9,13},{13,9},{2,6},{6,2},{1... | collective-permute-start | bytes 122888 | tf_op jit(solution)/shard_map/ppermute | solution.py:262
  49.5 1.9 %collective-permute-done.12.owner3 = bf16[80,256]{1,0:T(8,128)(2,1)S(1)} collective-permute-done((bf16[80,256]{1,0:T(8,128)(2,1)S(1)}, bf16[80,256]{1,0:T(8,128)(2,1)S(1)}, u32[]{:S(2)}, u32[]{:S(2)}) %collective-permute-start.12) | collective-permute-done | bytes 40992 | tf_op jit(solution)/shard_map/ppermute | solution.py:262
  51.4 1.6 %collective-permute-done.11.owner2 = bf16[80,256]{1,0:T(8,128)(2,1)S(1)} collective-permute-done((bf16[80,256]{1,0:T(8,128)(2,1)S(1)}, bf16[80,256]{1,0:T(8,128)(2,1)S(1)}, u32[]{:S(2)}, u32[]{:S(2)}) %collective-permute-start.11) | collective-permute-done | bytes 40992 | tf_op jit(solution)/shard_map/ppermute | solution.py:262
  52.9 0.0 collective-permute-done.10.owner1
  52.9 0.0 collective-permute-done.16.got
  52.9 0.0 collective-permute-done.15.up3
  53.0 1.7 %shard_map.73 = bf16[64,2048]{1,0:T(8,128)(2,1)} custom-call(bf16[80,256]{1,0:T(8,128)(2,1)S(1)} %shard_map.70.owner0, bf16[80,256]{1,0:T(8,128)(2,1)S(1)} %collective-permute-done.10.owner1, bf16[80,256]{1,0:T(8,128)(2,1)S(1)} %collective-permute-done.11.owner2, bf16[80,256]{1,0:T(8,128)(2,1)S(1)} %collective-permute-done.12.owner3, ...), custom_call_target="tpu_custom_call" | custom-call | flops 1 | bytes 1 | tf_op jit(solution)/shard_map/pallas_call | solution.py:100
  (4 shorter events, 0.0 us)
Async XLA Ops:
  0.0 29.9 %copy-start.6 = (s32[16]{0:T(128)S(1)}, s32[16]{0:T(128)}, u32[]{:S(2)}) copy-start(s32[16]{0:T(128)} %param.8) | copy-start | bytes 196
  0.0 29.9 %copy-start.7 = (s32[64]{0:T(128)S(1)}, s32[64]{0:T(128)}, u32[]{:S(2)}) copy-start(s32[64]{0:T(128)} %param.7) | copy-start | bytes 772
  0.0 28.6 %collective-permute-start.3 = (bf16[64,3584]{1,0:T(8,128)(2,1)}, bf16[64,3584]{1,0:T(8,128)(2,1)S(1)}, u32[]{:S(2)}, u32[]{:S(2)}) collective-permute-start(bf16[64,3584]{1,0:T(8,128)(2,1)} %x.3), channel_id=1, source_target_pairs={{0,4},{4,0},{8,12},{12,8},{1,5},{5,1},{9,13},{13,9},{2,6},{6,2},{1... | collective-permute-start | bytes 1376264 | tf_op jit(solution)/shard_map/ppermute | solution.py:262
  4.1 16.2 %collective-permute-start.4 = (bf16[64,1792]{1,0:T(8,128)(2,1)S(1)}, bf16[64,1792]{1,0:T(8,128)(2,1)S(1)}, u32[]{:S(2)}, u32[]{:S(2)}) collective-permute-start(bf16[64,1792]{1,0:T(8,128)(2,1)S(1)} %get-tuple-element.41), channel_id=1, source_target_pairs={{0,8},{8,0},{4,12},{12,4},{1,9},{9,1},{5,13},{13,5},{2,10},{10,2},... | collective-permute-start | bytes 688136 | tf_op jit(solution)/shard_map/ppermute | solution.py:262
  6.8 21.2 %collective-permute-start = (bf16[64,1792]{1,0:T(8,128)(2,1)S(1)}, bf16[64,1792]{1,0:T(8,128)(2,1)S(1)}, u32[]{:S(2)}, u32[]{:S(2)}) collective-permute-start(bf16[64,1792]{1,0:T(8,128)(2,1)S(1)} %get-tuple-element.42), channel_id=1, source_target_pairs={{0,8},{8,0},{4,12},{12,4},{1,9},{9,1},{5,13},{13,5},{2,10},{10,2},... | collective-permute-start | bytes 688136 | tf_op jit(solution)/shard_map/ppermute | solution.py:262
  7.1 36.1 %collective-permute-start.13 = (bf16[256,2048]{1,0:T(8,128)(2,1)}, bf16[256,2048]{1,0:T(8,128)(2,1)S(1)}, u32[]{:S(2)}, u32[]{:S(2)}) collective-permute-start(bf16[256,2048]{1,0:T(8,128)(2,1)} %bitcast.8), channel_id=1, source_target_pairs={{0,2},{2,0},{1,3},{3,1},{4,6},{6,4},{5,7},{7,5},{8,10},{10,8},{9,1... | collective-permute-start | bytes 3145736 | tf_op jit(solution)/shard_map/ppermute | solution.py:262
  8.6 5.2 %copy-start = (bf16[3584,2048]{1,0:T(8,128)(2,1)S(1)}, bf16[3584,2048]{1,0:T(8,128)(2,1)}, u32[]{:S(2)}) copy-start(bf16[3584,2048]{1,0:T(8,128)(2,1)} %w.7) | copy-start | bytes 44040196
  13.8 1.5 %copy-start.2 = (bf16[4,3584,64]{1,2,0:T(8,128)(2,1)S(1)}, bf16[4,3584,64]{1,2,0:T(8,128)(2,1)}, u32[]{:S(2)}) copy-start(bf16[4,3584,64]{1,2,0:T(8,128)(2,1)} %param.10) | copy-start | bytes 5505028
  15.3 1.0 %copy-start.4 = (bf16[64,3584]{1,0:T(8,128)(2,1)S(1)}, bf16[64,3584]{1,0:T(8,128)(2,1)}, u32[]{:S(2)}) copy-start(bf16[64,3584]{1,0:T(8,128)(2,1)} %x.3) | copy-start | bytes 1376260
  16.3 13.7 %copy-start.1 = (bf16[3584,2048]{1,0:T(8,128)(2,1)S(1)}, bf16[3584,2048]{1,0:T(8,128)(2,1)}, u32[]{:S(2)}) copy-start(bf16[3584,2048]{1,0:T(8,128)(2,1)} %w.7) | copy-start | bytes 44040196
  16.3 13.7 %copy-start.3 = (bf16[4,3584,64]{1,2,0:T(8,128)(2,1)S(1)}, bf16[4,3584,64]{1,2,0:T(8,128)(2,1)}, u32[]{:S(2)}) copy-start(bf16[4,3584,64]{1,2,0:T(8,128)(2,1)} %param.10) | copy-start | bytes 5505028
  19.5 13.1 %collective-permute-start.6 = (bf16[64,1792]{1,0:T(8,128)(2,1)S(1)}, bf16[64,1792]{1,0:T(8,128)(2,1)S(1)}, u32[]{:S(2)}, u32[]{:S(2)}) collective-permute-start(bf16[64,1792]{1,0:T(8,128)(2,1)S(1)} %get-tuple-element.26), channel_id=1, source_target_pairs={{4,8},{8,4},{5,9},{9,5},{6,10},{10,6},{7,11},{11,7},{20,24},{24,20... | collective-permute-start | bytes 688136 | tf_op jit(solution)/shard_map/ppermute | solution.py:262
  20.3 12.5 %collective-permute-start.5 = (bf16[64,1792]{1,0:T(8,128)(2,1)S(1)}, bf16[64,1792]{1,0:T(8,128)(2,1)S(1)}, u32[]{:S(2)}, u32[]{:S(2)}) collective-permute-start(bf16[64,1792]{1,0:T(8,128)(2,1)S(1)} %collective-permute-done.4.two_a), channel_id=1, source_target_pairs={{8,12},{4,0},{9,13},{5,1},{10,14},{6,2},{11,15},{7,3},{24,28},{20,... | collective-permute-start | bytes 688136 | tf_op jit(solution)/shard_map/ppermute | solution.py:262
  27.9 6.5 %collective-permute-start.2 = (bf16[64,1792]{1,0:T(8,128)(2,1)S(1)}, bf16[64,1792]{1,0:T(8,128)(2,1)S(1)}, u32[]{:S(2)}, u32[]{:S(2)}) collective-permute-start(bf16[64,1792]{1,0:T(8,128)(2,1)S(1)} %get-tuple-element.23), channel_id=1, source_target_pairs={{4,8},{8,4},{5,9},{9,5},{6,10},{10,6},{7,11},{11,7},{20,24},{24,20... | collective-permute-start | bytes 688136 | tf_op jit(solution)/shard_map/ppermute | solution.py:262
  28.6 7.9 %collective-permute-start.1 = (bf16[64,1792]{1,0:T(8,128)(2,1)S(1)}, bf16[64,1792]{1,0:T(8,128)(2,1)S(1)}, u32[]{:S(2)}, u32[]{:S(2)}) collective-permute-start(bf16[64,1792]{1,0:T(8,128)(2,1)S(1)} %collective-permute-done.two_b), channel_id=1, source_target_pairs={{8,12},{4,0},{9,13},{5,1},{10,14},{6,2},{11,15},{7,3},{24,28},{20,... | collective-permute-start | bytes 688136 | tf_op jit(solution)/shard_map/ppermute | solution.py:262
  34.4 4.8 %copy-start.5 = (bf16[4,64,2048]{2,1,0:T(8,128)(2,1)S(1)}, bf16[4,64,2048]{2,1,0:T(8,128)(2,1)}, u32[]{:S(2)}) copy-start(bf16[4,64,2048]{2,1,0:T(8,128)(2,1)} %param.11) | copy-start | bytes 3145732
  37.0 1.5 %collective-permute-start.7 = (f32[128,256]{1,0:T(8,128)S(1)}, f32[128,256]{1,0:T(8,128)S(1)}, u32[]{:S(2)}, u32[]{:S(2)}) collective-permute-start(f32[128,256]{1,0:T(8,128)S(1)} %get-tuple-element.30.low_give), channel_id=1, source_target_pairs={{0,1},{1,0},{2,3},{3,2},{4,5},{5,4},{6,7},{7,6},{8,9},{9,8},{10,11... | collective-permute-start | bytes 393224 | tf_op jit(solution)/shard_map/ppermute | solution.py:262
  38.6 4.6 %collective-permute-start.14 = (bf16[128,2048]{1,0:T(8,128)(2,1)S(1)}, bf16[128,2048]{1,0:T(8,128)(2,1)S(1)}, u32[]{:S(2)}, u32[]{:S(2)}) collective-permute-start(bf16[128,2048]{1,0:T(8,128)(2,1)S(1)} %get-tuple-element.37), channel_id=1, source_target_pairs={{0,1},{1,0},{2,3},{3,2},{4,5},{5,4},{6,7},{7,6},{8,9},{9,8},{10,11... | collective-permute-start | bytes 1572872 | tf_op jit(solution)/shard_map/ppermute | solution.py:262
  39.2 5.8 %collective-permute-start.9 = (bf16[256,2048]{1,0:T(8,128)(2,1)S(1)}, bf16[256,2048]{1,0:T(8,128)(2,1)S(1)}, u32[]{:S(2)}, u32[]{:S(2)}) collective-permute-start(bf16[256,2048]{1,0:T(8,128)(2,1)S(1)} %bitcast.9), channel_id=1, source_target_pairs={{0,1},{1,0},{2,3},{3,2},{4,5},{5,4},{6,7},{7,6},{8,9},{9,8},{10,11... | collective-permute-start | bytes 3145736 | tf_op jit(solution)/shard_map/ppermute | solution.py:262
  39.3 3.9 %collective-permute-start.8 = (bf16[64,256]{1,0:T(8,128)(2,1)S(1)}, bf16[64,256]{1,0:T(8,128)(2,1)S(1)}, u32[]{:S(2)}, u32[]{:S(2)}) collective-permute-start(bf16[64,256]{1,0:T(8,128)(2,1)S(1)} %get-tuple-element.33.low_other), channel_id=1, source_target_pairs={{0,2},{2,0},{1,3},{3,1},{4,6},{6,4},{5,7},{7,5},{8,10},{10,8},{9,1... | collective-permute-start | bytes 98312 | tf_op jit(solution)/shard_map/ppermute | solution.py:262
  43.4 9.5 %collective-permute-start.15 = (bf16[256,2048]{1,0:T(8,128)(2,1)S(1)}, bf16[256,2048]{1,0:T(8,128)(2,1)S(1)}, u32[]{:S(2)}, u32[]{:S(2)}) collective-permute-start(bf16[256,2048]{1,0:T(8,128)(2,1)S(1)} %get-tuple-element.38), channel_id=1, source_target_pairs={{0,1},{1,0},{2,3},{3,2},{4,5},{5,4},{6,7},{7,6},{8,9},{9,8},{10,11... | collective-permute-start | bytes 3145736 | tf_op jit(solution)/shard_map/ppermute | solution.py:262
  43.5 9.5 %collective-permute-start.16 = (bf16[64,2048]{1,0:T(8,128)(2,1)S(1)}, bf16[64,2048]{1,0:T(8,128)(2,1)S(1)}, u32[]{:S(2)}, u32[]{:S(2)}) collective-permute-start(bf16[64,2048]{1,0:T(8,128)(2,1)S(1)} %get-tuple-element.40), channel_id=1, source_target_pairs={{0,2},{2,0},{1,3},{3,1},{4,6},{6,4},{5,7},{7,5},{8,10},{10,8},{9,1... | collective-permute-start | bytes 786440 | tf_op jit(solution)/shard_map/ppermute | solution.py:262
  45.1 6.3 %collective-permute-start.12 = (bf16[80,256]{1,0:T(8,128)(2,1)S(1)}, bf16[80,256]{1,0:T(8,128)(2,1)S(1)}, u32[]{:S(2)}, u32[]{:S(2)}) collective-permute-start(bf16[80,256]{1,0:T(8,128)(2,1)S(1)} %shard_map.70.owner0), channel_id=1, source_target_pairs={{0,12},{12,0},{4,8},{8,4},{1,13},{13,1},{5,9},{9,5},{2,14},{14,2},... | collective-permute-start | bytes 122888 | tf_op jit(solution)/shard_map/ppermute | solution.py:262
  48.0 4.9 %collective-permute-start.11 = (bf16[80,256]{1,0:T(8,128)(2,1)S(1)}, bf16[80,256]{1,0:T(8,128)(2,1)S(1)}, u32[]{:S(2)}, u32[]{:S(2)}) collective-permute-start(bf16[80,256]{1,0:T(8,128)(2,1)S(1)} %shard_map.70.owner0), channel_id=1, source_target_pairs={{0,8},{8,0},{4,12},{12,4},{1,9},{9,1},{5,13},{13,5},{2,10},{10,2},... | collective-permute-start | bytes 122888 | tf_op jit(solution)/shard_map/ppermute | solution.py:262
  48.0 4.9 %collective-permute-start.10 = (bf16[80,256]{1,0:T(8,128)(2,1)S(1)}, bf16[80,256]{1,0:T(8,128)(2,1)S(1)}, u32[]{:S(2)}, u32[]{:S(2)}) collective-permute-start(bf16[80,256]{1,0:T(8,128)(2,1)S(1)} %shard_map.70.owner0), channel_id=1, source_target_pairs={{0,4},{4,0},{8,12},{12,8},{1,5},{5,1},{9,13},{13,9},{2,6},{6,2},{1... | collective-permute-start | bytes 122888 | tf_op jit(solution)/shard_map/ppermute | solution.py:262
